TPU v7x, 128 devices: a whole 4x4x4 slice. The times are simulated.
128 devices in a mesh: harm: 8 (over x, z_hi), rows: 16 (over y, z_lo, core).
Axes of the slice: x: 4, y: 4, z: 4 (z_hi: 2, z_lo: 2; z = z_hi * 2 + z_lo), core: 2. Of those that a mesh axis runs over, the one named last changes fastest.
Arguments:
- pressure: float32 [24, 1024, 2, 1024], P('harm', 'rows'), may hold values from -6 to 6
- contrast: float32 [1024, 1024], P('rows'), may hold values from -0.02 to 0.02
- absorption: float32 [1024, 1024], P('rows'), may hold values from 1e-05 to 0.0001
- nonlinearity: float32 [1024, 1024], P('rows'), may hold values from 0.5 to 2
Outputs:
- pressure_out: float32 [24, 1024, 2, 1024], P('harm', 'rows')
All inputs are finite; a program needn't handle non-finite values.
Results may differ from a plain program's by a relative error of at most 0.0003.
Values sent between devices are 32-bit elements; how exact they have to be, the bound alone decides.
No kernel may reach another device: no remote copies, remote signals or barrier semaphores. Data moves between devices by JAX's collectives and lax.ppermute only.
A program may use at most 128 MiB of HBM per device.

v0:
```python
import math

import jax
import jax.numpy as jnp
from jax import lax
from jax.sharding import PartitionSpec as P

H = 24
N = 1024
PLANES = 2
DZ = 128


def squared_freq_at(indices, length):
    centred = jnp.where(indices < length // 2, indices, indices - length).astype(jnp.float32)
    scaled = centred * (2.0 * math.pi / length)
    return scaled * scaled


def propagator(wave_number, down_square, across_square, march_step):
    axial_square = wave_number * wave_number - down_square - across_square
    axial_root = jnp.sqrt(jnp.abs(axial_square))
    phase_turn = march_step * axial_root
    propagating = axial_square >= 0.0
    prop_real = jnp.where(propagating, jnp.cos(phase_turn), jnp.exp(-phase_turn))
    prop_imag = jnp.where(propagating, jnp.sin(phase_turn), 0.0)
    return (prop_real, prop_imag)


def dft_tables(length):
    indices = jnp.arange(length, dtype=jnp.int32)
    product = indices[:, None] * indices[None, :] % length
    angle = product.astype(jnp.float32) * (2.0 * math.pi / length)
    return (jnp.cos(angle), jnp.sin(angle))


def combine(cosine_part, sine_part, direction, factor):
    out_real = (cosine_part[..., 0, :] - direction * sine_part[..., 1, :]) * factor
    out_imag = (cosine_part[..., 1, :] + direction * sine_part[..., 0, :]) * factor
    return jnp.stack([out_real, out_imag], axis=-2)


def along_last(wavefield, cosine_table, sine_table, direction, factor):
    flattened = wavefield.reshape(-1, wavefield.shape[-1])
    cosine_part = jnp.dot(flattened, cosine_table, precision=lax.Precision.HIGHEST).reshape(
        wavefield.shape
    )
    sine_part = jnp.dot(flattened, sine_table, precision=lax.Precision.HIGHEST).reshape(
        wavefield.shape
    )
    return combine(cosine_part, sine_part, direction, factor)


def along_rows(wavefield, cosine_table, sine_table, direction, factor):
    cosine_part = jnp.einsum(
        "kx,hxcm->hkcm", cosine_table, wavefield, precision=lax.Precision.HIGHEST
    )
    sine_part = jnp.einsum("kx,hxcm->hkcm", sine_table, wavefield, precision=lax.Precision.HIGHEST)
    return combine(cosine_part, sine_part, direction, factor)


def apply_factor(wavefield, factor_real, factor_imag):
    real_part = wavefield[:, :, 0, :]
    imag_part = wavefield[:, :, 1, :]
    return jnp.stack(
        [
            real_part * factor_real - imag_part * factor_imag,
            real_part * factor_imag + imag_part * factor_real,
        ],
        axis=2,
    )


def apply_screen(wavefield, orders, contrast, absorption, march_step):
    damping = jnp.exp(-absorption[None] * jnp.power(orders, 1.1) * march_step)
    angle = 3.0 / H * orders * march_step * contrast[None]
    return apply_factor(wavefield, damping * jnp.cos(angle), damping * jnp.sin(angle))


def couple(real_part, imag_part, gain):
    harmonic_count = real_part.shape[0]
    coupled_real = []
    coupled_imag = []
    for harmonic in range(1, harmonic_count + 1):
        source_real = jnp.zeros_like(real_part[0])
        source_imag = jnp.zeros_like(real_part[0])
        if harmonic > 1:
            first_real = real_part[: harmonic - 1]
            first_imag = imag_part[: harmonic - 1]
            second_real = real_part[harmonic - 2 :: -1]
            second_imag = imag_part[harmonic - 2 :: -1]
            source_real = jnp.sum(first_real * second_real - first_imag * second_imag, axis=0)
            source_imag = jnp.sum(first_real * second_imag + first_imag * second_real, axis=0)
        if harmonic < harmonic_count:
            high_real = real_part[harmonic:]
            high_imag = imag_part[harmonic:]
            low_real = real_part[: harmonic_count - harmonic]
            low_imag = imag_part[: harmonic_count - harmonic]
            source_real = source_real + 2.0 * jnp.sum(
                high_real * low_real + high_imag * low_imag, axis=0
            )
            source_imag = source_imag + 2.0 * jnp.sum(
                high_imag * low_real - high_real * low_imag, axis=0
            )
        weight = harmonic * gain
        coupled_real.append(real_part[harmonic - 1] - weight * source_imag)
        coupled_imag.append(imag_part[harmonic - 1] + weight * source_real)
    return (jnp.stack(coupled_real, axis=0), jnp.stack(coupled_imag, axis=0))


def apply_coupling(wavefield, gain):
    real_part, imag_part = couple(wavefield[:, :, 0, :], wavefield[:, :, 1, :], gain)
    return jnp.stack([real_part, imag_part], axis=2)


def shards(pressure, contrast, absorption, nonlinearity):
    local_harm = pressure.shape[0]
    slab_rows = pressure.shape[1]
    harm_count = lax.axis_size("harm")
    row_count = lax.axis_size("rows")
    column_block = N // row_count
    march_step = float(DZ)
    cosine_table, sine_table = dft_tables(N)
    local_orders = (
        lax.axis_index("harm") * local_harm + jnp.arange(local_harm, dtype=jnp.int32) + 1
    ).astype(jnp.float32)
    column_index = lax.axis_index("rows") * column_block + jnp.arange(column_block, dtype=jnp.int32)
    prop_real, prop_imag = propagator(
        3.0 / H * local_orders[:, None, None],
        squared_freq_at(jnp.arange(N, dtype=jnp.int32), N)[None, :, None],
        squared_freq_at(column_index, N)[None, None, :],
        march_step,
    )
    pixel_rows = slab_rows // harm_count
    row_start = lax.axis_index("harm") * pixel_rows
    pixel_gain = lax.dynamic_slice_in_dim(nonlinearity, row_start, pixel_rows, 0) * (
        1.0 / (H * math.sqrt(H))
    )
    wavefield = pressure
    for plane_index in range(PLANES):
        wavefield = along_last(wavefield, cosine_table, sine_table, -1.0, 1.0)
        wavefield = lax.all_to_all(wavefield, "rows", split_axis=3, concat_axis=1, tiled=True)
        spectrum = along_rows(wavefield, cosine_table, sine_table, -1.0, 1.0)
        spectrum = apply_factor(spectrum, prop_real, prop_imag)
        wavefield = along_rows(spectrum, cosine_table, sine_table, 1.0, 1.0 / N)
        wavefield = lax.all_to_all(wavefield, "rows", split_axis=1, concat_axis=3, tiled=True)
        wavefield = along_last(wavefield, cosine_table, sine_table, 1.0, 1.0 / N)
        wavefield = apply_screen(
            wavefield, local_orders[:, None, None], contrast, absorption, march_step
        )
        wavefield = lax.all_to_all(wavefield, "harm", split_axis=1, concat_axis=0, tiled=True)
        wavefield = apply_coupling(wavefield, pixel_gain)
        wavefield = lax.all_to_all(wavefield, "harm", split_axis=0, concat_axis=1, tiled=True)
    return wavefield


def solution(mesh):
    in_specs = (P("harm", "rows", None, None), P("rows", None), P("rows", None), P("rows", None))
    out_specs = P("harm", "rows", None, None)
    return jax.shard_map(shards, mesh=mesh, in_specs=in_specs, out_specs=out_specs, check_vma=False)
```

profile of v0, /device:TPU:0, one launch (start us, length us, event | category | flops | bytes accessed | tf_op | source)
XLA Modules:
  0.0 712.4 jit_solution(14092289652432941617)
XLA Ops:
  2.4 21.8 %fusion.56 = f32[384,1024]{1,0:T(8,128)} fusion(f32[384,1024]{1,0:T(8,128)S(1)} %reshape.634), kind=kOutput, calls=%fused_computation.57 | convolution fusion | flops 4846518272 | bytes 3145728 | tf_op jit(solution)/shard_map/dot_general | solution.py:48
  24.2 22.2 %fusion.59 = f32[384,1024]{1,0:T(8,128)S(1)} fusion(f32[384,1024]{1,0:T(8,128)S(1)} %reshape.634), kind=kOutput, calls=%fused_computation.58 | convolution fusion | flops 4846518272 | bytes 3145728 | tf_op jit(solution)/shard_map/dot_general | solution.py:45
  54.0 4.3 copy.153
  58.2 4.4 reshape.639
  62.6 6.0 all-to-all-start
  68.8 22.0 %all-to-all-done = f32[16,1,24576]{2,1,0:T(1,128)S(1)} async-done(((f32[16,1,24576]{2,1,0:T(1,128)}), f32[16,1,24576]{2,1,0:T(1,128)S(1)}, u32[]{:S(2)}, u32[]{:S(2)}) %all-to-all-start) | async-done | bytes 1572896 | tf_op jit(solution)/shard_map/all_to_all | solution.py:142
  91.2 5.9 reduce
  97.2 3.4 reshape.640
  100.6 3.5 copy.462
  107.0 22.1 %fusion.62 = f32[3,1024,2,64]{1,3,2,0:T(8,128)S(1)} fusion(f32[3,1024,2,64]{1,3,2,0:T(8,128)S(1)} %all_to_all.101), kind=kOutput, calls=%fused_computation.59 | convolution fusion | flops 4846518272 | bytes 3145728 | tf_op jit(solution)/shard_map/kx,hxcm->hkcm/dot_general | solution.py:58
  129.0 21.7 %fusion.74 = f32[3,1024,2,64]{1,3,2,0:T(8,128)S(1)} fusion(f32[3,1024,2,64]{1,3,2,0:T(8,128)S(1)} %all_to_all.101), kind=kOutput, calls=%fused_computation.63 | convolution fusion | flops 4846518272 | bytes 3145728 | tf_op jit(solution)/shard_map/kx,hxcm->hkcm/dot_general | solution.py:55
  150.8 4.2 fusion.100
  155.0 20.6 %fusion.65 = f32[3,1024,2,64]{1,3,2,0:T(8,128)S(1)} fusion(f32[3,1024,1,64]{1,3,2,0:T(8,128)S(1)} %get-tuple-element.188, f32[3,1024,1,64]{1,3,2,0:T(8,128)S(1)} %get-tuple-element.187), kind=kOutput, calls=%fused_computation.60 | convolution fusion | flops 4846911488 | bytes 3145728 | tf_op jit(solution)/shard_map/kx,hxcm->hkcm/dot_general | solution.py:58
  175.6 21.0 %fusion.77 = f32[3,1024,2,64]{1,3,2,0:T(8,128)S(1)} fusion(f32[3,1024,1,64]{1,3,2,0:T(8,128)S(1)} %get-tuple-element.188, f32[3,1024,1,64]{1,3,2,0:T(8,128)S(1)} %get-tuple-element.187), kind=kOutput, calls=%fused_computation.64 | convolution fusion | flops 4846911488 | bytes 3145728 | tf_op jit(solution)/shard_map/kx,hxcm->hkcm/dot_general | solution.py:55
  198.3 4.3 copy.155
  202.6 4.2 reshape.641
  206.8 4.3 all-to-all-start.1
  211.2 22.0 %all-to-all-done.1 = f32[16,1,24576]{2,1,0:T(1,128)S(1)} async-done(((f32[16,1,24576]{2,1,0:T(1,128)}), f32[16,1,24576]{2,1,0:T(1,128)S(1)}, u32[]{:S(2)}, u32[]{:S(2)}) %all-to-all-start.1) | async-done | bytes 1572896 | tf_op jit(solution)/shard_map/all_to_all | solution.py:146
  233.2 5.9 reduce.1
  242.6 3.5 copy.461
  248.9 22.1 %fusion.25 = f32[3,64,2,1024]{3,1,2,0:T(8,128)S(1)} fusion(f32[3,64,2,1024]{3,1,2,0:T(8,128)S(1)} %dot_general.66), kind=kOutput, calls=%fused_computation.28 | convolution fusion | flops 4846518272 | bytes 3145728 | tf_op jit(solution)/shard_map/dot_general | solution.py:48
  271.0 21.7 %fusion.11 = f32[3,64,2,1024]{3,1,2,0:T(8,128)S(1)} fusion(f32[3,64,2,1024]{3,1,2,0:T(8,128)S(1)} %dot_general.66), kind=kOutput, calls=%fused_computation.14 | convolution fusion | flops 4846518272 | bytes 3145728 | tf_op jit(solution)/shard_map/dot_general | solution.py:45
  292.7 3.7 multiply_subtract_fusion.1
  298.9 7.3 %all-to-all-start.2 = ((f32[3,64,2,1024]{3,2,0,1:T(2,128)}), f32[3,64,2,1024]{3,2,0,1:T(2,128)S(1)}, u32[]{:S(2)}, u32[]{:S(2)}) async-start(f32[3,64,2,1024]{3,2,0,1:T(2,128)} %copy.157), calls=%async_computation.2 | async-start | bytes 3145728 | tf_op jit(solution)/shard_map/all_to_all | solution.py:151
  306.2 23.4 %all-to-all-done.2 = f32[3,64,2,1024]{3,2,0,1:T(2,128)S(1)} async-done(((f32[3,64,2,1024]{3,2,0,1:T(2,128)}), f32[3,64,2,1024]{3,2,0,1:T(2,128)S(1)}, u32[]{:S(2)}, u32[]{:S(2)}) %all-to-all-start.2) | async-done | bytes 1572896 | tf_op jit(solution)/shard_map/all_to_all | solution.py:151
  339.7 24.5 %all_to_all.135 = f32[24,8,2,1024]{3,1,2,0:T(8,128)S(1)} all-to-all(f32[24,8,2,1024]{3,1,2,0:T(8,128)S(1)} %pad_maximum_fusion.4), channel_id=1, replica_groups=mesh['harm'=8,'rows'=16] {'harm'}, dimensions={0} | all-to-all | bytes 3145728 | tf_op jit(solution)/shard_map/all_to_all | solution.py:153
  364.2 21.8 %fusion.23 = f32[3,64,2,1024]{3,1,2,0:T(8,128)S(1)} fusion(f32[8,3,8,2,1024]{4,2,3,1,0:T(8,128)S(1)} %bitcast.2749), kind=kOutput, calls=%fused_computation.26 | convolution fusion | flops 4846518272 | bytes 3145728 | tf_op jit(solution)/shard_map/dot_general | solution.py:48
  386.0 21.7 %fusion.9 = f32[3,64,2,1024]{3,1,2,0:T(8,128)S(1)} fusion(f32[8,3,8,2,1024]{4,2,3,1,0:T(8,128)S(1)} %bitcast.2750), kind=kOutput, calls=%fused_computation.12 | convolution fusion | flops 4846518272 | bytes 3145728 | tf_op jit(solution)/shard_map/dot_general | solution.py:45
  409.4 4.3 copy.227
  413.7 4.4 reshape.643
  418.1 27.4 %all_to_all.136 = f32[16,1,24576]{2,1,0:T(1,128)S(1)} all-to-all(f32[16,1,24576]{2,1,0:T(1,128)} %reshape.643), channel_id=1, replica_groups=mesh['harm'=8,'rows'=16] {'rows'}, dimensions={0} | all-to-all | bytes 3145728 | tf_op jit(solution)/shard_map/all_to_all | solution.py:142
  445.5 5.9 reduce.2
  454.8 3.5 copy.460
  461.2 22.3 %fusion.68 = f32[3,1024,2,64]{1,3,2,0:T(8,128)S(1)} fusion(f32[3,1024,2,64]{1,3,2,0:T(8,128)S(1)} %all_to_all.115), kind=kOutput, calls=%fused_computation.61 | convolution fusion | flops 4846518272 | bytes 3145728 | tf_op jit(solution)/shard_map/kx,hxcm->hkcm/dot_general | solution.py:58
  483.5 21.7 %fusion.80 = f32[3,1024,2,64]{1,3,2,0:T(8,128)S(1)} fusion(f32[3,1024,2,64]{1,3,2,0:T(8,128)S(1)} %all_to_all.115), kind=kOutput, calls=%fused_computation.65 | convolution fusion | flops 4846518272 | bytes 3145728 | tf_op jit(solution)/shard_map/kx,hxcm->hkcm/dot_general | solution.py:55
  505.2 3.9 fusion.102
  509.1 20.7 %fusion.71 = f32[3,1024,2,64]{1,3,2,0:T(8,128)S(1)} fusion(f32[3,1024,1,64]{1,3,2,0:T(8,128)S(1)} %get-tuple-element.186, f32[3,1024,1,64]{1,3,2,0:T(8,128)S(1)} %get-tuple-element.185), kind=kOutput, calls=%fused_computation.62 | convolution fusion | flops 4846911488 | bytes 3145728 | tf_op jit(solution)/shard_map/kx,hxcm->hkcm/dot_general | solution.py:58
  529.8 20.9 %fusion.83 = f32[3,1024,2,64]{1,3,2,0:T(8,128)S(1)} fusion(f32[3,1024,1,64]{1,3,2,0:T(8,128)S(1)} %get-tuple-element.186, f32[3,1024,1,64]{1,3,2,0:T(8,128)S(1)} %get-tuple-element.185), kind=kOutput, calls=%fused_computation.66 | convolution fusion | flops 4846911488 | bytes 3145728 | tf_op jit(solution)/shard_map/kx,hxcm->hkcm/dot_general | solution.py:55
  552.4 4.3 copy.229
  556.7 4.2 reshape.645
  560.9 26.0 %all_to_all.137 = f32[16,1,24576]{2,1,0:T(1,128)S(1)} all-to-all(f32[16,1,24576]{2,1,0:T(1,128)} %reshape.645), channel_id=1, replica_groups=mesh['harm'=8,'rows'=16] {'rows'}, dimensions={0} | all-to-all | bytes 3145728 | tf_op jit(solution)/shard_map/all_to_all | solution.py:146
  586.9 5.9 reduce.3
  596.2 3.5 copy.459
  602.6 22.3 %fusion.17 = f32[3,64,2,1024]{3,1,2,0:T(8,128)S(1)} fusion(f32[3,64,2,1024]{3,1,2,0:T(8,128)S(1)} %dot_general.76), kind=kOutput, calls=%fused_computation.20 | convolution fusion | flops 4846518272 | bytes 3145728 | tf_op jit(solution)/shard_map/dot_general | solution.py:48
  624.9 21.7 %fusion.3 = f32[3,64,2,1024]{3,1,2,0:T(8,128)S(1)} fusion(f32[3,64,2,1024]{3,1,2,0:T(8,128)S(1)} %dot_general.76), kind=kOutput, calls=%fused_computation.6 | convolution fusion | flops 4846518272 | bytes 3145728 | tf_op jit(solution)/shard_map/dot_general | solution.py:45
  646.6 3.5 multiply_subtract_fusion
  651.4 25.3 %all_to_all.138 = f32[3,64,2,1024]{3,2,0,1:T(2,128)S(1)} all-to-all(f32[3,64,2,1024]{3,2,0,1:T(2,128)S(1)} %copy.231), channel_id=1, replica_groups=mesh['harm'=8,'rows'=16] {'harm'}, dimensions={1} | all-to-all | bytes 3145728 | tf_op jit(solution)/shard_map/all_to_all | solution.py:151
  686.4 23.5 %all_to_all.139 = f32[24,8,2,1024]{3,1,2,0:T(8,128)S(1)} all-to-all(f32[24,8,2,1024]{3,1,2,0:T(8,128)S(1)} %copy.299), channel_id=1, replica_groups=mesh['harm'=8,'rows'=16] {'harm'}, dimensions={0} | all-to-all | bytes 3145728 | tf_op jit(solution)/shard_map/all_to_all | solution.py:153
  (297 shorter events, 61.5 us)
Async XLA Ops:
  62.6 28.1 %all-to-all-start = ((f32[16,1,24576]{2,1,0:T(1,128)}), f32[16,1,24576]{2,1,0:T(1,128)S(1)}, u32[]{:S(2)}, u32[]{:S(2)}) async-start(f32[16,1,24576]{2,1,0:T(1,128)} %reshape.639), calls=%async_computation | async-start | bytes 3145728 | tf_op jit(solution)/shard_map/all_to_all | solution.py:142
  206.8 4.4 copy-start.5
  206.8 26.4 %all-to-all-start.1 = ((f32[16,1,24576]{2,1,0:T(1,128)}), f32[16,1,24576]{2,1,0:T(1,128)S(1)}, u32[]{:S(2)}, u32[]{:S(2)}) async-start(f32[16,1,24576]{2,1,0:T(1,128)} %reshape.641), calls=%async_computation.1 | async-start | bytes 3145728 | tf_op jit(solution)/shard_map/all_to_all | solution.py:146
  211.2 81.6 %copy-start.1 = (f32[64,1024]{1,0:T(8,128)}, f32[64,1024]{1,0:T(8,128)S(1)}, u32[]{:S(2)}) copy-start(f32[64,1024]{1,0:T(8,128)S(1)} %neg.19) | copy-start | bytes 786436
  271.0 21.7 %copy-start.3 = (f32[64,1024]{1,0:T(8,128)S(1)}, f32[64,1024]{1,0:T(8,128)}, u32[]{:S(2)}) copy-start(f32[64,1024]{1,0:T(8,128)} %param.5) | copy-start | bytes 786436
  298.9 30.7 %all-to-all-start.2 = ((f32[3,64,2,1024]{3,2,0,1:T(2,128)}), f32[3,64,2,1024]{3,2,0,1:T(2,128)S(1)}, u32[]{:S(2)}, u32[]{:S(2)}) async-start(f32[3,64,2,1024]{3,2,0,1:T(2,128)} %copy.157), calls=%async_computation.2 | async-start | bytes 3145728 | tf_op jit(solution)/shard_map/all_to_all | solution.py:151
  337.3 1.0 copy-start
  624.8 21.7 %copy-start.2 = (f32[64,1024]{1,0:T(8,128)S(1)}, f32[64,1024]{1,0:T(8,128)}, u32[]{:S(2)}) copy-start(f32[64,1024]{1,0:T(8,128)} %copy-done.1) | copy-start | bytes 786436
  624.9 21.7 %copy-start.4 = (f32[64,1024]{1,0:T(8,128)S(1)}, f32[64,1024]{1,0:T(8,128)}, u32[]{:S(2)}) copy-start(f32[64,1024]{1,0:T(8,128)} %param.5) | copy-start | bytes 786436
where the time goes:
time: 719 us; the launch traced here: 712 us
  matrix products  346 us (48%)
  blocking collectives  127 us (18%)
  local copies, waits for them, and re-layouts  93.7 us (13%)
  waiting for transfers between devices  67.4 us (9%)
  other arithmetic  58.5 us (8%)
  starting transfers between devices  17.7 us (2%)
    dot_general x4, matrix products, along_last(): jnp.dot(flattened, sine_table, precision=lax.Precision.HIGHEST)  88 us
    dot_general x4, matrix products, along_last(): jnp.dot(flattened, cosine_table, precision=lax.Precision.HIGHEST)  87.3 us
    dot_general x4, matrix products, along_rows(): jnp.einsum('kx,hxcm->hkcm', sine_table, wavefield, precision=lax.Precisio...  85.7 us
    dot_general x4, matrix products, along_rows(): jnp.einsum('kx,hxcm->hkcm', cosine_table, wavefield, precision=lax.Precis...  85.3 us
    all_to_all x2, blocking collectives, shards(): lax.all_to_all(wavefield, 'harm', split_axis=0, concat_axis=1, tiled=True)  48 us
    unnamed x20, local copies, waits for them, and re-layouts  31.4 us
    all_to_all x1, blocking collectives, shards(): lax.all_to_all(wavefield, 'rows', split_axis=3, concat_axis=1, tiled=True)  27.4 us
    all_to_all x1, blocking collectives, shards(): lax.all_to_all(wavefield, 'rows', split_axis=1, concat_axis=3, tiled=True)  26 us
  transfers between devices with their start and end apart: 3, of which 3 were waited for; matrix products, arithmetic and copies ran while one was open for 0% of the time, Pallas kernels for 0%

commit v1 on v0

v1 whole, which is shorter than its diff:
```python
import functools
import math

import jax
import jax.numpy as jnp
import ml_dtypes
import numpy as np
from jax import lax
from jax.experimental import pallas as pl
from jax.experimental.pallas import tpu as pltpu
from jax.sharding import PartitionSpec as P

H = 24
N = 1024
PLANES = 2
DZ = 128
RADIX = 8
SUB = N // RADIX
HALF = SUB // 2
ROOT_HALF = math.sqrt(0.5)
VMEM_LIMIT = 56 * 1024 * 1024


def split_constant(table):
    high = table.astype(np.float32).astype(ml_dtypes.bfloat16)
    low = (table - high.astype(np.float64)).astype(np.float32).astype(ml_dtypes.bfloat16)
    return high, low


def sub_angles():
    index = np.arange(SUB)
    return 2.0 * np.pi / SUB * ((index[:, None] * index[None, :]) % SUB)


def lane_matrices():
    cosine, sine = np.cos(sub_angles()), np.sin(sub_angles())
    forward_real = np.concatenate([cosine, sine], 0)
    forward_imag = np.concatenate([-sine, cosine], 0)
    inverse_real = np.concatenate([cosine, -sine], 0)
    inverse_imag = np.concatenate([sine, cosine], 0)
    forward = np.concatenate(
        [
            forward_real[:, :HALF],
            forward_imag[:, :HALF],
            forward_real[:, HALF:],
            forward_imag[:, HALF:],
        ],
        1,
    )
    inverse = np.concatenate([inverse_real, inverse_imag], 1)
    inverse = np.concatenate(
        [
            inverse[:HALF],
            inverse[SUB : SUB + HALF],
            inverse[HALF:SUB],
            inverse[SUB + HALF :],
        ],
        0,
    )
    return split_constant(forward), split_constant(inverse)


def lane_twiddles():
    angle = 2.0 * np.pi / N * (np.arange(RADIX)[:, None] * np.arange(SUB)[None, :])
    return np.cos(angle).astype(np.float32), np.sin(angle).astype(np.float32)


def row_matrices():
    both = np.concatenate([np.cos(sub_angles()), np.sin(sub_angles())], 0)
    high, low = split_constant(both)
    return np.concatenate([high, high], 1), low


def row_twiddles():
    angle = 2.0 * np.pi / N * (np.arange(RADIX)[:, None] * np.arange(SUB)[None, :])
    sign = np.where(np.arange(SUB) < HALF, 1.0, -1.0)
    cosine = np.broadcast_to(np.cos(angle)[:, :, None], (RADIX, SUB, SUB))
    sine = np.sin(angle)[:, :, None] * sign[None, None, :]
    return cosine.astype(np.float32), sine.astype(np.float32)


def split_value(value):
    high = value.astype(jnp.bfloat16)
    low = (value - high.astype(jnp.float32)).astype(jnp.bfloat16)
    return high, low


def add(left, right):
    return tuple(a + b for a, b in zip(left, right))


def subtract(left, right):
    return tuple(a - b for a, b in zip(left, right))


def scale(value, factor):
    return tuple(a * factor for a in value)


def turn_pair(direction):
    def turn(value):
        real, imag = value
        return (imag, -real) if direction < 0 else (-imag, real)

    return turn


def butterflies(points, turn):
    even = [add(points[k], points[k + 4]) for k in range(4)]
    odd = [subtract(points[k], points[k + 4]) for k in range(4)]
    turned = turn(odd[1])
    first = scale(add(odd[1], turned), ROOT_HALF)
    second = turn(odd[2])
    turned = turn(odd[3])
    third = scale(subtract(turned, odd[3]), ROOT_HALF)
    out = [None] * RADIX
    for offset, (a, b, c, d) in ((0, even), (1, (odd[0], first, second, third))):
        sum_ac, diff_ac = add(a, c), subtract(a, c)
        sum_bd, diff_bd = add(b, d), turn(subtract(b, d))
        out[offset] = add(sum_ac, sum_bd)
        out[offset + 4] = subtract(sum_ac, sum_bd)
        out[offset + 2] = add(diff_ac, diff_bd)
        out[offset + 6] = subtract(diff_ac, diff_bd)
    return out


def triple_dot(high, low, matrix_high, matrix_low):
    def product(left, right):
        return jnp.dot(left, right, preferred_element_type=jnp.float32)

    return product(high, matrix_high) + (product(low, matrix_high) + product(high, matrix_low))


def twiddle_pair(value, cosine, sine, direction):
    real, imag = value
    if direction < 0:
        return real * cosine + imag * sine, imag * cosine - real * sine
    return real * cosine - imag * sine, imag * cosine + real * sine


def forward_lanes(points, store, cosine_ref, sine_ref):
    for m, value in enumerate(butterflies(points, turn_pair(-1))):
        if m > 0:
            value = twiddle_pair(value, cosine_ref[m : m + 1], sine_ref[m : m + 1], -1)
        store(m, *split_value(jnp.concatenate(value, axis=1)))


def first_kernel(
    in_ref, gh_ref, gl_ref, cosine_ref, sine_ref, out_ref, high_ref, low_ref
):
    rows = out_ref.shape[2]
    for start in range(0, rows, 16):
        points = [
            tuple(
                in_ref[pl.ds(start * 16 + 2 * k + c, 16, stride=16), :] for c in range(2)
            )
            for k in range(RADIX)
        ]

        def store(m, high, low):
            high_ref[m, start : start + 16, :] = high
            low_ref[m, start : start + 16, :] = low

        forward_lanes(points, store, cosine_ref, sine_ref)
    for m in range(RADIX):
        result = triple_dot(high_ref[m], low_ref[m], gh_ref[...], gl_ref[...])
        out_ref[2 * m, 0] = result[:, :SUB]
        out_ref[2 * m + 1, 0] = result[:, SUB:]


def whole(shape):
    return pl.BlockSpec(shape, lambda *index: (0,) * len(shape))


def first_transform(pressure, constants):
    local_harm, rows = pressure.shape[0], pressure.shape[1]
    lines = pressure.reshape(local_harm, rows, 2, RADIX, SUB).transpose(0, 1, 3, 2, 4)
    lines = lines.reshape(local_harm * rows * 16, SUB)
    (gh, gl), _, (cosine, sine) = constants["lane"]
    return pl.pallas_call(
        first_kernel,
        grid=(local_harm,),
        in_specs=[
            pl.BlockSpec((rows * 16, SUB), lambda n: (n, 0)),
            whole(gh.shape),
            whole(gl.shape),
            whole(cosine.shape),
            whole(sine.shape),
        ],
        out_specs=pl.BlockSpec((16, 1, rows, SUB), lambda n: (0, n, 0, 0)),
        out_shape=jax.ShapeDtypeStruct((16, local_harm, rows, SUB), jnp.float32),
        scratch_shapes=[
            pltpu.VMEM((RADIX, rows, 2 * SUB), jnp.bfloat16),
            pltpu.VMEM((RADIX, rows, 2 * SUB), jnp.bfloat16),
        ],
        compiler_params=pltpu.CompilerParams(vmem_limit_bytes=VMEM_LIMIT),
        cost_estimate=pl.CostEstimate(
            flops=3 * 2 * local_harm * rows * RADIX * 65536,
            bytes_accessed=2 * lines.size * 4,
            transcendentals=0,
        ),
        name="first_transform",
    )(lines, gh, gl, cosine, sine)


def march_kernel(
    load, in_ref, pr_ref, pi_ref, mh_ref, ml_ref, cosine_ref, sine_ref, out_ref, part_ref, spec_ref
):
    lane = lax.broadcasted_iota(jnp.int32, (8, SUB), 1)
    sign = jnp.where(lane < HALF, 1.0, -1.0).astype(jnp.float32)

    def swap(value):
        return pltpu.roll(value, HALF, 1)

    def turn_forward(value):
        return (sign * swap(value[0]),)

    def turn_inverse(value):
        return (-sign * swap(value[0]),)

    def rows_product():
        halves = part_ref[...]
        return jnp.dot(
            mh_ref[...], halves, preferred_element_type=jnp.float32
        ) + jnp.dot(ml_ref[...], halves[:SUB], preferred_element_type=jnp.float32)

    for pair in range(SUB // 16):
        outs = []
        for tile in (2 * pair, 2 * pair + 1):
            points = [(load(in_ref, 2 * k + tile // 8, tile % 8),) for k in range(RADIX)]
            values = butterflies(points, turn_forward)
            rows = slice(8 * tile, 8 * tile + 8)
            outs.append(
                [
                    value[0]
                    if m == 0
                    else value[0] * cosine_ref[m, rows] + swap(value[0]) * sine_ref[m, rows]
                    for m, value in enumerate(values)
                ]
            )
        for m in range(RADIX):
            high, low = split_value(jnp.concatenate([outs[0][m], outs[1][m]], 0))
            part_ref[16 * pair : 16 * pair + 16, SUB * m : SUB * m + SUB] = high
            part_ref[SUB + 16 * pair : SUB + 16 * pair + 16, SUB * m : SUB * m + SUB] = low
    spec_ref[...] = rows_product()
    for m in range(RADIX):
        lanes = slice(SUB * m, SUB * m + SUB)
        for pair in range(SUB // 16):
            outs = []
            for tile in (2 * pair, 2 * pair + 1):
                rows = slice(8 * tile, 8 * tile + 8)
                value = spec_ref[rows, lanes] + sign * swap(
                    spec_ref[SUB + 8 * tile : SUB + 8 * tile + 8, lanes]
                )
                outs.append(value * pr_ref[0, m, rows] + swap(value) * pi_ref[0, m, rows])
            high, low = split_value(jnp.concatenate(outs, 0))
            part_ref[16 * pair : 16 * pair + 16, lanes] = high
            part_ref[SUB + 16 * pair : SUB + 16 * pair + 16, lanes] = low
    spec_ref[...] = rows_product()
    for tile in range(SUB // 8):
        rows = slice(8 * tile, 8 * tile + 8)
        points = []
        for m in range(RADIX):
            lanes = slice(SUB * m, SUB * m + SUB)
            value = spec_ref[rows, lanes] - sign * swap(
                spec_ref[SUB + 8 * tile : SUB + 8 * tile + 8, lanes]
            )
            if m > 0:
                value = value * cosine_ref[m, rows] - swap(value) * sine_ref[m, rows]
            points.append((value,))
        for k, value in enumerate(butterflies(points, turn_inverse)):
            out_ref[tile % 8, 2 * k + tile // 8, 0] = value[0]


def march(wavefield, prop_real, prop_imag, constants, by_rows):
    harm_count, row_count = 8, 16
    if by_rows:
        local_harm = wavefield.shape[1]
        in_spec = pl.BlockSpec((16, 1, 64, SUB), lambda n: (0, n, 0, 0))

        def load(ref, block, tile):
            return ref[block, 0, 8 * tile : 8 * tile + 8, :]
    else:
        local_harm = wavefield.shape[2]
        in_spec = pl.BlockSpec((harm_count, row_count, 1, 8, SUB), lambda n: (0, 0, n, 0, 0))

        def load(ref, block, tile):
            return ref[tile, block, 0]

    mh, ml = constants["row_matrices"]
    cosine, sine = constants["row_twiddles"]
    prop_spec = pl.BlockSpec((1, RADIX, SUB, SUB), lambda n: (n, 0, 0, 0))
    return pl.pallas_call(
        functools.partial(march_kernel, load),
        grid=(local_harm,),
        in_specs=[
            in_spec,
            prop_spec,
            prop_spec,
            whole(mh.shape),
            whole(ml.shape),
            whole(cosine.shape),
            whole(sine.shape),
        ],
        out_specs=pl.BlockSpec(
            (harm_count, row_count, 1, 8, SUB), lambda n: (0, 0, n, 0, 0)
        ),
        out_shape=jax.ShapeDtypeStruct(
            (harm_count, row_count, local_harm, 8, SUB), jnp.float32
        ),
        scratch_shapes=[
            pltpu.VMEM((2 * SUB, N), jnp.bfloat16),
            pltpu.VMEM((2 * SUB, N), jnp.float32),
        ],
        compiler_params=pltpu.CompilerParams(vmem_limit_bytes=VMEM_LIMIT),
        cost_estimate=pl.CostEstimate(
            flops=2 * 2 * 2 * local_harm * 256 * 256 * N,
            bytes_accessed=4 * wavefield.size * 4,
            transcendentals=0,
        ),
        name="march",
    )(wavefield, prop_real, prop_imag, mh, ml, cosine, sine)


def pair_order():
    block = 4
    order = []
    for low in range(0, H, block):
        for high in range(low, H, block):
            order += [
                (m, l)
                for m in range(high + 1, high + block + 1)
                for l in range(low + 1, low + block + 1)
                if m > l
            ]
    return order


def couple_pixels(load, gain, store):
    total_real = [None] * (H + 1)
    total_imag = [None] * (H + 1)

    def accumulate(n, real, imag):
        total_real[n] = real if total_real[n] is None else total_real[n] + real
        total_imag[n] = imag if total_imag[n] is None else total_imag[n] + imag

    for m, l in pair_order():
        (a, b), (c, d) = load(m), load(l)
        ac, bd, ad, bc = a * c, b * d, a * d, b * c
        accumulate(m - l, ac + bd, bc - ad)
        if m + l <= H:
            accumulate(m + l, ac - bd, ad + bc)
    for m in range(1, H // 2 + 1):
        a, b = load(m)
        accumulate(2 * m, 0.5 * (a * a - b * b), a * b)
    for n in range(1, H + 1):
        a, b = load(n)
        weight = (2.0 * n) * gain
        if total_real[n] is None:
            store(n, a, b)
        else:
            store(n, a - weight * total_imag[n], b + weight * total_real[n])


def pixel_kernel(
    last,
    in_ref,
    fr_ref,
    fi_ref,
    gain_ref,
    gh_ref,
    gl_ref,
    ih_ref,
    il_ref,
    cosine_ref,
    sine_ref,
    out_ref,
    high_ref,
    low_ref,
    line_ref,
    field_ref,
):
    local_harm = H // 8

    def tile_of(n, r):
        return in_ref[n // local_harm, r, n % local_harm]

    for n in range(0, H, 2):
        for m in range(RADIX):
            value = jnp.concatenate(
                [
                    jnp.concatenate([tile_of(n + i, 2 * m), tile_of(n + i, 2 * m + 1)], 1)
                    for i in range(2)
                ],
                0,
            )
            high, low = split_value(value)
            high_ref[m, 8 * n : 8 * n + 16, :] = high
            low_ref[m, 8 * n : 8 * n + 16, :] = low
    for m in range(RADIX):
        line_ref[m] = triple_dot(high_ref[m], low_ref[m], ih_ref[...], il_ref[...])
    for n in range(H):
        rows = slice(8 * n, 8 * n + 8)
        points = []
        for m in range(RADIX):
            value = (line_ref[m, rows, :SUB], line_ref[m, rows, SUB:])
            if m > 0:
                value = twiddle_pair(value, cosine_ref[m : m + 1], sine_ref[m : m + 1], 1)
            points.append(value)
        for k, (real, imag) in enumerate(butterflies(points, turn_pair(1))):
            lanes = slice(SUB * k, SUB * k + SUB)
            factor_real, factor_imag = fr_ref[n, :, lanes], fi_ref[n, :, lanes]
            field_ref[k, 2 * n] = real * factor_real - imag * factor_imag
            field_ref[k, 2 * n + 1] = real * factor_imag + imag * factor_real

    def one_block(k, carry):
        def load(n):
            return field_ref[k, 2 * n - 2], field_ref[k, 2 * n - 1]

        def store(n, real, imag):
            if last:
                start = 128 * (n - 1) + 2 * k
                out_ref[pl.ds(start, 8, stride=16), :] = real
                out_ref[pl.ds(start + 1, 8, stride=16), :] = imag
            else:
                line_ref[k, 8 * n - 8 : 8 * n, :SUB] = real
                line_ref[k, 8 * n - 8 : 8 * n, SUB:] = imag

        couple_pixels(load, gain_ref[k], store)
        return carry

    lax.fori_loop(0, RADIX, one_block, 0)
    if last:
        return
    for n in range(0, H, 2):
        rows = slice(8 * n, 8 * n + 16)
        points = [(line_ref[k, rows, :SUB], line_ref[k, rows, SUB:]) for k in range(RADIX)]

        def store_parts(m, high, low):
            high_ref[m, rows, :] = high
            low_ref[m, rows, :] = low

        forward_lanes(points, store_parts, cosine_ref, sine_ref)
    for m in range(RADIX):
        result = triple_dot(high_ref[m], low_ref[m], gh_ref[...], gl_ref[...])
        for n in range(H):
            for half in range(2):
                out_ref[n // local_harm, 2 * m + half, n % local_harm] = result[
                    8 * n : 8 * n + 8, SUB * half : SUB * half + SUB
                ]


def pixels(wavefield, factor_real, factor_imag, gain, constants, last):
    (gh, gl), (ih, il), (cosine, sine) = constants["lane"]
    operands = [wavefield, factor_real, factor_imag, gain, gh, gl, ih, il, cosine, sine]
    out_shape = (H * 8 * 16, SUB) if last else wavefield.shape
    return pl.pallas_call(
        functools.partial(pixel_kernel, last),
        in_specs=[pl.BlockSpec(memory_space=pltpu.VMEM) for _ in operands],
        out_specs=pl.BlockSpec(memory_space=pltpu.VMEM),
        out_shape=jax.ShapeDtypeStruct(out_shape, jnp.float32),
        scratch_shapes=[
            pltpu.VMEM((RADIX, 8 * H, 2 * SUB), jnp.bfloat16),
            pltpu.VMEM((RADIX, 8 * H, 2 * SUB), jnp.bfloat16),
            pltpu.VMEM((RADIX, 8 * H, 2 * SUB), jnp.float32),
            pltpu.VMEM((RADIX, 2 * H, 8, SUB), jnp.float32),
        ],
        compiler_params=pltpu.CompilerParams(vmem_limit_bytes=VMEM_LIMIT),
        cost_estimate=pl.CostEstimate(
            flops=2 * 3 * 2 * 8 * H * RADIX * 65536,
            bytes_accessed=4 * wavefield.size * 4,
            transcendentals=0,
        ),
        name="pixels_last" if last else "pixels",
    )(*operands)


def squared_freq_at(indices, length):
    centred = jnp.where(indices < length // 2, indices, indices - length).astype(jnp.float32)
    scaled = centred * (2.0 * math.pi / length)
    return scaled * scaled


def propagator(wave_number, down_square, across_square, march_step):
    axial_square = wave_number * wave_number - down_square - across_square
    axial_root = jnp.sqrt(jnp.abs(axial_square))
    phase_turn = march_step * axial_root
    propagating = axial_square >= 0.0
    prop_real = jnp.where(propagating, jnp.cos(phase_turn), jnp.exp(-phase_turn))
    prop_imag = jnp.where(propagating, jnp.sin(phase_turn), 0.0)
    return (prop_real, prop_imag)


def propagator_tables(local_harm):
    orders = (
        lax.axis_index("harm") * local_harm + jnp.arange(local_harm, dtype=jnp.int32) + 1
    ).astype(jnp.float32)
    place = lax.axis_index("rows")
    down = RADIX * jnp.arange(SUB, dtype=jnp.int32)[None, :] + jnp.arange(
        RADIX, dtype=jnp.int32
    )[:, None]
    lane = jnp.arange(SUB, dtype=jnp.int32)
    across = RADIX * (lax.rem(place, 2) * HALF + lax.rem(lane, HALF)) + place // 2
    real, imag = propagator(
        (3.0 / H * orders)[:, None, None, None],
        squared_freq_at(down, N)[None, :, :, None],
        squared_freq_at(across, N)[None, None, None, :],
        float(DZ),
    )
    factor = 1.0 / (N * N)
    sign = jnp.where(lane < HALF, -factor, factor).astype(jnp.float32)
    return real * factor, imag * sign


def screen_tables(contrast, absorption):
    orders = jnp.arange(1, H + 1, dtype=jnp.int32).astype(jnp.float32)[:, None, None]
    damping = jnp.exp(-absorption[None] * jnp.power(orders, 1.1) * float(DZ))
    angle = 3.0 / H * orders * float(DZ) * contrast[None]
    return damping * jnp.cos(angle), damping * jnp.sin(angle)


def shards(pressure, contrast, absorption, nonlinearity):
    local_harm = pressure.shape[0]
    constants = {
        "lane": lane_matrices() + (lane_twiddles(),),
        "row_matrices": row_matrices(),
        "row_twiddles": row_twiddles(),
    }
    constants = jax.tree.map(jnp.asarray, constants)
    axes = ("harm", "rows")
    pixel_rows = 8
    row_start = lax.axis_index("harm") * pixel_rows

    def own_rows(values):
        return lax.dynamic_slice_in_dim(values, row_start, pixel_rows, 0)

    gain = own_rows(nonlinearity) * (1.0 / (H * math.sqrt(H)))
    gain = gain.reshape(pixel_rows, RADIX, SUB).transpose(1, 0, 2)
    prop_real, prop_imag = propagator_tables(local_harm)
    factor_real, factor_imag = screen_tables(own_rows(contrast), own_rows(absorption))

    lines = first_transform(pressure, constants)
    lines = lax.all_to_all(lines, "rows", 0, 0, tiled=True)
    for plane_index in range(PLANES):
        marched = march(lines, prop_real, prop_imag, constants, plane_index == 0)
        shape = marched.shape
        marched = lax.all_to_all(marched.reshape((128,) + shape[2:]), axes, 0, 0, tiled=True)
        last = plane_index == PLANES - 1
        lines = pixels(
            marched.reshape(shape), factor_real, factor_imag, gain, constants, last
        )
        if not last:
            lines = lax.all_to_all(lines.reshape((128,) + shape[2:]), axes, 0, 0, tiled=True)
            lines = lines.reshape(shape)
    out = lines.reshape(8, local_harm * pixel_rows * 16, SUB)
    out = lax.all_to_all(out, "harm", 0, 0, tiled=True)
    out = out.reshape(8, local_harm, pixel_rows, RADIX, 2, SUB)
    out = out.transpose(1, 0, 2, 4, 3, 5)
    return out.reshape(local_harm, 8 * pixel_rows, 2, N)


def solution(mesh):
    in_specs = (P("harm", "rows", None, None), P("rows", None), P("rows", None), P("rows", None))
    out_specs = P("harm", "rows", None, None)
    return jax.shard_map(shards, mesh=mesh, in_specs=in_specs, out_specs=out_specs, check_vma=False)
```

time: 719 us -> 190 us (0.26)
  matrix products: 346 us -> 0 us
  local copies, waits for them, and re-layouts: 93.7 us -> 4.35 us
  other arithmetic: 58.5 us -> 14.5 us
  blocking collectives: 127 us -> 85.8 us
  Pallas kernels: 0 us -> 37.3 us
  waiting for transfers between devices: 67.4 us -> 31.8 us
    dot_general x16 -> x0, matrix products: 346 us -> none  [the longest x4 88 us: along_last(): jnp.dot(flattened, sine_table, precision=lax.Precision.HIGHEST)]
    all_to_all x5 -> x3, blocking collectives: 127 us -> 85.8 us  [the longest x1 29.9 us: shards(): lax.all_to_all(marched.reshape((128,) + shape[2:]), axes, 0, 0, tiled=True)]
    pallas_call x0 -> x5, Pallas kernels: none -> 37.3 us  [the longest x2 16.5 us: pixels(): pl.pallas_call(functools.partial(pixel_kernel, last), in_specs=[pl.BlockS...]
    all_to_all x3 -> x2, waiting for transfers between devices: 67.4 us -> 31.8 us  [the longest x1 17.7 us: shards(): lax.all_to_all(marched.reshape((128,) + shape[2:]), axes, 0, 0, tiled=True)]
    unnamed x20 -> x4, local copies, waits for them, and re-layouts: 31.4 us -> 2.28 us
    all_to_all x12 -> x0, local copies, waits for them, and re-layouts: 24.8 us -> none  [the longest x5 13.2 us: shards(): lax.all_to_all(wavefield, 'rows', split_axis=3, concat_axis=1, tiled=True)]
    all_to_all x4 -> x0, other arithmetic: 23.7 us -> none  [the longest x2 11.8 us: shards(): lax.all_to_all(wavefield, 'rows', split_axis=1, concat_axis=3, tiled=True)]
    another operation x7 -> x0, local copies, waits for them, and re-layouts: 20.8 us -> none  [the longest x4 17.1 us: combine(): return jnp.stack([out_real, out_imag], axis=-2)]
  transfers between devices with their start and end apart: 3 -> 2, of which waited for: 3 -> 2; matrix products, arithmetic and copies ran while one was open for 0% -> 8% of each run, Pallas kernels for 0% -> 0%
where the time goes in v1:
time: 190 us; the launch traced here: 189 us
  blocking collectives  85.8 us (45%)
  Pallas kernels  37.3 us (20%)
  waiting for transfers between devices  31.8 us (17%)
  starting transfers between devices  15.2 us (8%)
  other arithmetic  14.5 us (8%)
  local copies, waits for them, and re-layouts  4.35 us (2%)
    all_to_all x1, blocking collectives, shards(): lax.all_to_all(marched.reshape((128,) + shape[2:]), axes, 0, 0, tiled=True)  29.9 us
    all_to_all x1, blocking collectives, shards(): lax.all_to_all(lines.reshape((128,) + shape[2:]), axes, 0, 0, tiled=True)  29.9 us
    all_to_all x1, blocking collectives, shards(): out = lax.all_to_all(out, 'harm', 0, 0, tiled=True)  26.1 us
    all_to_all x1, waiting for transfers between devices, shards(): lax.all_to_all(marched.reshape((128,) + shape[2:]), axes, 0, 0, tiled=True)  17.7 us
    pallas_call x2, Pallas kernels, pixels(): pl.pallas_call(functools.partial(pixel_kernel, last), in_specs=[pl.BlockS...  16.5 us
    pallas_call x2, Pallas kernels, march(): pl.pallas_call(functools.partial(march_kernel, load), grid=(local_harm,),...  16 us
    all_to_all x1, waiting for transfers between devices, shards(): lines = lax.all_to_all(lines, 'rows', 0, 0, tiled=True)  14.1 us
    all_to_all x1, starting transfers between devices, shards(): lax.all_to_all(marched.reshape((128,) + shape[2:]), axes, 0, 0, tiled=True)  9.17 us
  transfers between devices with their start and end apart: 2, of which 2 were waited for; matrix products, arithmetic and copies ran while one was open for 8% of the time, Pallas kernels for 0%

profile of v1, /device:TPU:0, one launch (start us, length us, event | category | flops | bytes accessed | tf_op | source)
XLA Modules:
  0.0 189.0 jit_solution(10480336667750904837)
XLA Ops:
  0.0 4.7 %first_transform.1 = f32[16,3,64,128]{3,2,1,0:T(8,128)} custom-call(f32[3072,128]{1,0:T(8,128)} %bitcast.31, bf16[256,256]{1,0:T(8,128)(2,1)} %constant.91.clone.gh_ref, bf16[256,256]{1,0:T(8,128)(2,1)} %constant.92.clone.gl_ref, f32[8,128]{1,0:T(8,128)} %constant.95.clone.cosine_ref, f32[8,128]{1,0:T(8,128)} %constant.96.clone.sine_ref), custom_call_target="tpu_custom_call" | custom-call | flops 603979776 | bytes 3145728 | tf_op jit(solution)/shard_map/first_transform/pallas_call | solution.py:180
  4.7 6.0 %all-to-all-start = ((f32[16,3,64,128]{3,2,1,0:T(8,128)}), f32[16,3,64,128]{3,2,1,0:T(8,128)S(1)}, u32[]{:S(2)}, u32[]{:S(2)}) async-start(f32[16,3,64,128]{3,2,1,0:T(8,128)} %first_transform.1), calls=%async_computation | async-start | bytes 3145728 | tf_op jit(solution)/shard_map/all_to_all | solution.py:543
  10.8 0.1 broadcast_subtract_fusion
  10.9 7.8 %fusion.3 = (f32[3,8,128,128]{3,2,1,0:T(8,128)}, f32[3,8,128,128]{3,2,1,0:T(8,128)}) fusion(f32[128]{0:T(128)S(1)} %get-tuple-element.9, f32[128]{0:T(128)S(1)} %get-tuple-element.10, f32[3,8,128]{2,1,0:T(8,128)S(1)} %broadcast_subtract_fusion), kind=kLoop, calls=%fused_computation.5 | loop fusion | flops 3538944 | bytes 3159040 | tf_op jit(solution)/shard_map/mul | solution.py:512
  18.7 14.1 %all-to-all-done.in_ref = f32[16,3,64,128]{3,2,1,0:T(8,128)S(1)} async-done(((f32[16,3,64,128]{3,2,1,0:T(8,128)}), f32[16,3,64,128]{3,2,1,0:T(8,128)S(1)}, u32[]{:S(2)}, u32[]{:S(2)}) %all-to-all-start) | async-done | bytes 1572896 | tf_op jit(solution)/shard_map/all_to_all | solution.py:543
  32.8 0.0 copy-start
  32.8 1.1 copy-done
  34.0 7.9 %march.2 = f32[8,16,3,8,128]{4,3,2,1,0:T(8,128)} custom-call(f32[16,3,64,128]{3,2,1,0:T(8,128)} %copy-done, f32[3,8,128,128]{3,2,1,0:T(8,128)} %get-tuple-element.8.pr_ref, f32[3,8,128,128]{3,2,1,0:T(8,128)} %get-tuple-element.7.pi_ref, bf16[256,256]{1,0:T(8,128)(2,1)} %constant.97.clone.mh_ref, bf16[256,128]{1,0:T(8,128)(2,1)} %constant.98.clone.ml_ref, ...), custom_call_target="tpu_custom_call" | custom-call | flops 1610612736 | bytes 6291456 | tf_op jit(solution)/shard_map/march/pallas_call | solution.py:293
  41.9 9.2 %all-to-all-start.1 = ((f32[128,3,8,128]{3,2,1,0:T(8,128)}), f32[128,3,8,128]{3,2,1,0:T(8,128)S(1)}, u32[]{:S(2)}, u32[]{:S(2)}) async-start(f32[128,3,8,128]{3,2,1,0:T(8,128)} %bitcast.22), calls=%async_computation.1 | async-start | bytes 3145728 | tf_op jit(solution)/shard_map/all_to_all | solution.py:547
  51.1 1.4 multiply_bitcast_fusion.gain_ref
  52.5 0.8 dynamic-slice_negate_fusion
  53.3 4.4 %fusion.11 = (f32[24,8,1024]{2,1,0:T(8,128)}, f32[24,8,1024]{2,1,0:T(8,128)}) fusion(f32[8,1024]{1,0:T(8,128)S(1)} %get-tuple-element.12, f32[24]{0:T(128)S(1)} %get-tuple-element.13, f32[24]{0:T(128)S(1)} %get-tuple-element.14, f32[8,1024]{1,0:T(8,128)S(1)} %get-tuple-element.11), kind=kLoop, calls=%fused_computation.16 | loop fusion | flops 983040 | bytes 1638592 | tf_op jit(solution)/shard_map/mul | solution.py:519
  57.7 17.7 %all-to-all-done.1 = f32[128,3,8,128]{3,2,1,0:T(8,128)S(1)} async-done(((f32[128,3,8,128]{3,2,1,0:T(8,128)}), f32[128,3,8,128]{3,2,1,0:T(8,128)S(1)}, u32[]{:S(2)}, u32[]{:S(2)}) %all-to-all-start.1) | async-done | bytes 1572896 | tf_op jit(solution)/shard_map/all_to_all | solution.py:547
  75.4 0.0 copy-start.1
  75.4 1.1 copy-done.1
  76.5 8.7 %pixels.1 = f32[8,16,3,8,128]{4,3,2,1,0:T(8,128)} custom-call(f32[8,16,3,8,128]{4,3,2,1,0:T(8,128)} %bitcast.27, f32[24,8,1024]{2,1,0:T(8,128)} %get-tuple-element.6.fr_ref, f32[24,8,1024]{2,1,0:T(8,128)} %get-tuple-element.5.fi_ref, f32[8,8,128]{2,1,0:T(8,128)} %multiply_bitcast_fusion.gain_ref, bf16[256,256]{1,0:T(8,128)(2,1)} %constant.91.clone.gh_ref, ...), custom_call_target="tpu_custom_call" | custom-call | flops 1207959552 | bytes 6291456 | tf_op jit(solution)/shard_map/pixels/pallas_call | solution.py:457
  85.2 29.9 %all_to_all.25 = f32[128,3,8,128]{3,2,1,0:T(8,128)} all-to-all(f32[128,3,8,128]{3,2,1,0:T(8,128)} %bitcast.30), channel_id=1, replica_groups=mesh['harm'=8,'rows'=16] {'harm','rows'}, dimensions={0} | all-to-all | bytes 3145728 | tf_op jit(solution)/shard_map/all_to_all | solution.py:553
  115.1 8.1 %march.3 = f32[8,16,3,8,128]{4,3,2,1,0:T(8,128)} custom-call(f32[8,16,3,8,128]{4,3,2,1,0:T(8,128)} %bitcast.23, f32[3,8,128,128]{3,2,1,0:T(8,128)} %get-tuple-element.8.pr_ref, f32[3,8,128,128]{3,2,1,0:T(8,128)} %get-tuple-element.7.pi_ref, bf16[256,256]{1,0:T(8,128)(2,1)} %constant.97.clone.mh_ref, bf16[256,128]{1,0:T(8,128)(2,1)} %constant.98.clone.ml_ref, ...), custom_call_target="tpu_custom_call" | custom-call | flops 1610612736 | bytes 6291456 | tf_op jit(solution)/shard_map/march/pallas_call | solution.py:293
  123.1 29.9 %all_to_all.26 = f32[128,3,8,128]{3,2,1,0:T(8,128)} all-to-all(f32[128,3,8,128]{3,2,1,0:T(8,128)} %bitcast.24), channel_id=1, replica_groups=mesh['harm'=8,'rows'=16] {'harm','rows'}, dimensions={0} | all-to-all | bytes 3145728 | tf_op jit(solution)/shard_map/all_to_all | solution.py:547
  153.0 7.8 %pixels_last.1 = f32[3072,128]{1,0:T(8,128)} custom-call(f32[8,16,3,8,128]{4,3,2,1,0:T(8,128)} %bitcast.28, f32[24,8,1024]{2,1,0:T(8,128)} %get-tuple-element.6.fr_ref, f32[24,8,1024]{2,1,0:T(8,128)} %get-tuple-element.5.fi_ref, f32[8,8,128]{2,1,0:T(8,128)} %multiply_bitcast_fusion.gain_ref, bf16[256,256]{1,0:T(8,128)(2,1)} %constant.91.clone.gh_ref, ...), custom_call_target="tpu_custom_call" | custom-call | flops 1207959552 | bytes 6291456 | tf_op jit(solution)/shard_map/pixels_last/pallas_call | solution.py:457
  160.8 26.1 %all_to_all.27 = f32[8,384,128]{2,1,0:T(8,128)S(1)} all-to-all(f32[8,384,128]{2,1,0:T(8,128)} %bitcast.29), channel_id=1, replica_groups=mesh['harm'=8,'rows'=16] {'harm'}, dimensions={0} | all-to-all | bytes 3145728 | tf_op jit(solution)/shard_map/all_to_all | solution.py:556
  187.0 0.1 copy.18
  187.1 1.9 %reshape.127 = f32[3,64,2,1024]{3,2,1,0:T(2,128)} reshape(f32[3,8,8,2,8,128]{5,4,3,2,1,0:T(8,128)S(1)} %bitcast.26) | data formatting | bytes 3145728 | tf_op jit(solution)/shard_map/reshape | solution.py:559
  (5 shorter events, 0.0 us)
Async XLA Ops:
  4.7 28.1 %all-to-all-start = ((f32[16,3,64,128]{3,2,1,0:T(8,128)}), f32[16,3,64,128]{3,2,1,0:T(8,128)S(1)}, u32[]{:S(2)}, u32[]{:S(2)}) async-start(f32[16,3,64,128]{3,2,1,0:T(8,128)} %first_transform.1), calls=%async_computation | async-start | bytes 3145728 | tf_op jit(solution)/shard_map/all_to_all | solution.py:543
  32.8 1.1 copy-start
  41.9 33.5 %all-to-all-start.1 = ((f32[128,3,8,128]{3,2,1,0:T(8,128)}), f32[128,3,8,128]{3,2,1,0:T(8,128)S(1)}, u32[]{:S(2)}, u32[]{:S(2)}) async-start(f32[128,3,8,128]{3,2,1,0:T(8,128)} %bitcast.22), calls=%async_computation.1 | async-start | bytes 3145728 | tf_op jit(solution)/shard_map/all_to_all | solution.py:547
  75.4 1.1 copy-start.1

commit v2 on v1

v2 whole, which is shorter than its diff:
```python
import functools
import math

import jax
import jax.numpy as jnp
import ml_dtypes
import numpy as np
from jax import lax
from jax.experimental import pallas as pl
from jax.experimental.pallas import tpu as pltpu
from jax.sharding import PartitionSpec as P

H = 24
N = 1024
PLANES = 2
DZ = 128
RADIX = 8
SUB = N // RADIX
HALF = SUB // 2
ROOT_HALF = math.sqrt(0.5)
VMEM_LIMIT = 20 * 1024 * 1024


def split_constant(table):
    high = table.astype(np.float32).astype(ml_dtypes.bfloat16)
    low = (table - high.astype(np.float64)).astype(np.float32).astype(ml_dtypes.bfloat16)
    return high, low


def stack_constant(table):
    high, low = split_constant(table)
    return np.concatenate([high, high, low], 0)


def sub_angles():
    index = np.arange(SUB)
    return 2.0 * np.pi / SUB * ((index[:, None] * index[None, :]) % SUB)


def lane_matrices():
    cosine, sine = np.cos(sub_angles()), np.sin(sub_angles())
    forward_real = np.concatenate([cosine, sine], 0)
    forward_imag = np.concatenate([-sine, cosine], 0)
    inverse_real = np.concatenate([cosine, -sine], 0)
    inverse_imag = np.concatenate([sine, cosine], 0)
    forward = np.concatenate(
        [
            forward_real[:, :HALF],
            forward_imag[:, :HALF],
            forward_real[:, HALF:],
            forward_imag[:, HALF:],
        ],
        1,
    )
    inverse = np.concatenate([inverse_real, inverse_imag], 1)
    inverse = np.concatenate(
        [
            inverse[:HALF],
            inverse[SUB : SUB + HALF],
            inverse[HALF:SUB],
            inverse[SUB + HALF :],
        ],
        0,
    )
    return stack_constant(forward), stack_constant(inverse)


def lane_twiddles():
    angle = 2.0 * np.pi / N * (np.arange(RADIX)[:, None] * np.arange(SUB)[None, :])
    return np.stack([np.cos(angle), np.sin(angle)]).astype(np.float32)


def row_matrices():
    both = np.concatenate([np.cos(sub_angles()), np.sin(sub_angles())], 0)
    high, low = split_constant(both)
    return np.concatenate([high, high, low], 1)


def row_twiddles():
    angle = 2.0 * np.pi / N * (np.arange(RADIX)[:, None] * np.arange(SUB)[None, :])
    sign = np.where(np.arange(SUB) < HALF, 1.0, -1.0)
    cosine = np.broadcast_to(np.cos(angle)[:, :, None], (RADIX, SUB, SUB))
    sine = np.sin(angle)[:, :, None] * sign[None, None, :]
    return np.stack([cosine, sine]).astype(np.float32)


def split_value(value):
    high = value.astype(jnp.bfloat16)
    low = (value - high.astype(jnp.float32)).astype(jnp.bfloat16)
    return high, low


def add(left, right):
    return tuple(a + b for a, b in zip(left, right))


def subtract(left, right):
    return tuple(a - b for a, b in zip(left, right))


def scale(value, factor):
    return tuple(a * factor for a in value)


def turn_pair(direction):
    def turn(value):
        real, imag = value
        return (imag, -real) if direction < 0 else (-imag, real)

    return turn


def butterflies(points, turn):
    even = [add(points[k], points[k + 4]) for k in range(4)]
    odd = [subtract(points[k], points[k + 4]) for k in range(4)]
    turned = turn(odd[1])
    first = scale(add(odd[1], turned), ROOT_HALF)
    second = turn(odd[2])
    turned = turn(odd[3])
    third = scale(subtract(turned, odd[3]), ROOT_HALF)
    out = [None] * RADIX
    for offset, (a, b, c, d) in ((0, even), (1, (odd[0], first, second, third))):
        sum_ac, diff_ac = add(a, c), subtract(a, c)
        sum_bd, diff_bd = add(b, d), turn(subtract(b, d))
        out[offset] = add(sum_ac, sum_bd)
        out[offset + 4] = subtract(sum_ac, sum_bd)
        out[offset + 2] = add(diff_ac, diff_bd)
        out[offset + 6] = subtract(diff_ac, diff_bd)
    return out


def product(left, right):
    return jnp.dot(left, right, preferred_element_type=jnp.float32)


def store_parts(part_ref, rows, value):
    high, low = split_value(value)
    part_ref[rows, :256] = high
    part_ref[rows, 256:512] = low
    part_ref[rows, 512:] = high


def twiddle_pair(value, cosine, sine, direction):
    real, imag = value
    if direction < 0:
        return real * cosine + imag * sine, imag * cosine - real * sine
    return real * cosine - imag * sine, imag * cosine + real * sine


def fetch(sources, targets, sems):
    copies = [
        pltpu.make_async_copy(source, target, sems.at[index])
        for index, (source, target) in enumerate(zip(sources, targets))
    ]
    for copy in copies:
        copy.start()
    return copies


def forward_lanes(points, store, twiddle_ref):
    for m, value in enumerate(butterflies(points, turn_pair(-1))):
        if m > 0:
            value = twiddle_pair(value, twiddle_ref[0, m : m + 1], twiddle_ref[1, m : m + 1], -1)
        store(m, jnp.concatenate(value, axis=1))


def first_kernel(
    in_ref, g_hbm, twiddle_hbm, out_ref, line_ref, part_ref, g_ref, twiddle_ref, sems
):
    local_harm, rows = out_ref.shape[1], out_ref.shape[2]
    lines = rows * 2 * RADIX
    copies = fetch(
        [in_ref.at[pl.ds(n * lines, lines)] for n in range(local_harm)] + [twiddle_hbm, g_hbm],
        [line_ref.at[n] for n in range(local_harm)] + [twiddle_ref, g_ref],
        sems,
    )
    copies[local_harm].wait()
    for n in range(local_harm):
        copies[n].wait()

        def one_tile(t, carry, n=n):
            start = pl.multiple_of(t * 16, 16)
            points = [
                tuple(
                    line_ref[n, pl.ds(start * 16 + 2 * k + c, 16, stride=16), :]
                    for c in range(2)
                )
                for k in range(RADIX)
            ]

            def store(m, value):
                first = (m * local_harm + n) * rows
                store_parts(part_ref, pl.ds(pl.multiple_of(first + start, 16), 16), value)

            forward_lanes(points, store, twiddle_ref)
            return carry

        lax.fori_loop(0, rows // 16, one_tile, 0)
    copies[local_harm + 1].wait()
    result = product(part_ref[...], g_ref[...])
    for m in range(RADIX):
        for n in range(local_harm):
            first = (m * local_harm + n) * rows
            out_ref[2 * m, n] = result[first : first + rows, :SUB]
            out_ref[2 * m + 1, n] = result[first : first + rows, SUB:]


IN_VMEM = pl.BlockSpec(memory_space=pltpu.VMEM)
IN_HBM = pl.BlockSpec(memory_space=pltpu.HBM)


def in_vmem(*arrays):
    return [pltpu.with_memory_space_constraint(array, pltpu.VMEM) for array in arrays]


def in_hbm(*arrays):
    return [pltpu.with_memory_space_constraint(array, pltpu.HBM) for array in arrays]


def first_transform(pressure, constants):
    local_harm, rows = pressure.shape[0], pressure.shape[1]
    lines = pressure.reshape(local_harm, rows, 2, RADIX, SUB).transpose(0, 1, 3, 2, 4)
    lines = lines.reshape(local_harm * rows * 16, SUB)
    forward, _, twiddles = constants["lane"]
    return pl.pallas_call(
        first_kernel,
        in_specs=[IN_HBM] * 3,
        out_specs=IN_VMEM,
        out_shape=pltpu.VMEM((16, local_harm, rows, SUB), jnp.float32),
        scratch_shapes=[
            pltpu.VMEM((local_harm, rows * 16, SUB), jnp.float32),
            pltpu.VMEM((RADIX * local_harm * rows, 768), jnp.bfloat16),
            pltpu.VMEM(forward.shape, forward.dtype),
            pltpu.VMEM(twiddles.shape, twiddles.dtype),
            pltpu.SemaphoreType.DMA((local_harm + 2,)),
        ],
        compiler_params=pltpu.CompilerParams(vmem_limit_bytes=VMEM_LIMIT),
        cost_estimate=pl.CostEstimate(
            flops=3 * 2 * local_harm * rows * RADIX * 65536,
            bytes_accessed=2 * lines.size * 4,
            transcendentals=0,
        ),
        name="first_transform",
    )(*in_hbm(lines, forward, twiddles))


def march_fetching(
    in_ref,
    prop_hbm,
    m_hbm,
    twiddle_hbm,
    screen_ref,
    gain_ref,
    out_ref,
    part_ref,
    spec_ref,
    prop_ref,
    m_ref,
    twiddle_ref,
    sems,
):
    local_harm = out_ref.shape[2]
    copies = fetch(
        [twiddle_hbm, m_hbm] + [prop_hbm.at[:, n] for n in range(local_harm)],
        [twiddle_ref, m_ref] + [prop_ref.at[:, n] for n in range(local_harm)],
        sems,
    )
    copies[0].wait()
    copies[1].wait()

    def wait(n):
        pltpu.make_async_copy(prop_hbm.at[:, n], prop_ref.at[:, n], sems.at[2 + n]).wait()

    march_kernel(
        True, wait, in_ref, prop_ref, m_ref, twiddle_ref, out_ref, part_ref, spec_ref
    )


def march_kernel(
    by_rows, wait, in_ref, prop_ref, m_ref, twiddle_ref, out_ref, part_ref, spec_ref
):
    local_harm = out_ref.shape[2]
    lane = lax.broadcasted_iota(jnp.int32, (8, SUB), 1)
    sign = jnp.where(lane < HALF, 1.0, -1.0).astype(jnp.float32)

    def swap(value):
        return pltpu.roll(value, HALF, 1)

    def turn_forward(value):
        return (sign * swap(value[0]),)

    def turn_inverse(value):
        return (-sign * swap(value[0]),)

    def load(n, block, tile):
        if by_rows:
            return in_ref[block, n, 8 * tile : 8 * tile + 8, :]
        return in_ref[tile, block, n]

    def store(pair, m, value):
        lanes = slice(SUB * m, SUB * m + SUB)
        high, low = split_value(value)
        for part, data in enumerate((high, low, high)):
            first = SUB * part + 16 * pair
            part_ref[first : first + 16, lanes] = data

    def one_harmonic(n, carry):
        for pair in range(SUB // 16):
            outs = []
            for tile in (2 * pair, 2 * pair + 1):
                points = [(load(n, 2 * k + tile // 8, tile % 8),) for k in range(RADIX)]
                values = butterflies(points, turn_forward)
                rows = slice(8 * tile, 8 * tile + 8)
                outs.append(
                    [
                        value[0]
                        if m == 0
                        else value[0] * twiddle_ref[0, m, rows]
                        + swap(value[0]) * twiddle_ref[1, m, rows]
                        for m, value in enumerate(values)
                    ]
                )
            for m in range(RADIX):
                store(pair, m, jnp.concatenate([outs[0][m], outs[1][m]], 0))
        spec_ref[...] = product(m_ref[...], part_ref[...])
        wait(n)
        for m in range(RADIX):
            lanes = slice(SUB * m, SUB * m + SUB)
            for pair in range(SUB // 16):
                outs = []
                for tile in (2 * pair, 2 * pair + 1):
                    rows = slice(8 * tile, 8 * tile + 8)
                    value = spec_ref[rows, lanes] + sign * swap(
                        spec_ref[SUB + 8 * tile : SUB + 8 * tile + 8, lanes]
                    )
                    outs.append(value * prop_ref[0, n, m, rows] + swap(value) * prop_ref[1, n, m, rows])
                store(pair, m, jnp.concatenate(outs, 0))
        spec_ref[...] = product(m_ref[...], part_ref[...])
        for tile in range(SUB // 8):
            rows = slice(8 * tile, 8 * tile + 8)
            points = []
            for m in range(RADIX):
                lanes = slice(SUB * m, SUB * m + SUB)
                value = spec_ref[rows, lanes] - sign * swap(
                    spec_ref[SUB + 8 * tile : SUB + 8 * tile + 8, lanes]
                )
                if m > 0:
                    value = (
                        value * twiddle_ref[0, m, rows] - swap(value) * twiddle_ref[1, m, rows]
                    )
                points.append((value,))
            for k, value in enumerate(butterflies(points, turn_inverse)):
                out_ref[tile % 8, 2 * k + tile // 8, n] = value[0]
        return carry

    lax.fori_loop(0, local_harm, one_harmonic, 0)


def march(wavefield, prop, after, constants, by_rows):
    local_harm = wavefield.shape[1 if by_rows else 2]
    tables = [prop, constants["row_matrices"], constants["row_twiddles"]]
    scratch = [
        pltpu.VMEM((3 * SUB, N), jnp.bfloat16),
        pltpu.VMEM((2 * SUB, N), jnp.float32),
    ]
    if by_rows:
        kernel = march_fetching
        operands = in_vmem(wavefield) + in_hbm(*tables, *after)
        in_specs = [IN_VMEM] + [IN_HBM] * (len(operands) - 1)
        scratch += [pltpu.VMEM(table.shape, table.dtype) for table in tables]
        scratch.append(pltpu.SemaphoreType.DMA((2 + local_harm,)))
    else:
        kernel = functools.partial(march_kernel, False, lambda n: None)
        operands = in_vmem(wavefield, *tables)
        in_specs = [IN_VMEM] * len(operands)
    return pl.pallas_call(
        kernel,
        in_specs=in_specs,
        out_specs=IN_VMEM,
        out_shape=pltpu.VMEM((8, 16, local_harm, 8, SUB), jnp.float32),
        scratch_shapes=scratch,
        compiler_params=pltpu.CompilerParams(vmem_limit_bytes=VMEM_LIMIT),
        cost_estimate=pl.CostEstimate(
            flops=2 * 2 * 2 * local_harm * 256 * 256 * N,
            bytes_accessed=4 * wavefield.size * 4,
            transcendentals=0,
        ),
        name="march",
    )(*operands)


def pair_order():
    block = 4
    order = []
    for low in range(0, H, block):
        for high in range(low, H, block):
            order += [
                (m, l)
                for m in range(high + 1, high + block + 1)
                for l in range(low + 1, low + block + 1)
                if m > l
            ]
    return order


def couple_pixels(load, gain, store):
    total_real = [None] * (H + 1)
    total_imag = [None] * (H + 1)

    def accumulate(n, real, imag):
        total_real[n] = real if total_real[n] is None else total_real[n] + real
        total_imag[n] = imag if total_imag[n] is None else total_imag[n] + imag

    for m, l in pair_order():
        (a, b), (c, d) = load(m), load(l)
        ac, bd, ad, bc = a * c, b * d, a * d, b * c
        accumulate(m - l, ac + bd, bc - ad)
        if m + l <= H:
            accumulate(m + l, ac - bd, ad + bc)
    for m in range(1, H // 2 + 1):
        a, b = load(m)
        accumulate(2 * m, 0.5 * (a * a - b * b), a * b)
    for n in range(1, H + 1):
        a, b = load(n)
        weight = (2.0 * n) * gain
        if total_real[n] is None:
            store(n, a, b)
        else:
            store(n, a - weight * total_imag[n], b + weight * total_real[n])


def pixel_kernel(
    last,
    in_ref,
    inverse_ref,
    twiddle_ref,
    screen_ref,
    gain_ref,
    forward_ref,
    out_ref,
    part_ref,
    line_ref,
    field_ref,
):
    local_harm = H // 8
    height = 8 * H

    def tile_of(n, r):
        return in_ref[n // local_harm, r, n % local_harm]

    for n in range(0, H, 2):
        for m in range(RADIX):
            value = jnp.concatenate(
                [
                    jnp.concatenate([tile_of(n + i, 2 * m), tile_of(n + i, 2 * m + 1)], 1)
                    for i in range(2)
                ],
                0,
            )
            first = height * m + 8 * n
            store_parts(part_ref, slice(first, first + 16), value)
    line_ref[...] = product(part_ref[...], inverse_ref[...])

    def one_order(n, carry):
        points = []
        for m in range(RADIX):
            rows = pl.ds(pl.multiple_of(height * m + 8 * n, 8), 8)
            value = (line_ref[rows, :SUB], line_ref[rows, SUB:])
            if m > 0:
                value = twiddle_pair(value, twiddle_ref[0, m : m + 1], twiddle_ref[1, m : m + 1], 1)
            points.append(value)
        for k, (real, imag) in enumerate(butterflies(points, turn_pair(1))):
            lanes = slice(SUB * k, SUB * k + SUB)
            factor_real, factor_imag = screen_ref[0, n, :, lanes], screen_ref[1, n, :, lanes]
            field_ref[k, 2 * n] = real * factor_real - imag * factor_imag
            field_ref[k, 2 * n + 1] = real * factor_imag + imag * factor_real
        return carry

    lax.fori_loop(0, H, one_order, 0, unroll=2)

    def one_block(k, carry):
        def load(n):
            return field_ref[k, 2 * n - 2], field_ref[k, 2 * n - 1]

        def store(n, real, imag):
            if last:
                start = 128 * (n - 1) + 2 * k
                out_ref[pl.ds(start, 8, stride=16), :] = real
                out_ref[pl.ds(start + 1, 8, stride=16), :] = imag
            else:
                rows = pl.ds(pl.multiple_of(height * k + 8 * n - 8, 8), 8)
                line_ref[rows, :SUB] = real
                line_ref[rows, SUB:] = imag

        couple_pixels(load, gain_ref[k], store)
        return carry

    lax.fori_loop(0, RADIX, one_block, 0)
    if last:
        return

    def one_pair(pair, carry):
        def rows(block):
            return pl.ds(pl.multiple_of(height * block + 16 * pair, 16), 16)

        points = [(line_ref[rows(k), :SUB], line_ref[rows(k), SUB:]) for k in range(RADIX)]
        forward_lanes(
            points,
            lambda m, value: store_parts(part_ref, rows(m), value),
            twiddle_ref,
        )
        return carry

    lax.fori_loop(0, H // 2, one_pair, 0)
    result = product(part_ref[...], forward_ref[...])
    for m in range(RADIX):
        for n in range(H):
            first = height * m + 8 * n
            for half in range(2):
                out_ref[n // local_harm, 2 * m + half, n % local_harm] = result[
                    first : first + 8, SUB * half : SUB * half + SUB
                ]


def pixels(wavefield, screen, gain, constants, last):
    forward, inverse, twiddles = constants["lane"]
    tables = [inverse, twiddles, screen, gain, forward]
    operands = in_vmem(wavefield, *tables)
    out_shape = (H * 8 * 16, SUB) if last else wavefield.shape
    return pl.pallas_call(
        functools.partial(pixel_kernel, last),
        in_specs=[IN_VMEM] * len(operands),
        out_specs=IN_VMEM,
        out_shape=pltpu.VMEM(out_shape, jnp.float32),
        scratch_shapes=[
            pltpu.VMEM((RADIX * 8 * H, 768), jnp.bfloat16),
            pltpu.VMEM((RADIX * 8 * H, 2 * SUB), jnp.float32),
            pltpu.VMEM((RADIX, 2 * H, 8, SUB), jnp.float32),
        ],
        compiler_params=pltpu.CompilerParams(vmem_limit_bytes=VMEM_LIMIT),
        cost_estimate=pl.CostEstimate(
            flops=2 * 3 * 2 * 8 * H * RADIX * 65536,
            bytes_accessed=4 * wavefield.size * 4,
            transcendentals=0,
        ),
        name="pixels_last" if last else "pixels",
    )(*operands)


def order_kernel(in_ref, out_ref, sems):
    groups, local_harm = in_ref.shape[:2]
    pairs = [(h, n) for h in range(groups) for n in range(local_harm)]
    copies = fetch(
        [in_ref.at[h, n] for h, n in pairs], [out_ref.at[n, h] for h, n in pairs], sems
    )
    for copy in copies:
        copy.wait()


def order_rows(blocks):
    groups, local_harm = blocks.shape[:2]
    return pl.pallas_call(
        order_kernel,
        in_specs=[IN_VMEM],
        out_specs=IN_HBM,
        out_shape=jax.ShapeDtypeStruct((local_harm, groups) + blocks.shape[2:], blocks.dtype),
        scratch_shapes=[pltpu.SemaphoreType.DMA((groups * local_harm,))],
        name="order_rows",
    )(*in_vmem(blocks))


def squared_freq_at(indices, length):
    centred = jnp.where(indices < length // 2, indices, indices - length).astype(jnp.float32)
    scaled = centred * (2.0 * math.pi / length)
    return scaled * scaled


def propagator(wave_number, down_square, across_square, march_step):
    axial_square = wave_number * wave_number - down_square - across_square
    axial_root = jnp.sqrt(jnp.abs(axial_square))
    phase_turn = march_step * axial_root
    propagating = axial_square >= 0.0
    prop_real = jnp.where(propagating, jnp.cos(phase_turn), jnp.exp(-phase_turn))
    prop_imag = jnp.where(propagating, jnp.sin(phase_turn), 0.0)
    return (prop_real, prop_imag)


def propagator_tables(local_harm):
    orders = (
        lax.axis_index("harm") * local_harm + jnp.arange(local_harm, dtype=jnp.int32) + 1
    ).astype(jnp.float32)
    place = lax.axis_index("rows")
    down = RADIX * jnp.arange(SUB, dtype=jnp.int32)[None, :] + jnp.arange(
        RADIX, dtype=jnp.int32
    )[:, None]
    lane = jnp.arange(SUB, dtype=jnp.int32)
    across = RADIX * (lax.rem(place, 2) * HALF + lax.rem(lane, HALF)) + place // 2
    real, imag = propagator(
        (3.0 / H * orders)[:, None, None, None],
        squared_freq_at(down, N)[None, :, :, None],
        squared_freq_at(across, N)[None, None, None, :],
        float(DZ),
    )
    factor = 1.0 / (N * N)
    sign = jnp.where(lane < HALF, -factor, factor).astype(jnp.float32)
    return jnp.stack([real * factor, imag * sign])


def screen_tables(contrast, absorption):
    orders = jnp.arange(1, H + 1, dtype=jnp.int32).astype(jnp.float32)[:, None, None]
    damping = jnp.exp(-absorption[None] * jnp.power(orders, 1.1) * float(DZ))
    angle = 3.0 / H * orders * float(DZ) * contrast[None]
    return jnp.stack([damping * jnp.cos(angle), damping * jnp.sin(angle)])


def shards(pressure, contrast, absorption, nonlinearity):
    local_harm = pressure.shape[0]
    constants = {
        "lane": lane_matrices() + (lane_twiddles(),),
        "row_matrices": row_matrices(),
        "row_twiddles": row_twiddles(),
    }
    constants = jax.tree.map(jnp.asarray, constants)
    axes = ("harm", "rows")
    pixel_rows = 8
    row_start = lax.axis_index("harm") * pixel_rows

    def own_rows(values):
        return lax.dynamic_slice_in_dim(values, row_start, pixel_rows, 0)

    gain = own_rows(nonlinearity) * (1.0 / (H * math.sqrt(H)))
    gain = gain.reshape(pixel_rows, RADIX, SUB).transpose(1, 0, 2)
    prop = propagator_tables(local_harm)
    screen = screen_tables(own_rows(contrast), own_rows(absorption))

    lines = first_transform(pressure, constants)
    lines = lax.all_to_all(lines, "rows", 0, 0, tiled=True)
    for plane_index in range(PLANES):
        marched = march(lines, prop, (screen, gain), constants, plane_index == 0)
        shape = marched.shape
        marched = lax.all_to_all(marched.reshape((128,) + shape[2:]), axes, 0, 0, tiled=True)
        last = plane_index == PLANES - 1
        lines = pixels(marched.reshape(shape), screen, gain, constants, last)
        if not last:
            lines = lax.all_to_all(lines.reshape((128,) + shape[2:]), axes, 0, 0, tiled=True)
            lines = lines.reshape(shape)
    out = lines.reshape(8, local_harm, pixel_rows * 16, SUB)
    out = lax.all_to_all(out, "harm", 0, 0, tiled=True)
    out = order_rows(out).reshape(local_harm, 8 * pixel_rows, RADIX, 2, SUB)
    return out.transpose(0, 1, 3, 2, 4).reshape(local_harm, 8 * pixel_rows, 2, N)


def solution(mesh):
    in_specs = (P("harm", "rows", None, None), P("rows", None), P("rows", None), P("rows", None))
    out_specs = P("harm", "rows", None, None)
    return jax.shard_map(shards, mesh=mesh, in_specs=in_specs, out_specs=out_specs, check_vma=False)
```

time: 190 us -> 174 us (0.916)
  blocking collectives: 85.8 us -> 116 us
  waiting for transfers between devices: 31.8 us -> 7.29 us
  starting transfers between devices: 15.2 us -> 6.02 us
  Pallas kernels: 37.3 us -> 29.4 us
  local copies, waits for them, and re-layouts: 4.35 us -> 0.05 us
    all_to_all x1 -> x2, blocking collectives: 29.9 us -> 61.8 us  [shards(): lax.all_to_all(marched.reshape((128,) + shape[2:]), axes, 0, 0, tiled=True)]
    all_to_all x1 -> x0, waiting for transfers between devices: 17.7 us -> none  [shards(): lax.all_to_all(marched.reshape((128,) + shape[2:]), axes, 0, 0, tiled=True)]
    all_to_all x1 -> x0, starting transfers between devices: 9.17 us -> none  [shards(): lax.all_to_all(marched.reshape((128,) + shape[2:]), axes, 0, 0, tiled=True)]
    pallas_call x5 -> x6, Pallas kernels: 37.3 us -> 29.4 us  [the longest x2 12.2 us: pixels(): pl.pallas_call(functools.partial(pixel_kernel, last), in_specs=[IN_VMEM]...]
    all_to_all x1, waiting for transfers between devices: 14.1 us -> 7.29 us  [shards(): lines = lax.all_to_all(lines, 'rows', 0, 0, tiled=True)]
    another operation x0 -> x2, other arithmetic: none -> 3.09 us  [the longest x1 1.84 us: propagator_tables(): return jnp.stack([real * factor, imag * sign])]
    mul x2, other arithmetic: 12.3 us -> 9.36 us  [the longest x1 6.41 us: propagator_tables(): return jnp.stack([real * factor, imag * sign])]
    unnamed x4 -> x16, local copies, waits for them, and re-layouts: 2.28 us -> 0.05 us
  transfers between devices with their start and end apart: 2 -> 1, of which waited for: 2 -> 1; matrix products, arithmetic and copies ran while one was open for 8% -> 8% of each run, Pallas kernels for 0% -> 0%
where the time goes in v2:
time: 174 us
  blocking collectives  116 us (67%)
  Pallas kernels  29.4 us (17%)
  other arithmetic  14.7 us (8%)
  waiting for transfers between devices  7.29 us (4%)
  starting transfers between devices  6.02 us (3%)
    all_to_all x2, blocking collectives, shards(): lax.all_to_all(marched.reshape((128,) + shape[2:]), axes, 0, 0, tiled=True)  61.8 us
    all_to_all x1, blocking collectives, shards(): lax.all_to_all(lines.reshape((128,) + shape[2:]), axes, 0, 0, tiled=True)  28.6 us
    all_to_all x1, blocking collectives, shards(): out = lax.all_to_all(out, 'harm', 0, 0, tiled=True)  25.4 us
    pallas_call x2, Pallas kernels, pixels(): pl.pallas_call(functools.partial(pixel_kernel, last), in_specs=[IN_VMEM]...  12.2 us
    pallas_call x2, Pallas kernels, march(): pl.pallas_call(kernel, in_specs=in_specs, out_specs=IN_VMEM, out_shape=pl...  11.8 us
    all_to_all x1, waiting for transfers between devices, shards(): lines = lax.all_to_all(lines, 'rows', 0, 0, tiled=True)  7.29 us
    mul x1, other arithmetic, propagator_tables(): return jnp.stack([real * factor, imag * sign])  6.41 us
    all_to_all x1, starting transfers between devices, shards(): lines = lax.all_to_all(lines, 'rows', 0, 0, tiled=True)  6.02 us
  transfers between devices with their start and end apart: 1, of which 1 were waited for; matrix products, arithmetic and copies ran while one was open for 8% of the time, Pallas kernels for 0%

profile of v2, /device:TPU:0, one launch (start us, length us, event | category | flops | bytes accessed | tf_op | source)
XLA Modules:
  0.0 173.7 jit_solution(5526813998809234096)
XLA Ops:
  0.0 4.1 %first_transform.1 = f32[16,3,64,128]{3,2,1,0:T(8,128)} custom-call(f32[3072,128]{1,0:T(8,128)} %bitcast.28, bf16[768,256]{1,0:T(8,128)(2,1)} %constant.81.clone.g_hbm.forward_ref, f32[2,8,128]{2,1,0:T(8,128)} %constant.83.clone.twiddle_hbm.twiddle_ref), custom_call_target="tpu_custom_call" | custom-call | flops 603979776 | bytes 3145728 | tf_op jit(solution)/shard_map/first_transform/pallas_call | solution.py:225
  4.1 6.0 %all-to-all-start = ((f32[16,3,64,128]{3,2,1,0:T(8,128)}), f32[16,3,64,128]{3,2,1,0:T(8,128)S(1)}, u32[]{:S(2)}, u32[]{:S(2)}) async-start(f32[16,3,64,128]{3,2,1,0:T(8,128)} %first_transform.1), calls=%async_computation | async-start | bytes 3145728 | tf_op jit(solution)/shard_map/all_to_all | solution.py:637
  10.2 1.4 multiply_bitcast_fusion.gain_ref
  11.6 0.8 dynamic-slice_negate_fusion
  12.4 3.0 %fusion.10 = (f32[1,24,8,1024]{3,2,1,0:T(8,128)S(1)}, f32[1,24,8,1024]{3,2,1,0:T(8,128)S(1)}) fusion(f32[8,1024]{1,0:T(8,128)S(1)} %get-tuple-element.12, f32[24]{0:T(128)S(1)} %get-tuple-element.13, f32[24]{0:T(128)S(1)} %get-tuple-element.14, f32[8,1024]{1,0:T(8,128)S(1)} %get-tuple-element.11), kind=kLoop, calls=%fused_computation.16 | loop fusion | flops 983040 | bytes 1638592 | tf_op jit(solution)/shard_map/mul | solution.py:613
  15.4 1.3 pad_maximum_fusion.1.screen_ref
  16.6 0.1 broadcast_subtract_fusion
  16.7 6.4 %fusion.2 = (f32[1,3,8,128,128]{4,3,2,1,0:T(8,128)S(1)}, f32[1,3,8,128,128]{4,3,2,1,0:T(8,128)S(1)}) fusion(f32[128]{0:T(128)S(1)} %get-tuple-element.10, f32[3,8,128]{2,1,0:T(8,128)S(1)} %broadcast_subtract_fusion, f32[128]{0:T(128)S(1)} %get-tuple-element.9), kind=kLoop, calls=%fused_computation.5 | loop fusion | flops 3538944 | bytes 3159040 | tf_op jit(solution)/shard_map/mul | solution.py:606
  23.1 1.8 %pad_maximum_fusion.prop_hbm.prop_ref = f32[2,3,8,128,128]{4,3,2,1,0:T(8,128)} fusion(f32[1,3,8,128,128]{4,3,2,1,0:T(8,128)S(1)} %get-tuple-element.8, f32[1,3,8,128,128]{4,3,2,1,0:T(8,128)S(1)} %get-tuple-element.7), kind=kLoop, calls=%fused_computation | loop fusion | flops 786432 | bytes 6291456 | tf_op jit(solution)/shard_map/stack | solution.py:606
  25.0 7.3 %all-to-all-done.in_ref = f32[16,3,64,128]{3,2,1,0:T(8,128)S(1)} async-done(((f32[16,3,64,128]{3,2,1,0:T(8,128)}), f32[16,3,64,128]{3,2,1,0:T(8,128)S(1)}, u32[]{:S(2)}, u32[]{:S(2)}) %all-to-all-start) | async-done | bytes 1572896 | tf_op jit(solution)/shard_map/all_to_all | solution.py:637
  32.3 6.7 %march.2 = f32[8,16,3,8,128]{4,3,2,1,0:T(8,128)S(1)} custom-call(f32[16,3,64,128]{3,2,1,0:T(8,128)S(1)} %all-to-all-done.in_ref, f32[2,3,8,128,128]{4,3,2,1,0:T(8,128)} %pad_maximum_fusion.prop_hbm.prop_ref, bf16[256,384]{1,0:T(8,128)(2,1)} %constant.84.clone.m_hbm.m_ref, f32[2,8,128,128]{3,2,1,0:T(8,128)} %constant.85.clone.twiddle_hbm.twiddle_ref, ...), custom_call_target="tpu_custom_call" | custom-call | flops 1610612736 | bytes 6291456 | tf_op jit(solution)/shard_map/march/pallas_call | solution.py:376
  38.9 0.0 copy-start.1
  39.0 0.0 copy-start.3
  39.0 0.0 copy-start.4
  39.0 0.0 copy-start.6
  39.0 0.0 copy-start.7
  39.0 33.3 %all_to_all.25 = f32[128,3,8,128]{3,2,1,0:T(8,128)S(1)} all-to-all(f32[128,3,8,128]{3,2,1,0:T(8,128)S(1)} %bitcast.23), channel_id=1, replica_groups=mesh['harm'=8,'rows'=16] {'harm','rows'}, dimensions={0} | all-to-all | bytes 3145728 | tf_op jit(solution)/shard_map/all_to_all | solution.py:641
  72.3 0.0 copy-done.1
  72.3 0.0 copy-done.3
  72.3 0.0 copy-done.4
  72.3 0.0 copy-done.6
  72.3 0.0 copy-done.7
  72.3 0.0 copy-start.2
  72.3 0.0 copy-start.5
  72.3 7.2 %pixels.1 = f32[8,16,3,8,128]{4,3,2,1,0:T(8,128)S(1)} custom-call(f32[8,16,3,8,128]{4,3,2,1,0:T(8,128)S(1)} %bitcast.26, bf16[768,256]{1,0:T(8,128)(2,1)S(1)} %copy-done.4, f32[2,8,128]{2,1,0:T(8,128)S(1)} %copy-done.7, f32[2,24,8,1024]{3,2,1,0:T(8,128)S(1)} %copy-done.1, f32[8,8,128]{2,1,0:T(8,128)S(1)} %copy-done.6, bf16[768,256]{1,0:T(8,128)(2,1)S(1)} %copy-done.3), custom_call_target="tpu_custom_call" | custom-call | flops 1207959552 | bytes 6291456 | tf_op jit(solution)/shard_map/pixels/pallas_call | solution.py:530
  79.6 0.0 copy-start
  79.6 28.6 %all_to_all.26 = f32[128,3,8,128]{3,2,1,0:T(8,128)S(1)} all-to-all(f32[128,3,8,128]{3,2,1,0:T(8,128)S(1)} %bitcast.27), channel_id=1, replica_groups=mesh['harm'=8,'rows'=16] {'harm','rows'}, dimensions={0} | all-to-all | bytes 3145728 | tf_op jit(solution)/shard_map/all_to_all | solution.py:645
  108.2 0.0 copy-done.2
  108.2 0.0 copy-done.5
  108.2 0.0 copy-done
  108.2 5.1 %march.3 = f32[8,16,3,8,128]{4,3,2,1,0:T(8,128)S(1)} custom-call(f32[8,16,3,8,128]{4,3,2,1,0:T(8,128)S(1)} %bitcast.21, f32[2,3,8,128,128]{4,3,2,1,0:T(8,128)S(1)} %copy-done, bf16[256,384]{1,0:T(8,128)(2,1)S(1)} %copy-done.5, f32[2,8,128,128]{3,2,1,0:T(8,128)S(1)} %copy-done.2), custom_call_target="tpu_custom_call" | custom-call | flops 1610612736 | bytes 6291456 | tf_op jit(solution)/shard_map/march/pallas_call | solution.py:376
  113.3 28.6 %all_to_all.27 = f32[128,3,8,128]{3,2,1,0:T(8,128)S(1)} all-to-all(f32[128,3,8,128]{3,2,1,0:T(8,128)S(1)} %bitcast.22), channel_id=1, replica_groups=mesh['harm'=8,'rows'=16] {'harm','rows'}, dimensions={0} | all-to-all | bytes 3145728 | tf_op jit(solution)/shard_map/all_to_all | solution.py:641
  141.8 4.9 %pixels_last.1 = f32[3072,128]{1,0:T(8,128)S(1)} custom-call(f32[8,16,3,8,128]{4,3,2,1,0:T(8,128)S(1)} %bitcast.24, bf16[768,256]{1,0:T(8,128)(2,1)S(1)} %copy-done.4, f32[2,8,128]{2,1,0:T(8,128)S(1)} %copy-done.7, f32[2,24,8,1024]{3,2,1,0:T(8,128)S(1)} %copy-done.1, f32[8,8,128]{2,1,0:T(8,128)S(1)} %copy-done.6, bf16[768,256]{1,0:T(8,128)(2,1)S(1)} %copy-done.3), custom_call_target="tpu_custom_call" | custom-call | flops 1207959552 | bytes 6291456 | tf_op jit(solution)/shard_map/pixels_last/pallas_call | solution.py:530
  146.8 25.4 %all_to_all.28.in_ref = f32[8,3,128,128]{3,2,1,0:T(8,128)S(1)} all-to-all(f32[8,3,128,128]{3,2,1,0:T(8,128)S(1)} %bitcast.25), channel_id=1, replica_groups=mesh['harm'=8,'rows'=16] {'harm'}, dimensions={0} | all-to-all | bytes 3145728 | tf_op jit(solution)/shard_map/all_to_all | solution.py:648
  172.2 1.3 order_rows.1
  (5 shorter events, 0.0 us)
Async XLA Ops:
  4.1 28.1 %all-to-all-start = ((f32[16,3,64,128]{3,2,1,0:T(8,128)}), f32[16,3,64,128]{3,2,1,0:T(8,128)S(1)}, u32[]{:S(2)}, u32[]{:S(2)}) async-start(f32[16,3,64,128]{3,2,1,0:T(8,128)} %first_transform.1), calls=%async_computation | async-start | bytes 3145728 | tf_op jit(solution)/shard_map/all_to_all | solution.py:637
  38.9 33.3 %copy-start.1 = (f32[2,24,8,1024]{3,2,1,0:T(8,128)S(1)}, f32[2,24,8,1024]{3,2,1,0:T(8,128)}, u32[]{:S(2)}) copy-start(f32[2,24,8,1024]{3,2,1,0:T(8,128)} %pad_maximum_fusion.1.screen_ref) | copy-start | bytes 4718596
  39.0 33.3 %copy-start.3 = (bf16[768,256]{1,0:T(8,128)(2,1)S(1)}, bf16[768,256]{1,0:T(8,128)(2,1)}, u32[]{:S(2)}) copy-start(bf16[768,256]{1,0:T(8,128)(2,1)} %constant.81.clone.g_hbm.forward_ref) | copy-start | bytes 1179652
  39.0 33.3 %copy-start.4 = (bf16[768,256]{1,0:T(8,128)(2,1)S(1)}, bf16[768,256]{1,0:T(8,128)(2,1)}, u32[]{:S(2)}) copy-start(bf16[768,256]{1,0:T(8,128)(2,1)} %constant.82.clone.inverse_ref) | copy-start | bytes 1179652
  39.0 33.3 %copy-start.6 = (f32[8,8,128]{2,1,0:T(8,128)S(1)}, f32[8,8,128]{2,1,0:T(8,128)}, u32[]{:S(2)}) copy-start(f32[8,8,128]{2,1,0:T(8,128)} %multiply_bitcast_fusion.gain_ref) | copy-start | bytes 98308
  39.0 33.3 %copy-start.7 = (f32[2,8,128]{2,1,0:T(8,128)S(1)}, f32[2,8,128]{2,1,0:T(8,128)}, u32[]{:S(2)}) copy-start(f32[2,8,128]{2,1,0:T(8,128)} %constant.83.clone.twiddle_hbm.twiddle_ref) | copy-start | bytes 24580
  72.3 35.9 %copy-start.2 = (f32[2,8,128,128]{3,2,1,0:T(8,128)S(1)}, f32[2,8,128,128]{3,2,1,0:T(8,128)}, u32[]{:S(2)}) copy-start(f32[2,8,128,128]{3,2,1,0:T(8,128)} %constant.85.clone.twiddle_hbm.twiddle_ref) | copy-start | bytes 3145732
  72.3 35.8 %copy-start.5 = (bf16[256,384]{1,0:T(8,128)(2,1)S(1)}, bf16[256,384]{1,0:T(8,128)(2,1)}, u32[]{:S(2)}) copy-start(bf16[256,384]{1,0:T(8,128)(2,1)} %constant.84.clone.m_hbm.m_ref) | copy-start | bytes 589828
  79.6 28.6 %copy-start = (f32[2,3,8,128,128]{4,3,2,1,0:T(8,128)S(1)}, f32[2,3,8,128,128]{4,3,2,1,0:T(8,128)}, u32[]{:S(2)}) copy-start(f32[2,3,8,128,128]{4,3,2,1,0:T(8,128)} %pad_maximum_fusion.prop_hbm.prop_ref) | copy-start | bytes 9437188

commit v3 on v2

--- a/solution.py
+++ b/solution.py
@@ -39,49 +39,16 @@
 
 def lane_matrices():
     cosine, sine = np.cos(sub_angles()), np.sin(sub_angles())
-    forward_real = np.concatenate([cosine, sine], 0)
-    forward_imag = np.concatenate([-sine, cosine], 0)
-    inverse_real = np.concatenate([cosine, -sine], 0)
-    inverse_imag = np.concatenate([sine, cosine], 0)
-    forward = np.concatenate(
-        [
-            forward_real[:, :HALF],
-            forward_imag[:, :HALF],
-            forward_real[:, HALF:],
-            forward_imag[:, HALF:],
-        ],
-        1,
-    )
-    inverse = np.concatenate([inverse_real, inverse_imag], 1)
-    inverse = np.concatenate(
-        [
-            inverse[:HALF],
-            inverse[SUB : SUB + HALF],
-            inverse[HALF:SUB],
-            inverse[SUB + HALF :],
-        ],
-        0,
-    )
-    return stack_constant(forward), stack_constant(inverse)
+    forward = np.block([[cosine, -sine], [sine, cosine]])
+    inverse = np.block([[cosine, sine], [-sine, cosine]])
+    order = np.arange(2 * SUB).reshape(2, 2, HALF).transpose(1, 0, 2).reshape(-1)
+    tables = (forward, inverse, forward[:, order], inverse[order])
+    return tuple(stack_constant(table) for table in tables)
 
 
 def lane_twiddles():
     angle = 2.0 * np.pi / N * (np.arange(RADIX)[:, None] * np.arange(SUB)[None, :])
     return np.stack([np.cos(angle), np.sin(angle)]).astype(np.float32)
-
-
-def row_matrices():
-    both = np.concatenate([np.cos(sub_angles()), np.sin(sub_angles())], 0)
-    high, low = split_constant(both)
-    return np.concatenate([high, high, low], 1)
-
-
-def row_twiddles():
-    angle = 2.0 * np.pi / N * (np.arange(RADIX)[:, None] * np.arange(SUB)[None, :])
-    sign = np.where(np.arange(SUB) < HALF, 1.0, -1.0)
-    cosine = np.broadcast_to(np.cos(angle)[:, :, None], (RADIX, SUB, SUB))
-    sine = np.sin(angle)[:, :, None] * sign[None, None, :]
-    return np.stack([cosine, sine]).astype(np.float32)
 
 
 def split_value(value):
@@ -177,9 +144,7 @@
     copies[local_harm].wait()
     for n in range(local_harm):
         copies[n].wait()
-
-        def one_tile(t, carry, n=n):
-            start = pl.multiple_of(t * 16, 16)
+        for start in range(0, rows, 16):
             points = [
                 tuple(
                     line_ref[n, pl.ds(start * 16 + 2 * k + c, 16, stride=16), :]
@@ -189,13 +154,10 @@
             ]
 
             def store(m, value):
-                first = (m * local_harm + n) * rows
-                store_parts(part_ref, pl.ds(pl.multiple_of(first + start, 16), 16), value)
+                first = (m * local_harm + n) * rows + start
+                store_parts(part_ref, slice(first, first + 16), value)
 
             forward_lanes(points, store, twiddle_ref)
-            return carry
-
-        lax.fori_loop(0, rows // 16, one_tile, 0)
     copies[local_harm + 1].wait()
     result = product(part_ref[...], g_ref[...])
     for m in range(RADIX):
@@ -221,7 +183,7 @@
     local_harm, rows = pressure.shape[0], pressure.shape[1]
     lines = pressure.reshape(local_harm, rows, 2, RADIX, SUB).transpose(0, 1, 3, 2, 4)
     lines = lines.reshape(local_harm * rows * 16, SUB)
-    forward, _, twiddles = constants["lane"]
+    _, _, forward, _, twiddles = constants
     return pl.pallas_call(
         first_kernel,
         in_specs=[IN_HBM] * 3,
@@ -244,144 +206,113 @@
     )(*in_hbm(lines, forward, twiddles))
 
 
-def march_fetching(
-    in_ref,
-    prop_hbm,
-    m_hbm,
-    twiddle_hbm,
-    screen_ref,
-    gain_ref,
-    out_ref,
-    part_ref,
-    spec_ref,
-    prop_ref,
-    m_ref,
-    twiddle_ref,
-    sems,
-):
+def march_kernel(by_rows, in_ref, twiddle_ref, forward_ref, inverse_ref, prop_ref, *refs):
+    out_ref, line_ref, part_ref, spec_ref = refs[-4:]
     local_harm = out_ref.shape[2]
-    copies = fetch(
-        [twiddle_hbm, m_hbm] + [prop_hbm.at[:, n] for n in range(local_harm)],
-        [twiddle_ref, m_ref] + [prop_ref.at[:, n] for n in range(local_harm)],
-        sems,
-    )
-    copies[0].wait()
-    copies[1].wait()
-
-    def wait(n):
-        pltpu.make_async_copy(prop_hbm.at[:, n], prop_ref.at[:, n], sems.at[2 + n]).wait()
-
-    march_kernel(
-        True, wait, in_ref, prop_ref, m_ref, twiddle_ref, out_ref, part_ref, spec_ref
-    )
-
-
-def march_kernel(
-    by_rows, wait, in_ref, prop_ref, m_ref, twiddle_ref, out_ref, part_ref, spec_ref
-):
-    local_harm = out_ref.shape[2]
-    lane = lax.broadcasted_iota(jnp.int32, (8, SUB), 1)
-    sign = jnp.where(lane < HALF, 1.0, -1.0).astype(jnp.float32)
-
-    def swap(value):
-        return pltpu.roll(value, HALF, 1)
-
-    def turn_forward(value):
-        return (sign * swap(value[0]),)
-
-    def turn_inverse(value):
-        return (-sign * swap(value[0]),)
-
-    def load(n, block, tile):
+
+    def load(n, block):
         if by_rows:
-            return in_ref[block, n, 8 * tile : 8 * tile + 8, :]
-        return in_ref[tile, block, n]
-
-    def store(pair, m, value):
-        lanes = slice(SUB * m, SUB * m + SUB)
-        high, low = split_value(value)
-        for part, data in enumerate((high, low, high)):
-            first = SUB * part + 16 * pair
-            part_ref[first : first + 16, lanes] = data
-
-    def one_harmonic(n, carry):
-        for pair in range(SUB // 16):
-            outs = []
-            for tile in (2 * pair, 2 * pair + 1):
-                points = [(load(n, 2 * k + tile // 8, tile % 8),) for k in range(RADIX)]
-                values = butterflies(points, turn_forward)
-                rows = slice(8 * tile, 8 * tile + 8)
-                outs.append(
-                    [
-                        value[0]
-                        if m == 0
-                        else value[0] * twiddle_ref[0, m, rows]
-                        + swap(value[0]) * twiddle_ref[1, m, rows]
-                        for m, value in enumerate(values)
-                    ]
+            return [in_ref[block, n]]
+        return [in_ref[tile, block, n] for tile in range(8)]
+
+    def first_row(m, n):
+        return (m * local_harm + n) * HALF
+
+    for n in range(local_harm):
+        for k in range(RADIX):
+            columns = jnp.concatenate(load(n, 2 * k) + load(n, 2 * k + 1), 0)
+            line_ref[n, k] = columns.T
+    for n in range(local_harm):
+        for start in range(0, HALF, 16):
+            points = [
+                tuple(
+                    line_ref[n, k, HALF * c + start : HALF * c + start + 16] for c in range(2)
                 )
-            for m in range(RADIX):
-                store(pair, m, jnp.concatenate([outs[0][m], outs[1][m]], 0))
-        spec_ref[...] = product(m_ref[...], part_ref[...])
-        wait(n)
-        for m in range(RADIX):
-            lanes = slice(SUB * m, SUB * m + SUB)
-            for pair in range(SUB // 16):
-                outs = []
-                for tile in (2 * pair, 2 * pair + 1):
-                    rows = slice(8 * tile, 8 * tile + 8)
-                    value = spec_ref[rows, lanes] + sign * swap(
-                        spec_ref[SUB + 8 * tile : SUB + 8 * tile + 8, lanes]
-                    )
-                    outs.append(value * prop_ref[0, n, m, rows] + swap(value) * prop_ref[1, n, m, rows])
-                store(pair, m, jnp.concatenate(outs, 0))
-        spec_ref[...] = product(m_ref[...], part_ref[...])
-        for tile in range(SUB // 8):
-            rows = slice(8 * tile, 8 * tile + 8)
+                for k in range(RADIX)
+            ]
+
+            def store(m, value):
+                first = first_row(m, n) + start
+                store_parts(part_ref, slice(first, first + 16), value)
+
+            forward_lanes(points, store, twiddle_ref)
+    spec_ref[...] = product(part_ref[...], forward_ref[...])
+    for m in range(RADIX):
+        for n in range(local_harm):
+            for start in range(0, HALF, 16):
+                rows = slice(first_row(m, n) + start, first_row(m, n) + start + 16)
+                tile = slice(start, start + 16)
+                real, imag = spec_ref[rows, :SUB], spec_ref[rows, SUB:]
+                prop_real, prop_imag = prop_ref[0, n, m, tile], prop_ref[1, n, m, tile]
+                value = (
+                    real * prop_real - imag * prop_imag,
+                    real * prop_imag + imag * prop_real,
+                )
+                store_parts(part_ref, rows, jnp.concatenate(value, 1))
+    spec_ref[...] = product(part_ref[...], inverse_ref[...])
+    for n in range(local_harm):
+        for start in range(0, HALF, 8):
             points = []
             for m in range(RADIX):
-                lanes = slice(SUB * m, SUB * m + SUB)
-                value = spec_ref[rows, lanes] - sign * swap(
-                    spec_ref[SUB + 8 * tile : SUB + 8 * tile + 8, lanes]
-                )
+                rows = slice(first_row(m, n) + start, first_row(m, n) + start + 8)
+                value = (spec_ref[rows, :SUB], spec_ref[rows, SUB:])
                 if m > 0:
-                    value = (
-                        value * twiddle_ref[0, m, rows] - swap(value) * twiddle_ref[1, m, rows]
+                    value = twiddle_pair(
+                        value, twiddle_ref[0, m : m + 1], twiddle_ref[1, m : m + 1], 1
                     )
-                points.append((value,))
-            for k, value in enumerate(butterflies(points, turn_inverse)):
-                out_ref[tile % 8, 2 * k + tile // 8, n] = value[0]
-        return carry
-
-    lax.fori_loop(0, local_harm, one_harmonic, 0)
+                points.append(value)
+            for k, value in enumerate(butterflies(points, turn_pair(1))):
+                for c in range(2):
+                    line_ref[n, k, HALF * c + start : HALF * c + start + 8] = value[c]
+        for k in range(RADIX):
+            columns = line_ref[n, k].T
+            for tile in range(16):
+                out_ref[tile % 8, 2 * k + tile // 8, n] = columns[8 * tile : 8 * tile + 8]
+
+
+def bring_kernel(*refs):
+    count = (len(refs) - 2) // 2
+    for copy in fetch(refs[:count], refs[count + 1 : -1], refs[-1]):
+        copy.wait()
+
+
+def bring(arrays, after):
+    operands = in_hbm(*arrays) + [after]
+    return pl.pallas_call(
+        bring_kernel,
+        in_specs=[IN_HBM] * len(arrays) + [pl.BlockSpec(memory_space=pl.ANY)],
+        out_specs=[IN_VMEM] * len(arrays),
+        out_shape=[pltpu.VMEM(array.shape, array.dtype) for array in arrays],
+        scratch_shapes=[pltpu.SemaphoreType.DMA((len(arrays),))],
+        name="bring",
+    )(*operands)
 
 
 def march(wavefield, prop, after, constants, by_rows):
     local_harm = wavefield.shape[1 if by_rows else 2]
-    tables = [prop, constants["row_matrices"], constants["row_twiddles"]]
+    forward, inverse, _, _, twiddles = constants
+    tables = [twiddles, forward, inverse]
+    if by_rows:
+        tables = bring(tables, prop)
+    operands = in_vmem(wavefield, *tables, prop)
+    in_specs = [IN_VMEM] * len(operands)
+    if by_rows:
+        operands += in_hbm(*after)
+        in_specs += [IN_HBM] * len(after)
     scratch = [
-        pltpu.VMEM((3 * SUB, N), jnp.bfloat16),
-        pltpu.VMEM((2 * SUB, N), jnp.float32),
+        pltpu.VMEM((local_harm, RADIX, SUB, SUB), jnp.float32),
+        pltpu.VMEM((RADIX * local_harm * HALF, 768), jnp.bfloat16),
+        pltpu.VMEM((RADIX * local_harm * HALF, 2 * SUB), jnp.float32),
     ]
-    if by_rows:
-        kernel = march_fetching
-        operands = in_vmem(wavefield) + in_hbm(*tables, *after)
-        in_specs = [IN_VMEM] + [IN_HBM] * (len(operands) - 1)
-        scratch += [pltpu.VMEM(table.shape, table.dtype) for table in tables]
-        scratch.append(pltpu.SemaphoreType.DMA((2 + local_harm,)))
-    else:
-        kernel = functools.partial(march_kernel, False, lambda n: None)
-        operands = in_vmem(wavefield, *tables)
-        in_specs = [IN_VMEM] * len(operands)
     return pl.pallas_call(
-        kernel,
+        functools.partial(march_kernel, by_rows),
         in_specs=in_specs,
         out_specs=IN_VMEM,
         out_shape=pltpu.VMEM((8, 16, local_harm, 8, SUB), jnp.float32),
         scratch_shapes=scratch,
         compiler_params=pltpu.CompilerParams(vmem_limit_bytes=VMEM_LIMIT),
         cost_estimate=pl.CostEstimate(
-            flops=2 * 2 * 2 * local_harm * 256 * 256 * N,
+            flops=2 * 2 * local_harm * 512 * 768 * 256,
             bytes_accessed=4 * wavefield.size * 4,
             transcendentals=0,
         ),
@@ -389,44 +320,175 @@
     )(*operands)
 
 
-def pair_order():
-    block = 4
-    order = []
-    for low in range(0, H, block):
-        for high in range(low, H, block):
-            order += [
-                (m, l)
-                for m in range(high + 1, high + block + 1)
-                for l in range(low + 1, low + block + 1)
-                if m > l
-            ]
-    return order
+class Network:
+    def __init__(self, inputs):
+        self.inputs = inputs
+        self.terms = [()] * inputs
+        self.known = {}
+
+    def node(self, terms):
+        if terms not in self.known:
+            self.known[terms] = len(self.terms)
+            self.terms.append(terms)
+        return self.known[terms]
+
+    def negate(self, x):
+        return None if x is None else (-x[0], x[1])
+
+    def scale(self, factor, x):
+        if x is None:
+            return None
+        sign = x[0] if factor > 0 else -x[0]
+        return (sign, self.node(((abs(factor), x[1]),)))
+
+    def add(self, x, y):
+        if x is None or y is None:
+            return y if x is None else x
+        if x[1] > y[1]:
+            x, y = y, x
+        return (x[0], self.node(((1.0, x[1]), (float(x[0] * y[0]), y[1]))))
+
+    def subtract(self, x, y):
+        return self.add(x, self.negate(y))
+
+    def rotate(self, turns, z):
+        cosine, sine = math.cos(2.0 * math.pi * turns), math.sin(2.0 * math.pi * turns)
+        real, imag = z
+        if turns == 0.0:
+            return z
+        if turns == 0.25:
+            return (self.negate(imag), real)
+        if turns == 0.125:
+            return (
+                self.scale(cosine, self.subtract(real, imag)),
+                self.scale(cosine, self.add(imag, real)),
+            )
+        return (
+            self.subtract(self.scale(cosine, real), self.scale(sine, imag)),
+            self.add(self.scale(cosine, imag), self.scale(sine, real)),
+        )
+
+    def five_points(self, x):
+        def both(operation, a, b):
+            return (operation(a[0], b[0]), operation(a[1], b[1]))
+
+        def times(factor, a):
+            return (self.scale(factor, a[0]), self.scale(factor, a[1]))
+
+        def turned(a):
+            return (self.negate(a[1]), a[0])
+
+        plus, minus = self.add, self.subtract
+        sum_1, sum_2 = both(plus, x[1], x[4]), both(plus, x[2], x[3])
+        diff_1, diff_2 = both(minus, x[1], x[4]), both(minus, x[2], x[3])
+        total, gap = both(plus, sum_1, sum_2), both(minus, sum_1, sum_2)
+        base, step = both(plus, x[0], times(-0.25, total)), times(math.sqrt(5.0) / 4.0, gap)
+        even_1, even_2 = both(plus, base, step), both(minus, base, step)
+        sine_1, sine_2 = math.sin(0.4 * math.pi), math.sin(0.8 * math.pi)
+        odd_1 = turned(both(plus, times(sine_1, diff_1), times(sine_2, diff_2)))
+        odd_2 = turned(both(minus, times(sine_2, diff_1), times(sine_1, diff_2)))
+        return [
+            both(plus, x[0], total),
+            both(plus, even_1, odd_1),
+            both(plus, even_2, odd_2),
+            both(minus, even_2, odd_2),
+            both(minus, even_1, odd_1),
+        ]
+
+    def real_points(self, u, length):
+        if length == 1:
+            return [u[0][0]]
+        half = length // 2
+        out = [None] * length
+        for odd in range(2):
+            folded = {}
+            for k, z in u.items():
+                z = self.rotate(k * odd / length, z)
+                k %= half
+                if 2 * k > half:
+                    k, z = half - k, (z[0], self.negate(z[1]))
+                old = folded.get(k, (None, None))
+                folded[k] = (self.add(old[0], z[0]), self.add(old[1], z[1]))
+            for k in folded:
+                if k == 0 or 2 * k == half:
+                    folded[k] = (folded[k][0], None)
+            out[odd::2] = self.real_points(folded, half)
+        return out
+
+
+def sample_network():
+    assert 3 * H < 80
+    network = Network(2 * H)
+    grid = [[(None, None)] * 5 for _ in range(9)]
+    for n in range(1, H + 1):
+        real, imag = (1, 2 * n - 2), (1, 2 * n - 1)
+        k, place = n % 16, n % 5
+        if k > 8:
+            k, place, imag = 16 - k, -n % 5, network.negate(imag)
+        grid[k][place] = (real, imag)
+    columns = [network.five_points(row) for row in grid]
+    groups = []
+    for instant in range(5):
+        start = len(network.terms)
+        u = {k: columns[k][instant] for k in range(9)}
+        u[0], u[8] = (u[0][0], None), (u[8][0], None)
+        groups.append((start, network.real_points(u, 16)))
+    return network, groups
+
+
+def signed_sum(old, sign, value):
+    if old is None:
+        return (sign, value)
+    if old[0] == sign:
+        return (sign, old[1] + value)
+    return (1, old[1] - value) if old[0] > 0 else (1, value - old[1])
 
 
 def couple_pixels(load, gain, store):
-    total_real = [None] * (H + 1)
-    total_imag = [None] * (H + 1)
-
-    def accumulate(n, real, imag):
-        total_real[n] = real if total_real[n] is None else total_real[n] + real
-        total_imag[n] = imag if total_imag[n] is None else total_imag[n] + imag
-
-    for m, l in pair_order():
-        (a, b), (c, d) = load(m), load(l)
-        ac, bd, ad, bc = a * c, b * d, a * d, b * c
-        accumulate(m - l, ac + bd, bc - ad)
-        if m + l <= H:
-            accumulate(m + l, ac - bd, ad + bc)
-    for m in range(1, H // 2 + 1):
-        a, b = load(m)
-        accumulate(2 * m, 0.5 * (a * a - b * b), a * b)
+    network, groups = sample_network()
+    values = {}
+
+    def value(node):
+        if node not in values:
+            if node < network.inputs:
+                values[node] = load(node)
+            else:
+                terms = network.terms[node]
+                first = value(terms[0][1])
+                if len(terms) == 1:
+                    values[node] = terms[0][0] * first
+                else:
+                    second = value(terms[1][1])
+                    values[node] = first + second if terms[1][0] > 0 else first - second
+        return values[node]
+
+    sums = [None] * len(network.terms)
+    end = len(network.terms)
+    for start, outputs in reversed([(network.inputs, [])] + groups):
+        for sign, node in outputs:
+            sample = value(node)
+            sums[node] = signed_sum(sums[node], sign, sample * sample)
+        for node in range(end - 1, start - 1, -1):
+            if sums[node] is None:
+                continue
+            sign, total = sums[node]
+            for factor, source in network.terms[node]:
+                if abs(factor) == 1.0:
+                    part = (sign if factor > 0 else -sign, total)
+                else:
+                    part = (sign, factor * total)
+                sums[source] = signed_sum(sums[source], *part)
+        end = start
     for n in range(1, H + 1):
-        a, b = load(n)
-        weight = (2.0 * n) * gain
-        if total_real[n] is None:
-            store(n, a, b)
-        else:
-            store(n, a - weight * total_imag[n], b + weight * total_real[n])
+        weight = (n * 4.0 / 80.0) * gain
+        (sign_real, real), (sign_imag, imag) = sums[2 * n - 2], sums[2 * n - 1]
+        old_real, old_imag = load(2 * n - 2), load(2 * n - 1)
+        turn_real, turn_imag = weight * imag, weight * real
+        store(
+            n,
+            old_real - turn_real if sign_imag > 0 else old_real + turn_real,
+            old_imag + turn_imag if sign_real > 0 else old_imag - turn_imag,
+        )
 
 
 def pixel_kernel(
@@ -461,10 +523,10 @@
             store_parts(part_ref, slice(first, first + 16), value)
     line_ref[...] = product(part_ref[...], inverse_ref[...])
 
-    def one_order(n, carry):
+    for n in range(H):
         points = []
         for m in range(RADIX):
-            rows = pl.ds(pl.multiple_of(height * m + 8 * n, 8), 8)
+            rows = slice(height * m + 8 * n, height * m + 8 * n + 8)
             value = (line_ref[rows, :SUB], line_ref[rows, SUB:])
             if m > 0:
                 value = twiddle_pair(value, twiddle_ref[0, m : m + 1], twiddle_ref[1, m : m + 1], 1)
@@ -474,13 +536,10 @@
             factor_real, factor_imag = screen_ref[0, n, :, lanes], screen_ref[1, n, :, lanes]
             field_ref[k, 2 * n] = real * factor_real - imag * factor_imag
             field_ref[k, 2 * n + 1] = real * factor_imag + imag * factor_real
-        return carry
-
-    lax.fori_loop(0, H, one_order, 0, unroll=2)
 
     def one_block(k, carry):
-        def load(n):
-            return field_ref[k, 2 * n - 2], field_ref[k, 2 * n - 1]
+        def load(index):
+            return field_ref[k, index]
 
         def store(n, real, imag):
             if last:
@@ -499,19 +558,15 @@
     if last:
         return
 
-    def one_pair(pair, carry):
-        def rows(block):
-            return pl.ds(pl.multiple_of(height * block + 16 * pair, 16), 16)
+    for n in range(0, H, 2):
+
+        def rows(block, n=n):
+            return slice(height * block + 8 * n, height * block + 8 * n + 16)
 
         points = [(line_ref[rows(k), :SUB], line_ref[rows(k), SUB:]) for k in range(RADIX)]
         forward_lanes(
-            points,
-            lambda m, value: store_parts(part_ref, rows(m), value),
-            twiddle_ref,
+            points, lambda m, value: store_parts(part_ref, rows(m), value), twiddle_ref
         )
-        return carry
-
-    lax.fori_loop(0, H // 2, one_pair, 0)
     result = product(part_ref[...], forward_ref[...])
     for m in range(RADIX):
         for n in range(H):
@@ -523,7 +578,7 @@
 
 
 def pixels(wavefield, screen, gain, constants, last):
-    forward, inverse, twiddles = constants["lane"]
+    _, _, forward, inverse, twiddles = constants
     tables = [inverse, twiddles, screen, gain, forward]
     operands = in_vmem(wavefield, *tables)
     out_shape = (H * 8 * 16, SUB) if last else wavefield.shape
@@ -593,17 +648,16 @@
     down = RADIX * jnp.arange(SUB, dtype=jnp.int32)[None, :] + jnp.arange(
         RADIX, dtype=jnp.int32
     )[:, None]
-    lane = jnp.arange(SUB, dtype=jnp.int32)
-    across = RADIX * (lax.rem(place, 2) * HALF + lax.rem(lane, HALF)) + place // 2
+    across = (
+        RADIX * (lax.rem(place, 2) * HALF + jnp.arange(HALF, dtype=jnp.int32)) + place // 2
+    )
     real, imag = propagator(
         (3.0 / H * orders)[:, None, None, None],
-        squared_freq_at(down, N)[None, :, :, None],
-        squared_freq_at(across, N)[None, None, None, :],
+        squared_freq_at(down, N)[None, :, None, :],
+        squared_freq_at(across, N)[None, None, :, None],
         float(DZ),
     )
-    factor = 1.0 / (N * N)
-    sign = jnp.where(lane < HALF, -factor, factor).astype(jnp.float32)
-    return jnp.stack([real * factor, imag * sign])
+    return jnp.stack([real, imag]) * (1.0 / (N * N))
 
 
 def screen_tables(contrast, absorption):
@@ -613,14 +667,13 @@
     return jnp.stack([damping * jnp.cos(angle), damping * jnp.sin(angle)])
 
 
+def make_constants():
+    return tuple(jnp.asarray(table) for table in lane_matrices() + (lane_twiddles(),))
+
+
 def shards(pressure, contrast, absorption, nonlinearity):
     local_harm = pressure.shape[0]
-    constants = {
-        "lane": lane_matrices() + (lane_twiddles(),),
-        "row_matrices": row_matrices(),
-        "row_twiddles": row_twiddles(),
-    }
-    constants = jax.tree.map(jnp.asarray, constants)
+    constants = make_constants()
     axes = ("harm", "rows")
     pixel_rows = 8
     row_start = lax.axis_index("harm") * pixel_rows

time: 174 us -> 166 us (0.954)
  Pallas kernels: 29.4 us -> 21.5 us
  other arithmetic: 14.7 us -> 11 us
  waiting for transfers between devices: 7.29 us -> 9.84 us
    mul x1, other arithmetic: 6.41 us -> 1.3 us  [propagator_tables(): return jnp.stack([real, imag]) * (1.0 / (N * N))]
    pallas_call x2 -> x3, Pallas kernels: 11.8 us -> 7.79 us  [the longest x2 6.63 us: march(): pl.pallas_call(functools.partial(march_kernel, by_rows), in_specs=in_spec...]
    pallas_call x2, Pallas kernels: 12.2 us -> 8.44 us  [pixels(): pl.pallas_call(functools.partial(pixel_kernel, last), in_specs=[IN_VMEM]...]
    select_n x1, other arithmetic: 0.01 us -> 3.17 us  [propagator(): jnp.where(propagating, jnp.cos(phase_turn), jnp.exp(-phase_turn))]
    all_to_all x1, waiting for transfers between devices: 7.29 us -> 9.84 us  [shards(): lines = lax.all_to_all(lines, 'rows', 0, 0, tiled=True)]
    another operation x1 -> x0, other arithmetic: 1.84 us -> none  [propagator_tables(): return jnp.stack([real * factor, imag * sign])]
  transfers between devices with their start and end apart: 1 -> 1, of which waited for: 1 -> 1; matrix products, arithmetic and copies ran while one was open for 8% -> 7% of each run, Pallas kernels for 0% -> 1%
where the time goes in v3:
time: 166 us
  blocking collectives  116 us (70%)
  Pallas kernels  21.5 us (13%)
  other arithmetic  11 us (7%)
  waiting for transfers between devices  9.84 us (6%)
  starting transfers between devices  6.02 us (4%)
    all_to_all x2, blocking collectives, shards(): lax.all_to_all(marched.reshape((128,) + shape[2:]), axes, 0, 0, tiled=True)  61.8 us
    all_to_all x1, blocking collectives, shards(): lax.all_to_all(lines.reshape((128,) + shape[2:]), axes, 0, 0, tiled=True)  28.6 us
    all_to_all x1, blocking collectives, shards(): out = lax.all_to_all(out, 'harm', 0, 0, tiled=True)  25.4 us
    all_to_all x1, waiting for transfers between devices, shards(): lines = lax.all_to_all(lines, 'rows', 0, 0, tiled=True)  9.84 us
    pallas_call x2, Pallas kernels, pixels(): pl.pallas_call(functools.partial(pixel_kernel, last), in_specs=[IN_VMEM]...  8.44 us
    pallas_call x2, Pallas kernels, march(): pl.pallas_call(functools.partial(march_kernel, by_rows), in_specs=in_spec...  6.63 us
    all_to_all x1, starting transfers between devices, shards(): lines = lax.all_to_all(lines, 'rows', 0, 0, tiled=True)  6.02 us
    pallas_call x1, Pallas kernels, first_transform(): pl.pallas_call(first_kernel, in_specs=[IN_HBM] * 3, out_specs=IN_VMEM, ou...  3.93 us
  transfers between devices with their start and end apart: 1, of which 1 were waited for; matrix products, arithmetic and copies ran while one was open for 7% of the time, Pallas kernels for 1%

profile of v3, /device:TPU:0, one launch (start us, length us, event | category | flops | bytes accessed | tf_op | source)
XLA Modules:
  0.0 165.6 jit_solution(7141569145048216749)
XLA Ops:
  0.0 3.9 %first_transform.1 = f32[16,3,64,128]{3,2,1,0:T(8,128)} custom-call(f32[3072,128]{1,0:T(8,128)} %bitcast.28, bf16[768,256]{1,0:T(8,128)(2,1)} %constant.75.clone.g_hbm.forward_ref, f32[2,8,128]{2,1,0:T(8,128)} %constant.77.clone.twiddle_hbm.refs_0_.twiddle_ref), custom_call_target="tpu_custom_call" | custom-call | flops 603979776 | bytes 3145728 | tf_op jit(solution)/shard_map/first_transform/pallas_call | solution.py:187
  3.9 6.0 %all-to-all-start = ((f32[16,3,64,128]{3,2,1,0:T(8,128)}), f32[16,3,64,128]{3,2,1,0:T(8,128)S(1)}, u32[]{:S(2)}, u32[]{:S(2)}) async-start(f32[16,3,64,128]{3,2,1,0:T(8,128)} %first_transform.1), calls=%async_computation | async-start | bytes 3145728 | tf_op jit(solution)/shard_map/all_to_all | solution.py:690
  10.1 0.1 broadcast_subtract_fusion
  10.1 3.2 %fusion.1 = (f32[1,3,8,64,128]{4,3,2,1,0:T(8,128)S(1)}, f32[1,3,8,64,128]{4,3,2,1,0:T(8,128)S(1)}) fusion(f32[64]{0:T(128)S(1)} %fusion.15, f32[3,8,128]{2,1,0:T(8,128)S(1)} %broadcast_subtract_fusion), kind=kLoop, calls=%fused_computation.7 | loop fusion | flops 1376256 | bytes 1585408 | tf_op jit(solution)/shard_map/jit(_where)/select_n | solution.py:638
  13.3 1.3 maximum_multiply_fusion.refs_3_.prop_ref
  14.6 1.2 bring.1
  15.8 0.0 copy-start.7
  15.8 1.4 multiply_bitcast_fusion.refs_1_.gain_ref
  17.2 0.8 dynamic-slice_negate_fusion
  18.0 3.0 %fusion.8 = (f32[1,24,8,1024]{3,2,1,0:T(8,128)S(1)}, f32[1,24,8,1024]{3,2,1,0:T(8,128)S(1)}) fusion(f32[8,1024]{1,0:T(8,128)S(1)} %get-tuple-element.16, f32[24]{0:T(128)S(1)} %get-tuple-element.17, f32[24]{0:T(128)S(1)} %get-tuple-element.18, f32[8,1024]{1,0:T(8,128)S(1)} %get-tuple-element.15), kind=kLoop, calls=%fused_computation.14 | loop fusion | flops 983040 | bytes 1638592 | tf_op jit(solution)/shard_map/mul | solution.py:667
  21.0 0.0 copy-done.7
  21.0 0.0 copy-start
  21.0 1.2 pad_maximum_fusion.refs_0_.screen_ref
  22.2 9.8 %all-to-all-done.in_ref = f32[16,3,64,128]{3,2,1,0:T(8,128)S(1)} async-done(((f32[16,3,64,128]{3,2,1,0:T(8,128)}), f32[16,3,64,128]{3,2,1,0:T(8,128)S(1)}, u32[]{:S(2)}, u32[]{:S(2)}) %all-to-all-start) | async-done | bytes 1572896 | tf_op jit(solution)/shard_map/all_to_all | solution.py:690
  32.1 0.0 copy-done
  32.1 0.0 copy-start.8
  32.1 1.0 copy-done.8
  33.1 3.3 %march.2 = f32[8,16,3,8,128]{4,3,2,1,0:T(8,128)S(1)} custom-call(f32[16,3,64,128]{3,2,1,0:T(8,128)S(1)} %all-to-all-done.in_ref, f32[2,8,128]{2,1,0:T(8,128)S(1)} %get-tuple-element.8.twiddle_ref, bf16[768,256]{1,0:T(8,128)(2,1)S(1)} %get-tuple-element.9.forward_ref, bf16[768,256]{1,0:T(8,128)(2,1)S(1)} %copy-done.8, f32[2,3,8,64,128]{4,3,2,1,0:T(8,128)S(1)} %copy-done, ...), custom_call_target="tpu_custom_call" | custom-call | flops 1207959552 | bytes 6291456 | tf_op jit(solution)/shard_map/march/pallas_call | solution.py:307
  36.4 0.0 copy-start.1
  36.4 0.0 copy-start.2
  36.4 0.0 copy-start.5
  36.4 0.0 copy-start.6
  36.4 0.0 copy-start.9
  36.4 33.3 %all_to_all.25 = f32[128,3,8,128]{3,2,1,0:T(8,128)S(1)} all-to-all(f32[128,3,8,128]{3,2,1,0:T(8,128)S(1)} %bitcast.23), channel_id=1, replica_groups=mesh['harm'=8,'rows'=16] {'harm','rows'}, dimensions={0} | all-to-all | bytes 3145728 | tf_op jit(solution)/shard_map/all_to_all | solution.py:694
  69.7 0.0 copy-done.1
  69.7 0.0 copy-done.2
  69.7 0.0 copy-done.5
  69.7 0.0 copy-done.6
  69.7 0.0 copy-done.9
  69.7 5.1 %pixels.1 = f32[8,16,3,8,128]{4,3,2,1,0:T(8,128)S(1)} custom-call(f32[8,16,3,8,128]{4,3,2,1,0:T(8,128)S(1)} %bitcast.26, bf16[768,256]{1,0:T(8,128)(2,1)S(1)} %copy-done.5, f32[2,8,128]{2,1,0:T(8,128)S(1)} %copy-done.9, f32[2,24,8,1024]{3,2,1,0:T(8,128)S(1)} %copy-done.1, f32[8,8,128]{2,1,0:T(8,128)S(1)} %copy-done.6, bf16[768,256]{1,0:T(8,128)(2,1)S(1)} %copy-done.2), custom_call_target="tpu_custom_call" | custom-call | flops 1207959552 | bytes 6291456 | tf_op jit(solution)/shard_map/pixels/pallas_call | solution.py:585
  74.8 0.0 copy-start.3
  74.8 0.0 copy-start.4
  74.8 28.6 %all_to_all.26 = f32[128,3,8,128]{3,2,1,0:T(8,128)S(1)} all-to-all(f32[128,3,8,128]{3,2,1,0:T(8,128)S(1)} %bitcast.27), channel_id=1, replica_groups=mesh['harm'=8,'rows'=16] {'harm','rows'}, dimensions={0} | all-to-all | bytes 3145728 | tf_op jit(solution)/shard_map/all_to_all | solution.py:698
  103.4 0.0 copy-done.3
  103.4 0.0 copy-done.4
  103.4 3.3 %march.3 = f32[8,16,3,8,128]{4,3,2,1,0:T(8,128)S(1)} custom-call(f32[8,16,3,8,128]{4,3,2,1,0:T(8,128)S(1)} %bitcast.24, f32[2,8,128]{2,1,0:T(8,128)S(1)} %copy-done.9, bf16[768,256]{1,0:T(8,128)(2,1)S(1)} %copy-done.3, bf16[768,256]{1,0:T(8,128)(2,1)S(1)} %copy-done.4, f32[2,3,8,64,128]{4,3,2,1,0:T(8,128)S(1)} %copy-done), custom_call_target="tpu_custom_call" | custom-call | flops 1207959552 | bytes 6291456 | tf_op jit(solution)/shard_map/march/pallas_call | solution.py:307
  106.7 28.6 %all_to_all.27 = f32[128,3,8,128]{3,2,1,0:T(8,128)S(1)} all-to-all(f32[128,3,8,128]{3,2,1,0:T(8,128)S(1)} %bitcast.25), channel_id=1, replica_groups=mesh['harm'=8,'rows'=16] {'harm','rows'}, dimensions={0} | all-to-all | bytes 3145728 | tf_op jit(solution)/shard_map/all_to_all | solution.py:694
  135.3 3.4 %pixels_last.1 = f32[3072,128]{1,0:T(8,128)S(1)} custom-call(f32[8,16,3,8,128]{4,3,2,1,0:T(8,128)S(1)} %bitcast.21, bf16[768,256]{1,0:T(8,128)(2,1)S(1)} %copy-done.5, f32[2,8,128]{2,1,0:T(8,128)S(1)} %copy-done.9, f32[2,24,8,1024]{3,2,1,0:T(8,128)S(1)} %copy-done.1, f32[8,8,128]{2,1,0:T(8,128)S(1)} %copy-done.6, bf16[768,256]{1,0:T(8,128)(2,1)S(1)} %copy-done.2), custom_call_target="tpu_custom_call" | custom-call | flops 1207959552 | bytes 6291456 | tf_op jit(solution)/shard_map/pixels_last/pallas_call | solution.py:585
  138.7 25.4 %all_to_all.28.in_ref = f32[8,3,128,128]{3,2,1,0:T(8,128)S(1)} all-to-all(f32[8,3,128,128]{3,2,1,0:T(8,128)S(1)} %bitcast.22), channel_id=1, replica_groups=mesh['harm'=8,'rows'=16] {'harm'}, dimensions={0} | all-to-all | bytes 3145728 | tf_op jit(solution)/shard_map/all_to_all | solution.py:701
  164.1 1.3 order_rows.1
  (5 shorter events, 0.0 us)
Async XLA Ops:
  3.9 28.1 %all-to-all-start = ((f32[16,3,64,128]{3,2,1,0:T(8,128)}), f32[16,3,64,128]{3,2,1,0:T(8,128)S(1)}, u32[]{:S(2)}, u32[]{:S(2)}) async-start(f32[16,3,64,128]{3,2,1,0:T(8,128)} %first_transform.1), calls=%async_computation | async-start | bytes 3145728 | tf_op jit(solution)/shard_map/all_to_all | solution.py:690
  15.8 5.2 %copy-start.7 = (bf16[768,256]{1,0:T(8,128)(2,1)}, bf16[768,256]{1,0:T(8,128)(2,1)S(1)}, u32[]{:S(2)}) copy-start(bf16[768,256]{1,0:T(8,128)(2,1)S(1)} %get-tuple-element.10.inverse_ref) | copy-start | bytes 1179652
  21.0 11.1 %copy-start = (f32[2,3,8,64,128]{4,3,2,1,0:T(8,128)S(1)}, f32[2,3,8,64,128]{4,3,2,1,0:T(8,128)}, u32[]{:S(2)}) copy-start(f32[2,3,8,64,128]{4,3,2,1,0:T(8,128)} %maximum_multiply_fusion.refs_3_.prop_ref) | copy-start | bytes 4718596
  32.1 1.0 copy-start.8
  36.4 33.3 %copy-start.1 = (f32[2,24,8,1024]{3,2,1,0:T(8,128)S(1)}, f32[2,24,8,1024]{3,2,1,0:T(8,128)}, u32[]{:S(2)}) copy-start(f32[2,24,8,1024]{3,2,1,0:T(8,128)} %pad_maximum_fusion.refs_0_.screen_ref) | copy-start | bytes 4718596
  36.4 33.3 %copy-start.2 = (bf16[768,256]{1,0:T(8,128)(2,1)S(1)}, bf16[768,256]{1,0:T(8,128)(2,1)}, u32[]{:S(2)}) copy-start(bf16[768,256]{1,0:T(8,128)(2,1)} %constant.75.clone.g_hbm.forward_ref) | copy-start | bytes 1179652
  36.4 33.3 %copy-start.5 = (bf16[768,256]{1,0:T(8,128)(2,1)S(1)}, bf16[768,256]{1,0:T(8,128)(2,1)}, u32[]{:S(2)}) copy-start(bf16[768,256]{1,0:T(8,128)(2,1)} %constant.76.clone.inverse_ref) | copy-start | bytes 1179652
  36.4 33.3 %copy-start.6 = (f32[8,8,128]{2,1,0:T(8,128)S(1)}, f32[8,8,128]{2,1,0:T(8,128)}, u32[]{:S(2)}) copy-start(f32[8,8,128]{2,1,0:T(8,128)} %multiply_bitcast_fusion.refs_1_.gain_ref) | copy-start | bytes 98308
  36.4 33.3 %copy-start.9 = (f32[2,8,128]{2,1,0:T(8,128)S(1)}, f32[2,8,128]{2,1,0:T(8,128)}, u32[]{:S(2)}) copy-start(f32[2,8,128]{2,1,0:T(8,128)} %constant.77.clone.twiddle_hbm.refs_0_.twiddle_ref) | copy-start | bytes 24580
  74.8 28.6 %copy-start.3 = (bf16[768,256]{1,0:T(8,128)(2,1)S(1)}, bf16[768,256]{1,0:T(8,128)(2,1)}, u32[]{:S(2)}) copy-start(bf16[768,256]{1,0:T(8,128)(2,1)} %constant.73.clone.refs_1_.forward_ref) | copy-start | bytes 1179652
  74.8 28.6 %copy-start.4 = (bf16[768,256]{1,0:T(8,128)(2,1)S(1)}, bf16[768,256]{1,0:T(8,128)(2,1)}, u32[]{:S(2)}) copy-start(bf16[768,256]{1,0:T(8,128)(2,1)} %constant.74.clone.refs_2_.inverse_ref) | copy-start | bytes 1179652

commit v4 on v3

--- a/solution.py
+++ b/solution.py
@@ -132,9 +132,19 @@
 
 
 def first_kernel(
-    in_ref, g_hbm, twiddle_hbm, out_ref, line_ref, part_ref, g_ref, twiddle_ref, sems
+    in_ref,
+    g_hbm,
+    twiddle_hbm,
+    out_hbm,
+    line_ref,
+    part_ref,
+    result_ref,
+    g_ref,
+    twiddle_ref,
+    sems,
+    out_sems,
 ):
-    local_harm, rows = out_ref.shape[1], out_ref.shape[2]
+    local_harm, rows = line_ref.shape[0], result_ref.shape[2]
     lines = rows * 2 * RADIX
     copies = fetch(
         [in_ref.at[pl.ds(n * lines, lines)] for n in range(local_harm)] + [twiddle_hbm, g_hbm],
@@ -142,6 +152,7 @@
         sems,
     )
     copies[local_harm].wait()
+    out_copies = []
     for n in range(local_harm):
         copies[n].wait()
         for start in range(0, rows, 16):
@@ -154,17 +165,23 @@
             ]
 
             def store(m, value):
-                first = (m * local_harm + n) * rows + start
-                store_parts(part_ref, slice(first, first + 16), value)
+                first = m * rows + start
+                store_parts(part_ref.at[n], slice(first, first + 16), value)
 
             forward_lanes(points, store, twiddle_ref)
-    copies[local_harm + 1].wait()
-    result = product(part_ref[...], g_ref[...])
-    for m in range(RADIX):
-        for n in range(local_harm):
-            first = (m * local_harm + n) * rows
-            out_ref[2 * m, n] = result[first : first + rows, :SUB]
-            out_ref[2 * m + 1, n] = result[first : first + rows, SUB:]
+        if n == 0:
+            copies[local_harm + 1].wait()
+        result = product(part_ref[n], g_ref[...])
+        for m in range(RADIX):
+            for half in range(2):
+                result_ref[n, 2 * m + half] = result[
+                    rows * m : rows * m + rows, SUB * half : SUB * half + SUB
+                ]
+        copy = pltpu.make_async_copy(result_ref.at[n], out_hbm.at[:, n], out_sems.at[n])
+        copy.start()
+        out_copies.append(copy)
+    for copy in out_copies:
+        copy.wait()
 
 
 IN_VMEM = pl.BlockSpec(memory_space=pltpu.VMEM)
@@ -187,14 +204,16 @@
     return pl.pallas_call(
         first_kernel,
         in_specs=[IN_HBM] * 3,
-        out_specs=IN_VMEM,
-        out_shape=pltpu.VMEM((16, local_harm, rows, SUB), jnp.float32),
+        out_specs=IN_HBM,
+        out_shape=jax.ShapeDtypeStruct((16, local_harm, rows, SUB), jnp.float32),
         scratch_shapes=[
             pltpu.VMEM((local_harm, rows * 16, SUB), jnp.float32),
-            pltpu.VMEM((RADIX * local_harm * rows, 768), jnp.bfloat16),
+            pltpu.VMEM((local_harm, RADIX * rows, 768), jnp.bfloat16),
+            pltpu.VMEM((local_harm, 16, rows, SUB), jnp.float32),
             pltpu.VMEM(forward.shape, forward.dtype),
             pltpu.VMEM(twiddles.shape, twiddles.dtype),
             pltpu.SemaphoreType.DMA((local_harm + 2,)),
+            pltpu.SemaphoreType.DMA((local_harm,)),
         ],
         compiler_params=pltpu.CompilerParams(vmem_limit_bytes=VMEM_LIMIT),
         cost_estimate=pl.CostEstimate(
@@ -207,7 +226,7 @@
 
 
 def march_kernel(by_rows, in_ref, twiddle_ref, forward_ref, inverse_ref, prop_ref, *refs):
-    out_ref, line_ref, part_ref, spec_ref = refs[-4:]
+    out_ref, line_ref, part_ref, spec_ref, back_ref = refs[-5:]
     local_harm = out_ref.shape[2]
 
     def load(n, block):
@@ -215,47 +234,54 @@
             return [in_ref[block, n]]
         return [in_ref[tile, block, n] for tile in range(8)]
 
-    def first_row(m, n):
-        return (m * local_harm + n) * HALF
-
-    for n in range(local_harm):
-        for k in range(RADIX):
-            columns = jnp.concatenate(load(n, 2 * k) + load(n, 2 * k + 1), 0)
-            line_ref[n, k] = columns.T
-    for n in range(local_harm):
-        for start in range(0, HALF, 16):
-            points = [
-                tuple(
-                    line_ref[n, k, HALF * c + start : HALF * c + start + 16] for c in range(2)
+    part = HALF // 2
+    middle = RADIX * local_harm * part
+    halves = [slice(half * middle, (half + 1) * middle) for half in range(2)]
+
+    def rows_of(m, n, start, count):
+        half, start = divmod(start, part)
+        first = half * middle + (m * local_harm + n) * part + start
+        return slice(first, first + count)
+
+    def starts(half, count):
+        return range(half * part, (half + 1) * part, count)
+
+    def spread(half):
+        for n in range(local_harm):
+            for start in starts(half, 16):
+                points = [
+                    tuple(
+                        line_ref[n, k, HALF * c + start : HALF * c + start + 16]
+                        for c in range(2)
+                    )
+                    for k in range(RADIX)
+                ]
+                forward_lanes(
+                    points,
+                    lambda m, value: store_parts(part_ref, rows_of(m, n, start, 16), value),
+                    twiddle_ref,
                 )
-                for k in range(RADIX)
-            ]
-
-            def store(m, value):
-                first = first_row(m, n) + start
-                store_parts(part_ref, slice(first, first + 16), value)
-
-            forward_lanes(points, store, twiddle_ref)
-    spec_ref[...] = product(part_ref[...], forward_ref[...])
-    for m in range(RADIX):
-        for n in range(local_harm):
-            for start in range(0, HALF, 16):
-                rows = slice(first_row(m, n) + start, first_row(m, n) + start + 16)
-                tile = slice(start, start + 16)
-                real, imag = spec_ref[rows, :SUB], spec_ref[rows, SUB:]
-                prop_real, prop_imag = prop_ref[0, n, m, tile], prop_ref[1, n, m, tile]
-                value = (
-                    real * prop_real - imag * prop_imag,
-                    real * prop_imag + imag * prop_real,
-                )
-                store_parts(part_ref, rows, jnp.concatenate(value, 1))
-    spec_ref[...] = product(part_ref[...], inverse_ref[...])
-    for n in range(local_harm):
-        for start in range(0, HALF, 8):
+
+    def propagate(half):
+        for m in range(RADIX):
+            for n in range(local_harm):
+                for start in starts(half, 16):
+                    rows = rows_of(m, n, start, 16)
+                    tile = slice(start, start + 16)
+                    real, imag = spec_ref[rows, :SUB], spec_ref[rows, SUB:]
+                    prop_real, prop_imag = prop_ref[0, n, m, tile], prop_ref[1, n, m, tile]
+                    value = (
+                        real * prop_real - imag * prop_imag,
+                        real * prop_imag + imag * prop_real,
+                    )
+                    store_parts(part_ref, rows, jnp.concatenate(value, 1))
+
+    def gather(half, n):
+        for start in starts(half, 8):
             points = []
             for m in range(RADIX):
-                rows = slice(first_row(m, n) + start, first_row(m, n) + start + 8)
-                value = (spec_ref[rows, :SUB], spec_ref[rows, SUB:])
+                rows = rows_of(m, n, start, 8)
+                value = (back_ref[rows, :SUB], back_ref[rows, SUB:])
                 if m > 0:
                     value = twiddle_pair(
                         value, twiddle_ref[0, m : m + 1], twiddle_ref[1, m : m + 1], 1
@@ -264,6 +290,24 @@
             for k, value in enumerate(butterflies(points, turn_pair(1))):
                 for c in range(2):
                     line_ref[n, k, HALF * c + start : HALF * c + start + 8] = value[c]
+
+    for n in range(local_harm):
+        for k in range(RADIX):
+            columns = jnp.concatenate(load(n, 2 * k) + load(n, 2 * k + 1), 0)
+            line_ref[n, k] = columns.T
+    first, second = halves
+    spread(0)
+    spec_ref[first] = product(part_ref[first], forward_ref[...])
+    spread(1)
+    spec_ref[second] = product(part_ref[second], forward_ref[...])
+    propagate(0)
+    back_ref[first] = product(part_ref[first], inverse_ref[...])
+    propagate(1)
+    back_ref[second] = product(part_ref[second], inverse_ref[...])
+    for n in range(local_harm):
+        gather(0, n)
+    for n in range(local_harm):
+        gather(1, n)
         for k in range(RADIX):
             columns = line_ref[n, k].T
             for tile in range(16):
@@ -271,16 +315,16 @@
 
 
 def bring_kernel(*refs):
-    count = (len(refs) - 2) // 2
-    for copy in fetch(refs[:count], refs[count + 1 : -1], refs[-1]):
+    count = 3
+    for copy in fetch(refs[:count], refs[-count - 1 : -1], refs[-1]):
         copy.wait()
 
 
 def bring(arrays, after):
-    operands = in_hbm(*arrays) + [after]
+    operands = in_hbm(*arrays) + list(after)
     return pl.pallas_call(
         bring_kernel,
-        in_specs=[IN_HBM] * len(arrays) + [pl.BlockSpec(memory_space=pl.ANY)],
+        in_specs=[IN_HBM] * len(arrays) + [pl.BlockSpec(memory_space=pl.ANY)] * len(after),
         out_specs=[IN_VMEM] * len(arrays),
         out_shape=[pltpu.VMEM(array.shape, array.dtype) for array in arrays],
         scratch_shapes=[pltpu.SemaphoreType.DMA((len(arrays),))],
@@ -293,7 +337,7 @@
     forward, inverse, _, _, twiddles = constants
     tables = [twiddles, forward, inverse]
     if by_rows:
-        tables = bring(tables, prop)
+        tables = bring(tables, after[:1])
     operands = in_vmem(wavefield, *tables, prop)
     in_specs = [IN_VMEM] * len(operands)
     if by_rows:
@@ -302,6 +346,7 @@
     scratch = [
         pltpu.VMEM((local_harm, RADIX, SUB, SUB), jnp.float32),
         pltpu.VMEM((RADIX * local_harm * HALF, 768), jnp.bfloat16),
+        pltpu.VMEM((RADIX * local_harm * HALF, 2 * SUB), jnp.float32),
         pltpu.VMEM((RADIX * local_harm * HALF, 2 * SUB), jnp.float32),
     ]
     return pl.pallas_call(
@@ -505,37 +550,58 @@
     field_ref,
 ):
     local_harm = H // 8
-    height = 8 * H
+    part = H // 2
+    height = 8 * part
+    middle = RADIX * height
+    halves = [slice(half * middle, (half + 1) * middle) for half in range(2)]
+
+    def orders(half, step):
+        return range(half * part, (half + 1) * part, step)
+
+    def rows_of(block, n, count):
+        half, n = divmod(n, part)
+        first = half * middle + height * block + 8 * n
+        return slice(first, first + count)
 
     def tile_of(n, r):
         return in_ref[n // local_harm, r, n % local_harm]
 
-    for n in range(0, H, 2):
-        for m in range(RADIX):
-            value = jnp.concatenate(
-                [
-                    jnp.concatenate([tile_of(n + i, 2 * m), tile_of(n + i, 2 * m + 1)], 1)
-                    for i in range(2)
-                ],
-                0,
-            )
-            first = height * m + 8 * n
-            store_parts(part_ref, slice(first, first + 16), value)
-    line_ref[...] = product(part_ref[...], inverse_ref[...])
-
-    for n in range(H):
-        points = []
-        for m in range(RADIX):
-            rows = slice(height * m + 8 * n, height * m + 8 * n + 8)
-            value = (line_ref[rows, :SUB], line_ref[rows, SUB:])
-            if m > 0:
-                value = twiddle_pair(value, twiddle_ref[0, m : m + 1], twiddle_ref[1, m : m + 1], 1)
-            points.append(value)
-        for k, (real, imag) in enumerate(butterflies(points, turn_pair(1))):
-            lanes = slice(SUB * k, SUB * k + SUB)
-            factor_real, factor_imag = screen_ref[0, n, :, lanes], screen_ref[1, n, :, lanes]
-            field_ref[k, 2 * n] = real * factor_real - imag * factor_imag
-            field_ref[k, 2 * n + 1] = real * factor_imag + imag * factor_real
+    def split_half(half):
+        for n in orders(half, 2):
+            for m in range(RADIX):
+                value = jnp.concatenate(
+                    [
+                        jnp.concatenate([tile_of(n + i, 2 * m), tile_of(n + i, 2 * m + 1)], 1)
+                        for i in range(2)
+                    ],
+                    0,
+                )
+                store_parts(part_ref, rows_of(m, n, 16), value)
+
+    def screen_half(half):
+        for n in orders(half, 1):
+            points = []
+            for m in range(RADIX):
+                rows = rows_of(m, n, 8)
+                value = (line_ref[rows, :SUB], line_ref[rows, SUB:])
+                if m > 0:
+                    value = twiddle_pair(
+                        value, twiddle_ref[0, m : m + 1], twiddle_ref[1, m : m + 1], 1
+                    )
+                points.append(value)
+            for k, (real, imag) in enumerate(butterflies(points, turn_pair(1))):
+                lanes = slice(SUB * k, SUB * k + SUB)
+                factor_real, factor_imag = screen_ref[0, n, :, lanes], screen_ref[1, n, :, lanes]
+                field_ref[k, 2 * n] = real * factor_real - imag * factor_imag
+                field_ref[k, 2 * n + 1] = real * factor_imag + imag * factor_real
+
+    first, second = halves
+    split_half(0)
+    line_ref[first] = product(part_ref[first], inverse_ref[...])
+    split_half(1)
+    line_ref[second] = product(part_ref[second], inverse_ref[...])
+    screen_half(0)
+    screen_half(1)
 
     def one_block(k, carry):
         def load(index):
@@ -547,9 +613,8 @@
                 out_ref[pl.ds(start, 8, stride=16), :] = real
                 out_ref[pl.ds(start + 1, 8, stride=16), :] = imag
             else:
-                rows = pl.ds(pl.multiple_of(height * k + 8 * n - 8, 8), 8)
-                line_ref[rows, :SUB] = real
-                line_ref[rows, SUB:] = imag
+                field_ref[k, 2 * n - 2] = real
+                field_ref[k, 2 * n - 1] = imag
 
         couple_pixels(load, gain_ref[k], store)
         return carry
@@ -558,23 +623,35 @@
     if last:
         return
 
-    for n in range(0, H, 2):
-
-        def rows(block, n=n):
-            return slice(height * block + 8 * n, height * block + 8 * n + 16)
-
-        points = [(line_ref[rows(k), :SUB], line_ref[rows(k), SUB:]) for k in range(RADIX)]
-        forward_lanes(
-            points, lambda m, value: store_parts(part_ref, rows(m), value), twiddle_ref
-        )
-    result = product(part_ref[...], forward_ref[...])
-    for m in range(RADIX):
-        for n in range(H):
-            first = height * m + 8 * n
-            for half in range(2):
-                out_ref[n // local_harm, 2 * m + half, n % local_harm] = result[
-                    first : first + 8, SUB * half : SUB * half + SUB
-                ]
+    def spread_half(half):
+        for n in orders(half, 2):
+            points = [
+                tuple(
+                    jnp.concatenate([field_ref[k, 2 * n + c], field_ref[k, 2 * n + 2 + c]], 0)
+                    for c in range(2)
+                )
+                for k in range(RADIX)
+            ]
+            forward_lanes(
+                points,
+                lambda m, value: store_parts(part_ref, rows_of(m, n, 16), value),
+                twiddle_ref,
+            )
+
+    def store_half(half):
+        result = product(part_ref[halves[half]], forward_ref[...])
+        for m in range(RADIX):
+            for n in orders(half, 1):
+                row = height * m + 8 * (n - half * part)
+                for side in range(2):
+                    out_ref[n // local_harm, 2 * m + side, n % local_harm] = result[
+                        row : row + 8, SUB * side : SUB * side + SUB
+                    ]
+
+    spread_half(0)
+    store_half(0)
+    spread_half(1)
+    store_half(1)
 
 
 def pixels(wavefield, screen, gain, constants, last):
@@ -603,11 +680,8 @@
 
 
 def order_kernel(in_ref, out_ref, sems):
-    groups, local_harm = in_ref.shape[:2]
-    pairs = [(h, n) for h in range(groups) for n in range(local_harm)]
-    copies = fetch(
-        [in_ref.at[h, n] for h, n in pairs], [out_ref.at[n, h] for h, n in pairs], sems
-    )
+    orders = range(in_ref.shape[1])
+    copies = fetch([in_ref.at[:, n] for n in orders], [out_ref.at[n] for n in orders], sems)
     for copy in copies:
         copy.wait()
 
@@ -619,7 +693,7 @@
         in_specs=[IN_VMEM],
         out_specs=IN_HBM,
         out_shape=jax.ShapeDtypeStruct((local_harm, groups) + blocks.shape[2:], blocks.dtype),
-        scratch_shapes=[pltpu.SemaphoreType.DMA((groups * local_harm,))],
+        scratch_shapes=[pltpu.SemaphoreType.DMA((local_harm,))],
         name="order_rows",
     )(*in_vmem(blocks))
 

time: 166 us -> 164 us (0.988)
  Pallas kernels: 21.5 us -> 19.2 us
  transfers between devices with their start and end apart: 1 -> 1, of which waited for: 1 -> 1; matrix products, arithmetic and copies ran while one was open for 7% -> 6% of each run, Pallas kernels for 1% -> 1%
where the time goes in v4:
time: 164 us; the launch traced here: 163 us
  blocking collectives  116 us (71%)
  Pallas kernels  19.2 us (12%)
  waiting for transfers between devices  11 us (7%)
  other arithmetic  9.89 us (6%)
  starting transfers between devices  6.02 us (4%)
    all_to_all x2, blocking collectives, shards(): lax.all_to_all(marched.reshape((128,) + shape[2:]), axes, 0, 0, tiled=True)  61.8 us
    all_to_all x1, blocking collectives, shards(): lax.all_to_all(lines.reshape((128,) + shape[2:]), axes, 0, 0, tiled=True)  28.6 us
    all_to_all x1, blocking collectives, shards(): out = lax.all_to_all(out, 'harm', 0, 0, tiled=True)  25.4 us
    all_to_all x1, waiting for transfers between devices, shards(): lines = lax.all_to_all(lines, 'rows', 0, 0, tiled=True)  11 us
    pallas_call x2, Pallas kernels, pixels(): pl.pallas_call(functools.partial(pixel_kernel, last), in_specs=[IN_VMEM]...  7.54 us
    all_to_all x1, starting transfers between devices, shards(): lines = lax.all_to_all(lines, 'rows', 0, 0, tiled=True)  6.02 us
    pallas_call x2, Pallas kernels, march(): pl.pallas_call(functools.partial(march_kernel, by_rows), in_specs=in_spec...  5.25 us
    pallas_call x1, Pallas kernels, first_transform(): pl.pallas_call(first_kernel, in_specs=[IN_HBM] * 3, out_specs=IN_HBM, out...  4.13 us
  transfers between devices with their start and end apart: 1, of which 1 were waited for; matrix products, arithmetic and copies ran while one was open for 6% of the time, Pallas kernels for 1%

profile of v4, /device:TPU:0, one launch (start us, length us, event | category | flops | bytes accessed | tf_op | source)
XLA Modules:
  0.0 163.3 jit_solution(15532992150344402945)
XLA Ops:
  0.0 4.1 %first_transform.1 = f32[16,3,64,128]{3,2,1,0:T(8,128)} custom-call(f32[3072,128]{1,0:T(8,128)} %bitcast.28, bf16[768,256]{1,0:T(8,128)(2,1)} %constant.75.clone.g_hbm.forward_ref, f32[2,8,128]{2,1,0:T(8,128)} %constant.77.clone.twiddle_hbm.refs_0_.twiddle_ref), custom_call_target="tpu_custom_call" | custom-call | flops 603979776 | bytes 3145728 | tf_op jit(solution)/shard_map/first_transform/pallas_call | solution.py:204
  4.1 6.0 %all-to-all-start = ((f32[16,3,64,128]{3,2,1,0:T(8,128)}), f32[16,3,64,128]{3,2,1,0:T(8,128)S(1)}, u32[]{:S(2)}, u32[]{:S(2)}) async-start(f32[16,3,64,128]{3,2,1,0:T(8,128)} %first_transform.1), calls=%async_computation | async-start | bytes 3145728 | tf_op jit(solution)/shard_map/all_to_all | solution.py:764
  10.2 0.8 dynamic-slice_negate_fusion
  11.0 3.0 %fusion.2 = (f32[1,24,8,1024]{3,2,1,0:T(8,128)S(1)}, f32[1,24,8,1024]{3,2,1,0:T(8,128)S(1)}) fusion(f32[8,1024]{1,0:T(8,128)S(1)} %get-tuple-element.16, f32[24]{0:T(128)S(1)} %get-tuple-element.17, f32[24]{0:T(128)S(1)} %get-tuple-element.18, f32[8,1024]{1,0:T(8,128)S(1)} %get-tuple-element.15), kind=kLoop, calls=%fused_computation.8 | loop fusion | flops 983040 | bytes 1638592 | tf_op jit(solution)/shard_map/mul | solution.py:741
  14.0 1.3 pad_maximum_fusion.refs_3_.refs_0_.screen_ref
  15.2 1.2 bring.1
  16.4 0.0 copy-start.6
  16.4 1.4 multiply_bitcast_fusion.refs_1_.gain_ref
  17.9 0.1 broadcast_subtract_fusion
  17.9 3.2 %fusion.1 = (f32[1,3,8,64,128]{4,3,2,1,0:T(8,128)S(1)}, f32[1,3,8,64,128]{4,3,2,1,0:T(8,128)S(1)}) fusion(f32[64]{0:T(128)S(1)} %fusion.15, f32[3,8,128]{2,1,0:T(8,128)S(1)} %broadcast_subtract_fusion), kind=kLoop, calls=%fused_computation.7 | loop fusion | flops 1376256 | bytes 1585408 | tf_op jit(solution)/shard_map/jit(_where)/select_n | solution.py:712
  21.1 0.0 copy-done.6
  21.1 0.2 maximum_multiply_fusion.prop_ref
  21.3 11.0 %all-to-all-done.in_ref = f32[16,3,64,128]{3,2,1,0:T(8,128)S(1)} async-done(((f32[16,3,64,128]{3,2,1,0:T(8,128)}), f32[16,3,64,128]{3,2,1,0:T(8,128)S(1)}, u32[]{:S(2)}, u32[]{:S(2)}) %all-to-all-start) | async-done | bytes 1572896 | tf_op jit(solution)/shard_map/all_to_all | solution.py:764
  32.3 0.0 copy-start.7
  32.3 1.0 copy-done.7
  33.3 2.6 %march.2 = f32[8,16,3,8,128]{4,3,2,1,0:T(8,128)S(1)} custom-call(f32[16,3,64,128]{3,2,1,0:T(8,128)S(1)} %all-to-all-done.in_ref, f32[2,8,128]{2,1,0:T(8,128)S(1)} %get-tuple-element.8.twiddle_ref, bf16[768,256]{1,0:T(8,128)(2,1)S(1)} %get-tuple-element.9.forward_ref, bf16[768,256]{1,0:T(8,128)(2,1)S(1)} %copy-done.7, ...), custom_call_target="tpu_custom_call" | custom-call | flops 1207959552 | bytes 6291456 | tf_op jit(solution)/shard_map/march/pallas_call | solution.py:352
  35.9 0.0 copy-start
  35.9 0.0 copy-start.1
  35.9 0.0 copy-start.4
  35.9 0.0 copy-start.5
  35.9 0.0 copy-start.8
  35.9 33.3 %all_to_all.25 = f32[128,3,8,128]{3,2,1,0:T(8,128)S(1)} all-to-all(f32[128,3,8,128]{3,2,1,0:T(8,128)S(1)} %bitcast.23), channel_id=1, replica_groups=mesh['harm'=8,'rows'=16] {'harm','rows'}, dimensions={0} | all-to-all | bytes 3145728 | tf_op jit(solution)/shard_map/all_to_all | solution.py:768
  69.2 0.0 copy-done
  69.2 0.0 copy-done.1
  69.2 0.0 copy-done.4
  69.2 0.0 copy-done.5
  69.2 0.0 copy-done.8
  69.2 4.1 %pixels.1 = f32[8,16,3,8,128]{4,3,2,1,0:T(8,128)S(1)} custom-call(f32[8,16,3,8,128]{4,3,2,1,0:T(8,128)S(1)} %bitcast.26, bf16[768,256]{1,0:T(8,128)(2,1)S(1)} %copy-done.4, f32[2,8,128]{2,1,0:T(8,128)S(1)} %copy-done.8, f32[2,24,8,1024]{3,2,1,0:T(8,128)S(1)} %copy-done, f32[8,8,128]{2,1,0:T(8,128)S(1)} %copy-done.5, bf16[768,256]{1,0:T(8,128)(2,1)S(1)} %copy-done.1), custom_call_target="tpu_custom_call" | custom-call | flops 1207959552 | bytes 6291456 | tf_op jit(solution)/shard_map/pixels/pallas_call | solution.py:662
  73.4 0.0 copy-start.2
  73.4 0.0 copy-start.3
  73.4 28.6 %all_to_all.26 = f32[128,3,8,128]{3,2,1,0:T(8,128)S(1)} all-to-all(f32[128,3,8,128]{3,2,1,0:T(8,128)S(1)} %bitcast.27), channel_id=1, replica_groups=mesh['harm'=8,'rows'=16] {'harm','rows'}, dimensions={0} | all-to-all | bytes 3145728 | tf_op jit(solution)/shard_map/all_to_all | solution.py:772
  102.0 0.0 copy-done.2
  102.0 0.0 copy-done.3
  102.0 2.6 %march.3 = f32[8,16,3,8,128]{4,3,2,1,0:T(8,128)S(1)} custom-call(f32[8,16,3,8,128]{4,3,2,1,0:T(8,128)S(1)} %bitcast.24, f32[2,8,128]{2,1,0:T(8,128)S(1)} %copy-done.8, bf16[768,256]{1,0:T(8,128)(2,1)S(1)} %copy-done.2, bf16[768,256]{1,0:T(8,128)(2,1)S(1)} %copy-done.3, f32[2,3,8,64,128]{4,3,2,1,0:T(8,128)S(1)} %maximum_multiply_fusion.prop_ref), custom_call_target="tpu_custom_call" | custom-call | flops 1207959552 | bytes 6291456 | tf_op jit(solution)/shard_map/march/pallas_call | solution.py:352
  104.6 28.6 %all_to_all.27 = f32[128,3,8,128]{3,2,1,0:T(8,128)S(1)} all-to-all(f32[128,3,8,128]{3,2,1,0:T(8,128)S(1)} %bitcast.25), channel_id=1, replica_groups=mesh['harm'=8,'rows'=16] {'harm','rows'}, dimensions={0} | all-to-all | bytes 3145728 | tf_op jit(solution)/shard_map/all_to_all | solution.py:768
  133.2 3.4 %pixels_last.1 = f32[3072,128]{1,0:T(8,128)S(1)} custom-call(f32[8,16,3,8,128]{4,3,2,1,0:T(8,128)S(1)} %bitcast.21, bf16[768,256]{1,0:T(8,128)(2,1)S(1)} %copy-done.4, f32[2,8,128]{2,1,0:T(8,128)S(1)} %copy-done.8, f32[2,24,8,1024]{3,2,1,0:T(8,128)S(1)} %copy-done, f32[8,8,128]{2,1,0:T(8,128)S(1)} %copy-done.5, bf16[768,256]{1,0:T(8,128)(2,1)S(1)} %copy-done.1), custom_call_target="tpu_custom_call" | custom-call | flops 1207959552 | bytes 6291456 | tf_op jit(solution)/shard_map/pixels_last/pallas_call | solution.py:662
  136.6 25.4 %all_to_all.28.in_ref = f32[8,3,128,128]{3,2,1,0:T(8,128)S(1)} all-to-all(f32[8,3,128,128]{3,2,1,0:T(8,128)S(1)} %bitcast.22), channel_id=1, replica_groups=mesh['harm'=8,'rows'=16] {'harm'}, dimensions={0} | all-to-all | bytes 3145728 | tf_op jit(solution)/shard_map/all_to_all | solution.py:775
  162.0 1.2 order_rows.1
  (5 shorter events, 0.0 us)
Async XLA Ops:
  4.1 28.1 %all-to-all-start = ((f32[16,3,64,128]{3,2,1,0:T(8,128)}), f32[16,3,64,128]{3,2,1,0:T(8,128)S(1)}, u32[]{:S(2)}, u32[]{:S(2)}) async-start(f32[16,3,64,128]{3,2,1,0:T(8,128)} %first_transform.1), calls=%async_computation | async-start | bytes 3145728 | tf_op jit(solution)/shard_map/all_to_all | solution.py:764
  16.4 4.7 %copy-start.6 = (bf16[768,256]{1,0:T(8,128)(2,1)}, bf16[768,256]{1,0:T(8,128)(2,1)S(1)}, u32[]{:S(2)}) copy-start(bf16[768,256]{1,0:T(8,128)(2,1)S(1)} %get-tuple-element.10.inverse_ref) | copy-start | bytes 1179652
  32.3 1.0 copy-start.7
  35.9 33.3 %copy-start = (f32[2,24,8,1024]{3,2,1,0:T(8,128)S(1)}, f32[2,24,8,1024]{3,2,1,0:T(8,128)}, u32[]{:S(2)}) copy-start(f32[2,24,8,1024]{3,2,1,0:T(8,128)} %pad_maximum_fusion.refs_3_.refs_0_.screen_ref) | copy-start | bytes 4718596
  35.9 33.3 %copy-start.1 = (bf16[768,256]{1,0:T(8,128)(2,1)S(1)}, bf16[768,256]{1,0:T(8,128)(2,1)}, u32[]{:S(2)}) copy-start(bf16[768,256]{1,0:T(8,128)(2,1)} %constant.75.clone.g_hbm.forward_ref) | copy-start | bytes 1179652
  35.9 33.3 %copy-start.4 = (bf16[768,256]{1,0:T(8,128)(2,1)S(1)}, bf16[768,256]{1,0:T(8,128)(2,1)}, u32[]{:S(2)}) copy-start(bf16[768,256]{1,0:T(8,128)(2,1)} %constant.76.clone.inverse_ref) | copy-start | bytes 1179652
  35.9 33.3 %copy-start.5 = (f32[8,8,128]{2,1,0:T(8,128)S(1)}, f32[8,8,128]{2,1,0:T(8,128)}, u32[]{:S(2)}) copy-start(f32[8,8,128]{2,1,0:T(8,128)} %multiply_bitcast_fusion.refs_1_.gain_ref) | copy-start | bytes 98308
  35.9 33.3 %copy-start.8 = (f32[2,8,128]{2,1,0:T(8,128)S(1)}, f32[2,8,128]{2,1,0:T(8,128)}, u32[]{:S(2)}) copy-start(f32[2,8,128]{2,1,0:T(8,128)} %constant.77.clone.twiddle_hbm.refs_0_.twiddle_ref) | copy-start | bytes 24580
  73.4 28.6 %copy-start.2 = (bf16[768,256]{1,0:T(8,128)(2,1)S(1)}, bf16[768,256]{1,0:T(8,128)(2,1)}, u32[]{:S(2)}) copy-start(bf16[768,256]{1,0:T(8,128)(2,1)} %constant.73.clone.refs_1_.forward_ref) | copy-start | bytes 1179652
  73.4 28.6 %copy-start.3 = (bf16[768,256]{1,0:T(8,128)(2,1)S(1)}, bf16[768,256]{1,0:T(8,128)(2,1)}, u32[]{:S(2)}) copy-start(bf16[768,256]{1,0:T(8,128)(2,1)} %constant.74.clone.refs_2_.inverse_ref) | copy-start | bytes 1179652

commit v5 on v4

--- a/solution.py
+++ b/solution.py
@@ -146,12 +146,15 @@
 ):
     local_harm, rows = line_ref.shape[0], result_ref.shape[2]
     lines = rows * 2 * RADIX
-    copies = fetch(
-        [in_ref.at[pl.ds(n * lines, lines)] for n in range(local_harm)] + [twiddle_hbm, g_hbm],
-        [line_ref.at[n] for n in range(local_harm)] + [twiddle_ref, g_ref],
+    sources = [in_ref.at[pl.ds(n * lines, lines)] for n in range(local_harm)]
+    targets = [line_ref.at[n] for n in range(local_harm)]
+    twiddle_copy, *copies = fetch(
+        [twiddle_hbm, sources[0], g_hbm] + sources[1:],
+        [twiddle_ref, targets[0], g_ref] + targets[1:],
         sems,
     )
-    copies[local_harm].wait()
+    g_copy = copies.pop(1)
+    twiddle_copy.wait()
     out_copies = []
     for n in range(local_harm):
         copies[n].wait()
@@ -170,7 +173,7 @@
 
             forward_lanes(points, store, twiddle_ref)
         if n == 0:
-            copies[local_harm + 1].wait()
+            g_copy.wait()
         result = product(part_ref[n], g_ref[...])
         for m in range(RADIX):
             for half in range(2):
@@ -225,7 +228,18 @@
     )(*in_hbm(lines, forward, twiddles))
 
 
-def march_kernel(by_rows, in_ref, twiddle_ref, forward_ref, inverse_ref, prop_ref, *refs):
+def march_fetching(in_ref, twiddle_ref, forward_ref, inverse_hbm, prop_ref, *refs):
+    inverse_ref, sem = refs[-2:]
+    copy = pltpu.make_async_copy(inverse_hbm, inverse_ref, sem)
+    copy.start()
+    march_kernel(
+        True, copy.wait, in_ref, twiddle_ref, forward_ref, inverse_ref, prop_ref, *refs[:-2]
+    )
+
+
+def march_kernel(
+    by_rows, wait, in_ref, twiddle_ref, forward_ref, inverse_ref, prop_ref, *refs
+):
     out_ref, line_ref, part_ref, spec_ref, back_ref = refs[-5:]
     local_harm = out_ref.shape[2]
 
@@ -300,6 +314,7 @@
     spec_ref[first] = product(part_ref[first], forward_ref[...])
     spread(1)
     spec_ref[second] = product(part_ref[second], forward_ref[...])
+    wait()
     propagate(0)
     back_ref[first] = product(part_ref[first], inverse_ref[...])
     propagate(1)
@@ -315,7 +330,7 @@
 
 
 def bring_kernel(*refs):
-    count = 3
+    count = 2
     for copy in fetch(refs[:count], refs[-count - 1 : -1], refs[-1]):
         copy.wait()
 
@@ -335,13 +350,15 @@
 def march(wavefield, prop, after, constants, by_rows):
     local_harm = wavefield.shape[1 if by_rows else 2]
     forward, inverse, _, _, twiddles = constants
-    tables = [twiddles, forward, inverse]
-    if by_rows:
-        tables = bring(tables, after[:1])
-    operands = in_vmem(wavefield, *tables, prop)
+    kernel = functools.partial(march_kernel, False, lambda: None)
+    operands = in_vmem(wavefield, twiddles, forward, inverse, prop)
     in_specs = [IN_VMEM] * len(operands)
     if by_rows:
+        kernel = march_fetching
+        operands[1:3] = in_vmem(*bring([twiddles, forward], after[:1]))
+        operands[3:4] = in_hbm(inverse)
         operands += in_hbm(*after)
+        in_specs[3] = IN_HBM
         in_specs += [IN_HBM] * len(after)
     scratch = [
         pltpu.VMEM((local_harm, RADIX, SUB, SUB), jnp.float32),
@@ -349,8 +366,10 @@
         pltpu.VMEM((RADIX * local_harm * HALF, 2 * SUB), jnp.float32),
         pltpu.VMEM((RADIX * local_harm * HALF, 2 * SUB), jnp.float32),
     ]
+    if by_rows:
+        scratch += [pltpu.VMEM(inverse.shape, inverse.dtype), pltpu.SemaphoreType.DMA]
     return pl.pallas_call(
-        functools.partial(march_kernel, by_rows),
+        kernel,
         in_specs=in_specs,
         out_specs=IN_VMEM,
         out_shape=pltpu.VMEM((8, 16, local_harm, 8, SUB), jnp.float32),

time: 164 us -> 163 us (level)
  no operation moved by 1% of the time
where the time goes in v5:
time: 163 us
  blocking collectives  116 us (71%)
  Pallas kernels  19.7 us (12%)
  waiting for transfers between devices  11.1 us (7%)
  other arithmetic  9.87 us (6%)
  starting transfers between devices  6.02 us (4%)
    all_to_all x2, blocking collectives, shards(): lax.all_to_all(marched.reshape((128,) + shape[2:]), axes, 0, 0, tiled=True)  61.8 us
    all_to_all x1, blocking collectives, shards(): lax.all_to_all(lines.reshape((128,) + shape[2:]), axes, 0, 0, tiled=True)  28.6 us
    all_to_all x1, blocking collectives, shards(): out = lax.all_to_all(out, 'harm', 0, 0, tiled=True)  25.4 us
    all_to_all x1, waiting for transfers between devices, shards(): lines = lax.all_to_all(lines, 'rows', 0, 0, tiled=True)  11.1 us
    pallas_call x2, Pallas kernels, pixels(): pl.pallas_call(functools.partial(pixel_kernel, last), in_specs=[IN_VMEM]...  7.53 us
    all_to_all x1, starting transfers between devices, shards(): lines = lax.all_to_all(lines, 'rows', 0, 0, tiled=True)  6.02 us
    pallas_call x2, Pallas kernels, march(): pl.pallas_call(kernel, in_specs=in_specs, out_specs=IN_VMEM, out_shape=pl...  5.99 us
    pallas_call x1, Pallas kernels, first_transform(): pl.pallas_call(first_kernel, in_specs=[IN_HBM] * 3, out_specs=IN_HBM, out...  3.95 us
  transfers between devices with their start and end apart: 1, of which 1 were waited for; matrix products, arithmetic and copies ran while one was open for 6% of the time, Pallas kernels for 1%

profile of v5, /device:TPU:0, one launch (start us, length us, event | category | flops | bytes accessed | tf_op | source)
XLA Modules:
  0.0 162.9 jit_solution(4529407217348241016)
XLA Ops:
  0.0 4.0 %first_transform.1 = f32[16,3,64,128]{3,2,1,0:T(8,128)} custom-call(f32[3072,128]{1,0:T(8,128)} %bitcast.28, bf16[768,256]{1,0:T(8,128)(2,1)} %constant.75.clone.g_hbm.forward_ref, f32[2,8,128]{2,1,0:T(8,128)} %constant.77.clone.twiddle_hbm.refs_0_.twiddle_ref), custom_call_target="tpu_custom_call" | custom-call | flops 603979776 | bytes 3145728 | tf_op jit(solution)/shard_map/first_transform/pallas_call | solution.py:207
  4.0 6.0 %all-to-all-start = ((f32[16,3,64,128]{3,2,1,0:T(8,128)}), f32[16,3,64,128]{3,2,1,0:T(8,128)S(1)}, u32[]{:S(2)}, u32[]{:S(2)}) async-start(f32[16,3,64,128]{3,2,1,0:T(8,128)} %first_transform.1), calls=%async_computation | async-start | bytes 3145728 | tf_op jit(solution)/shard_map/all_to_all | solution.py:783
  10.0 0.8 dynamic-slice_negate_fusion
  10.8 3.0 %fusion.2 = (f32[1,24,8,1024]{3,2,1,0:T(8,128)S(1)}, f32[1,24,8,1024]{3,2,1,0:T(8,128)S(1)}) fusion(f32[8,1024]{1,0:T(8,128)S(1)} %get-tuple-element.14, f32[24]{0:T(128)S(1)} %get-tuple-element.15, f32[24]{0:T(128)S(1)} %get-tuple-element.16, f32[8,1024]{1,0:T(8,128)S(1)} %get-tuple-element.13), kind=kLoop, calls=%fused_computation.8 | loop fusion | flops 983040 | bytes 1638592 | tf_op jit(solution)/shard_map/mul | solution.py:760
  13.8 1.3 pad_maximum_fusion.refs_2_.refs_0_.screen_ref
  15.0 1.0 bring.1
  16.1 1.4 multiply_bitcast_fusion.refs_1_.gain_ref
  17.5 0.1 broadcast_subtract_fusion
  17.6 3.2 %fusion.1 = (f32[1,3,8,64,128]{4,3,2,1,0:T(8,128)S(1)}, f32[1,3,8,64,128]{4,3,2,1,0:T(8,128)S(1)}) fusion(f32[64]{0:T(128)S(1)} %fusion.15, f32[3,8,128]{2,1,0:T(8,128)S(1)} %broadcast_subtract_fusion), kind=kLoop, calls=%fused_computation.7 | loop fusion | flops 1376256 | bytes 1585408 | tf_op jit(solution)/shard_map/jit(_where)/select_n | solution.py:731
  20.8 0.2 maximum_multiply_fusion.prop_ref
  21.0 11.1 %all-to-all-done.in_ref = f32[16,3,64,128]{3,2,1,0:T(8,128)S(1)} async-done(((f32[16,3,64,128]{3,2,1,0:T(8,128)}), f32[16,3,64,128]{3,2,1,0:T(8,128)S(1)}, u32[]{:S(2)}, u32[]{:S(2)}) %all-to-all-start) | async-done | bytes 1572896 | tf_op jit(solution)/shard_map/all_to_all | solution.py:783
  32.1 3.3 %march.2 = f32[8,16,3,8,128]{4,3,2,1,0:T(8,128)S(1)} custom-call(f32[16,3,64,128]{3,2,1,0:T(8,128)S(1)} %all-to-all-done.in_ref, f32[2,8,128]{2,1,0:T(8,128)S(1)} %get-tuple-element.7.twiddle_ref, bf16[768,256]{1,0:T(8,128)(2,1)S(1)} %get-tuple-element.8.forward_ref, bf16[768,256]{1,0:T(8,128)(2,1)} %constant.74.clone.inverse_hbm.inverse_ref, ...), custom_call_target="tpu_custom_call" | custom-call | flops 1207959552 | bytes 6291456 | tf_op jit(solution)/shard_map/march/pallas_call | solution.py:371
  35.4 0.0 copy-start
  35.4 0.0 copy-start.1
  35.5 0.0 copy-start.3
  35.5 0.0 copy-start.5
  35.5 0.0 copy-start.6
  35.5 33.3 %all_to_all.25 = f32[128,3,8,128]{3,2,1,0:T(8,128)S(1)} all-to-all(f32[128,3,8,128]{3,2,1,0:T(8,128)S(1)} %bitcast.25), channel_id=1, replica_groups=mesh['harm'=8,'rows'=16] {'harm','rows'}, dimensions={0} | all-to-all | bytes 3145728 | tf_op jit(solution)/shard_map/all_to_all | solution.py:787
  68.8 0.0 copy-done
  68.8 0.0 copy-done.1
  68.8 0.0 copy-done.3
  68.8 0.0 copy-done.5
  68.8 0.0 copy-done.6
  68.8 4.1 %pixels.1 = f32[8,16,3,8,128]{4,3,2,1,0:T(8,128)S(1)} custom-call(f32[8,16,3,8,128]{4,3,2,1,0:T(8,128)S(1)} %bitcast.26, bf16[768,256]{1,0:T(8,128)(2,1)S(1)} %copy-done.3, f32[2,8,128]{2,1,0:T(8,128)S(1)} %copy-done.6, f32[2,24,8,1024]{3,2,1,0:T(8,128)S(1)} %copy-done, f32[8,8,128]{2,1,0:T(8,128)S(1)} %copy-done.5, bf16[768,256]{1,0:T(8,128)(2,1)S(1)} %copy-done.1), custom_call_target="tpu_custom_call" | custom-call | flops 1207959552 | bytes 6291456 | tf_op jit(solution)/shard_map/pixels/pallas_call | solution.py:681
  72.9 0.0 copy-start.2
  72.9 0.0 copy-start.4
  73.0 28.6 %all_to_all.26 = f32[128,3,8,128]{3,2,1,0:T(8,128)S(1)} all-to-all(f32[128,3,8,128]{3,2,1,0:T(8,128)S(1)} %bitcast.27), channel_id=1, replica_groups=mesh['harm'=8,'rows'=16] {'harm','rows'}, dimensions={0} | all-to-all | bytes 3145728 | tf_op jit(solution)/shard_map/all_to_all | solution.py:791
  101.5 0.0 copy-done.2
  101.5 0.0 copy-done.4
  101.5 2.6 %march.3 = f32[8,16,3,8,128]{4,3,2,1,0:T(8,128)S(1)} custom-call(f32[8,16,3,8,128]{4,3,2,1,0:T(8,128)S(1)} %bitcast.23, f32[2,8,128]{2,1,0:T(8,128)S(1)} %copy-done.6, bf16[768,256]{1,0:T(8,128)(2,1)S(1)} %copy-done.2, bf16[768,256]{1,0:T(8,128)(2,1)S(1)} %copy-done.4, f32[2,3,8,64,128]{4,3,2,1,0:T(8,128)S(1)} %maximum_multiply_fusion.prop_ref), custom_call_target="tpu_custom_call" | custom-call | flops 1207959552 | bytes 6291456 | tf_op jit(solution)/shard_map/march/pallas_call | solution.py:371
  104.2 28.6 %all_to_all.27 = f32[128,3,8,128]{3,2,1,0:T(8,128)S(1)} all-to-all(f32[128,3,8,128]{3,2,1,0:T(8,128)S(1)} %bitcast.24), channel_id=1, replica_groups=mesh['harm'=8,'rows'=16] {'harm','rows'}, dimensions={0} | all-to-all | bytes 3145728 | tf_op jit(solution)/shard_map/all_to_all | solution.py:787
  132.7 3.4 %pixels_last.1 = f32[3072,128]{1,0:T(8,128)S(1)} custom-call(f32[8,16,3,8,128]{4,3,2,1,0:T(8,128)S(1)} %bitcast.21, bf16[768,256]{1,0:T(8,128)(2,1)S(1)} %copy-done.3, f32[2,8,128]{2,1,0:T(8,128)S(1)} %copy-done.6, f32[2,24,8,1024]{3,2,1,0:T(8,128)S(1)} %copy-done, f32[8,8,128]{2,1,0:T(8,128)S(1)} %copy-done.5, bf16[768,256]{1,0:T(8,128)(2,1)S(1)} %copy-done.1), custom_call_target="tpu_custom_call" | custom-call | flops 1207959552 | bytes 6291456 | tf_op jit(solution)/shard_map/pixels_last/pallas_call | solution.py:681
  136.1 25.4 %all_to_all.28.in_ref = f32[8,3,128,128]{3,2,1,0:T(8,128)S(1)} all-to-all(f32[8,3,128,128]{3,2,1,0:T(8,128)S(1)} %bitcast.22), channel_id=1, replica_groups=mesh['harm'=8,'rows'=16] {'harm'}, dimensions={0} | all-to-all | bytes 3145728 | tf_op jit(solution)/shard_map/all_to_all | solution.py:794
  161.6 1.2 order_rows.1
  (5 shorter events, 0.0 us)
Async XLA Ops:
  4.0 28.1 %all-to-all-start = ((f32[16,3,64,128]{3,2,1,0:T(8,128)}), f32[16,3,64,128]{3,2,1,0:T(8,128)S(1)}, u32[]{:S(2)}, u32[]{:S(2)}) async-start(f32[16,3,64,128]{3,2,1,0:T(8,128)} %first_transform.1), calls=%async_computation | async-start | bytes 3145728 | tf_op jit(solution)/shard_map/all_to_all | solution.py:783
  35.4 33.3 %copy-start = (f32[2,24,8,1024]{3,2,1,0:T(8,128)S(1)}, f32[2,24,8,1024]{3,2,1,0:T(8,128)}, u32[]{:S(2)}) copy-start(f32[2,24,8,1024]{3,2,1,0:T(8,128)} %pad_maximum_fusion.refs_2_.refs_0_.screen_ref) | copy-start | bytes 4718596
  35.4 33.3 %copy-start.1 = (bf16[768,256]{1,0:T(8,128)(2,1)S(1)}, bf16[768,256]{1,0:T(8,128)(2,1)}, u32[]{:S(2)}) copy-start(bf16[768,256]{1,0:T(8,128)(2,1)} %constant.75.clone.g_hbm.forward_ref) | copy-start | bytes 1179652
  35.5 33.3 %copy-start.3 = (bf16[768,256]{1,0:T(8,128)(2,1)S(1)}, bf16[768,256]{1,0:T(8,128)(2,1)}, u32[]{:S(2)}) copy-start(bf16[768,256]{1,0:T(8,128)(2,1)} %constant.76.clone.inverse_ref) | copy-start | bytes 1179652
  35.5 33.3 %copy-start.5 = (f32[8,8,128]{2,1,0:T(8,128)S(1)}, f32[8,8,128]{2,1,0:T(8,128)}, u32[]{:S(2)}) copy-start(f32[8,8,128]{2,1,0:T(8,128)} %multiply_bitcast_fusion.refs_1_.gain_ref) | copy-start | bytes 98308
  35.5 33.3 %copy-start.6 = (f32[2,8,128]{2,1,0:T(8,128)S(1)}, f32[2,8,128]{2,1,0:T(8,128)}, u32[]{:S(2)}) copy-start(f32[2,8,128]{2,1,0:T(8,128)} %constant.77.clone.twiddle_hbm.refs_0_.twiddle_ref) | copy-start | bytes 24580
  72.9 28.6 %copy-start.2 = (bf16[768,256]{1,0:T(8,128)(2,1)S(1)}, bf16[768,256]{1,0:T(8,128)(2,1)}, u32[]{:S(2)}) copy-start(bf16[768,256]{1,0:T(8,128)(2,1)} %constant.73.clone.refs_1_.forward_ref) | copy-start | bytes 1179652
  72.9 28.6 %copy-start.4 = (bf16[768,256]{1,0:T(8,128)(2,1)S(1)}, bf16[768,256]{1,0:T(8,128)(2,1)}, u32[]{:S(2)}) copy-start(bf16[768,256]{1,0:T(8,128)(2,1)} %constant.74.clone.inverse_hbm.inverse_ref) | copy-start | bytes 1179652

commit v6 on v5

--- a/solution.py
+++ b/solution.py
@@ -146,8 +146,9 @@
 ):
     local_harm, rows = line_ref.shape[0], result_ref.shape[2]
     lines = rows * 2 * RADIX
-    sources = [in_ref.at[pl.ds(n * lines, lines)] for n in range(local_harm)]
-    targets = [line_ref.at[n] for n in range(local_harm)]
+    pieces = [(n, start) for n in range(local_harm) for start in range(0, lines, 256)]
+    sources = [in_ref.at[pl.ds(n * lines + start, 256)] for n, start in pieces]
+    targets = [line_ref.at[n, pl.ds(start, 256)] for n, start in pieces]
     twiddle_copy, *copies = fetch(
         [twiddle_hbm, sources[0], g_hbm] + sources[1:],
         [twiddle_ref, targets[0], g_ref] + targets[1:],
@@ -157,8 +158,8 @@
     twiddle_copy.wait()
     out_copies = []
     for n in range(local_harm):
-        copies[n].wait()
         for start in range(0, rows, 16):
+            copies[(n * rows + start) // 16].wait()
             points = [
                 tuple(
                     line_ref[n, pl.ds(start * 16 + 2 * k + c, 16, stride=16), :]
@@ -215,7 +216,7 @@
             pltpu.VMEM((local_harm, 16, rows, SUB), jnp.float32),
             pltpu.VMEM(forward.shape, forward.dtype),
             pltpu.VMEM(twiddles.shape, twiddles.dtype),
-            pltpu.SemaphoreType.DMA((local_harm + 2,)),
+            pltpu.SemaphoreType.DMA((local_harm * rows // 16 + 2,)),
             pltpu.SemaphoreType.DMA((local_harm,)),
         ],
         compiler_params=pltpu.CompilerParams(vmem_limit_bytes=VMEM_LIMIT),

time: 163 us -> 164 us (level)
  no operation moved by 1% of the time
where the time goes in v6:
time: 164 us; the launch traced here: 163 us
  blocking collectives  116 us (71%)
  Pallas kernels  19.9 us (12%)
  waiting for transfers between devices  11.1 us (7%)
  other arithmetic  9.87 us (6%)
  starting transfers between devices  6.02 us (4%)
    all_to_all x2, blocking collectives, shards(): lax.all_to_all(marched.reshape((128,) + shape[2:]), axes, 0, 0, tiled=True)  61.8 us
    all_to_all x1, blocking collectives, shards(): lax.all_to_all(lines.reshape((128,) + shape[2:]), axes, 0, 0, tiled=True)  28.6 us
    all_to_all x1, blocking collectives, shards(): out = lax.all_to_all(out, 'harm', 0, 0, tiled=True)  25.4 us
    all_to_all x1, waiting for transfers between devices, shards(): lines = lax.all_to_all(lines, 'rows', 0, 0, tiled=True)  11.1 us
    pallas_call x2, Pallas kernels, pixels(): pl.pallas_call(functools.partial(pixel_kernel, last), in_specs=[IN_VMEM]...  7.54 us
    all_to_all x1, starting transfers between devices, shards(): lines = lax.all_to_all(lines, 'rows', 0, 0, tiled=True)  6.02 us
    pallas_call x2, Pallas kernels, march(): pl.pallas_call(kernel, in_specs=in_specs, out_specs=IN_VMEM, out_shape=pl...  5.99 us
    pallas_call x1, Pallas kernels, first_transform(): pl.pallas_call(first_kernel, in_specs=[IN_HBM] * 3, out_specs=IN_HBM, out...  4.19 us
  transfers between devices with their start and end apart: 1, of which 1 were waited for; matrix products, arithmetic and copies ran while one was open for 6% of the time, Pallas kernels for 1%

profile of v6, /device:TPU:0, one launch (start us, length us, event | category | flops | bytes accessed | tf_op | source)
XLA Modules:
  0.0 163.1 jit_solution(15867110904072489102)
XLA Ops:
  0.0 4.2 %first_transform.1 = f32[16,3,64,128]{3,2,1,0:T(8,128)} custom-call(f32[3072,128]{1,0:T(8,128)} %bitcast.28, bf16[768,256]{1,0:T(8,128)(2,1)} %constant.75.clone.g_hbm.forward_ref, f32[2,8,128]{2,1,0:T(8,128)} %constant.77.clone.twiddle_hbm.refs_0_.twiddle_ref), custom_call_target="tpu_custom_call" | custom-call | flops 603979776 | bytes 3145728 | tf_op jit(solution)/shard_map/first_transform/pallas_call | solution.py:208
  4.2 6.0 %all-to-all-start = ((f32[16,3,64,128]{3,2,1,0:T(8,128)}), f32[16,3,64,128]{3,2,1,0:T(8,128)S(1)}, u32[]{:S(2)}, u32[]{:S(2)}) async-start(f32[16,3,64,128]{3,2,1,0:T(8,128)} %first_transform.1), calls=%async_computation | async-start | bytes 3145728 | tf_op jit(solution)/shard_map/all_to_all | solution.py:784
  10.3 0.8 dynamic-slice_negate_fusion
  11.0 3.0 %fusion.2 = (f32[1,24,8,1024]{3,2,1,0:T(8,128)S(1)}, f32[1,24,8,1024]{3,2,1,0:T(8,128)S(1)}) fusion(f32[8,1024]{1,0:T(8,128)S(1)} %get-tuple-element.14, f32[24]{0:T(128)S(1)} %get-tuple-element.15, f32[24]{0:T(128)S(1)} %get-tuple-element.16, f32[8,1024]{1,0:T(8,128)S(1)} %get-tuple-element.13), kind=kLoop, calls=%fused_computation.8 | loop fusion | flops 983040 | bytes 1638592 | tf_op jit(solution)/shard_map/mul | solution.py:761
  14.0 1.3 pad_maximum_fusion.refs_2_.refs_0_.screen_ref
  15.3 1.0 bring.1
  16.4 1.4 multiply_bitcast_fusion.refs_1_.gain_ref
  17.7 0.1 broadcast_subtract_fusion
  17.8 3.2 %fusion.1 = (f32[1,3,8,64,128]{4,3,2,1,0:T(8,128)S(1)}, f32[1,3,8,64,128]{4,3,2,1,0:T(8,128)S(1)}) fusion(f32[64]{0:T(128)S(1)} %fusion.15, f32[3,8,128]{2,1,0:T(8,128)S(1)} %broadcast_subtract_fusion), kind=kLoop, calls=%fused_computation.7 | loop fusion | flops 1376256 | bytes 1585408 | tf_op jit(solution)/shard_map/jit(_where)/select_n | solution.py:732
  21.0 0.2 maximum_multiply_fusion.prop_ref
  21.2 11.1 %all-to-all-done.in_ref = f32[16,3,64,128]{3,2,1,0:T(8,128)S(1)} async-done(((f32[16,3,64,128]{3,2,1,0:T(8,128)}), f32[16,3,64,128]{3,2,1,0:T(8,128)S(1)}, u32[]{:S(2)}, u32[]{:S(2)}) %all-to-all-start) | async-done | bytes 1572896 | tf_op jit(solution)/shard_map/all_to_all | solution.py:784
  32.3 3.3 %march.2 = f32[8,16,3,8,128]{4,3,2,1,0:T(8,128)S(1)} custom-call(f32[16,3,64,128]{3,2,1,0:T(8,128)S(1)} %all-to-all-done.in_ref, f32[2,8,128]{2,1,0:T(8,128)S(1)} %get-tuple-element.7.twiddle_ref, bf16[768,256]{1,0:T(8,128)(2,1)S(1)} %get-tuple-element.8.forward_ref, bf16[768,256]{1,0:T(8,128)(2,1)} %constant.74.clone.inverse_hbm.inverse_ref, ...), custom_call_target="tpu_custom_call" | custom-call | flops 1207959552 | bytes 6291456 | tf_op jit(solution)/shard_map/march/pallas_call | solution.py:372
  35.7 0.0 copy-start
  35.7 0.0 copy-start.1
  35.7 0.0 copy-start.3
  35.7 0.0 copy-start.5
  35.7 0.0 copy-start.6
  35.7 33.3 %all_to_all.25 = f32[128,3,8,128]{3,2,1,0:T(8,128)S(1)} all-to-all(f32[128,3,8,128]{3,2,1,0:T(8,128)S(1)} %bitcast.25), channel_id=1, replica_groups=mesh['harm'=8,'rows'=16] {'harm','rows'}, dimensions={0} | all-to-all | bytes 3145728 | tf_op jit(solution)/shard_map/all_to_all | solution.py:788
  69.0 0.0 copy-done
  69.0 0.0 copy-done.1
  69.0 0.0 copy-done.3
  69.0 0.0 copy-done.5
  69.0 0.0 copy-done.6
  69.0 4.1 %pixels.1 = f32[8,16,3,8,128]{4,3,2,1,0:T(8,128)S(1)} custom-call(f32[8,16,3,8,128]{4,3,2,1,0:T(8,128)S(1)} %bitcast.26, bf16[768,256]{1,0:T(8,128)(2,1)S(1)} %copy-done.3, f32[2,8,128]{2,1,0:T(8,128)S(1)} %copy-done.6, f32[2,24,8,1024]{3,2,1,0:T(8,128)S(1)} %copy-done, f32[8,8,128]{2,1,0:T(8,128)S(1)} %copy-done.5, bf16[768,256]{1,0:T(8,128)(2,1)S(1)} %copy-done.1), custom_call_target="tpu_custom_call" | custom-call | flops 1207959552 | bytes 6291456 | tf_op jit(solution)/shard_map/pixels/pallas_call | solution.py:682
  73.2 0.0 copy-start.2
  73.2 0.0 copy-start.4
  73.2 28.6 %all_to_all.26 = f32[128,3,8,128]{3,2,1,0:T(8,128)S(1)} all-to-all(f32[128,3,8,128]{3,2,1,0:T(8,128)S(1)} %bitcast.27), channel_id=1, replica_groups=mesh['harm'=8,'rows'=16] {'harm','rows'}, dimensions={0} | all-to-all | bytes 3145728 | tf_op jit(solution)/shard_map/all_to_all | solution.py:792
  101.8 0.0 copy-done.2
  101.8 0.0 copy-done.4
  101.8 2.6 %march.3 = f32[8,16,3,8,128]{4,3,2,1,0:T(8,128)S(1)} custom-call(f32[8,16,3,8,128]{4,3,2,1,0:T(8,128)S(1)} %bitcast.23, f32[2,8,128]{2,1,0:T(8,128)S(1)} %copy-done.6, bf16[768,256]{1,0:T(8,128)(2,1)S(1)} %copy-done.2, bf16[768,256]{1,0:T(8,128)(2,1)S(1)} %copy-done.4, f32[2,3,8,64,128]{4,3,2,1,0:T(8,128)S(1)} %maximum_multiply_fusion.prop_ref), custom_call_target="tpu_custom_call" | custom-call | flops 1207959552 | bytes 6291456 | tf_op jit(solution)/shard_map/march/pallas_call | solution.py:372
  104.4 28.6 %all_to_all.27 = f32[128,3,8,128]{3,2,1,0:T(8,128)S(1)} all-to-all(f32[128,3,8,128]{3,2,1,0:T(8,128)S(1)} %bitcast.24), channel_id=1, replica_groups=mesh['harm'=8,'rows'=16] {'harm','rows'}, dimensions={0} | all-to-all | bytes 3145728 | tf_op jit(solution)/shard_map/all_to_all | solution.py:788
  133.0 3.4 %pixels_last.1 = f32[3072,128]{1,0:T(8,128)S(1)} custom-call(f32[8,16,3,8,128]{4,3,2,1,0:T(8,128)S(1)} %bitcast.21, bf16[768,256]{1,0:T(8,128)(2,1)S(1)} %copy-done.3, f32[2,8,128]{2,1,0:T(8,128)S(1)} %copy-done.6, f32[2,24,8,1024]{3,2,1,0:T(8,128)S(1)} %copy-done, f32[8,8,128]{2,1,0:T(8,128)S(1)} %copy-done.5, bf16[768,256]{1,0:T(8,128)(2,1)S(1)} %copy-done.1), custom_call_target="tpu_custom_call" | custom-call | flops 1207959552 | bytes 6291456 | tf_op jit(solution)/shard_map/pixels_last/pallas_call | solution.py:682
  136.4 25.4 %all_to_all.28.in_ref = f32[8,3,128,128]{3,2,1,0:T(8,128)S(1)} all-to-all(f32[8,3,128,128]{3,2,1,0:T(8,128)S(1)} %bitcast.22), channel_id=1, replica_groups=mesh['harm'=8,'rows'=16] {'harm'}, dimensions={0} | all-to-all | bytes 3145728 | tf_op jit(solution)/shard_map/all_to_all | solution.py:795
  161.8 1.2 order_rows.1
  (5 shorter events, 0.0 us)
Async XLA Ops:
  4.2 28.1 %all-to-all-start = ((f32[16,3,64,128]{3,2,1,0:T(8,128)}), f32[16,3,64,128]{3,2,1,0:T(8,128)S(1)}, u32[]{:S(2)}, u32[]{:S(2)}) async-start(f32[16,3,64,128]{3,2,1,0:T(8,128)} %first_transform.1), calls=%async_computation | async-start | bytes 3145728 | tf_op jit(solution)/shard_map/all_to_all | solution.py:784
  35.7 33.3 %copy-start = (f32[2,24,8,1024]{3,2,1,0:T(8,128)S(1)}, f32[2,24,8,1024]{3,2,1,0:T(8,128)}, u32[]{:S(2)}) copy-start(f32[2,24,8,1024]{3,2,1,0:T(8,128)} %pad_maximum_fusion.refs_2_.refs_0_.screen_ref) | copy-start | bytes 4718596
  35.7 33.3 %copy-start.1 = (bf16[768,256]{1,0:T(8,128)(2,1)S(1)}, bf16[768,256]{1,0:T(8,128)(2,1)}, u32[]{:S(2)}) copy-start(bf16[768,256]{1,0:T(8,128)(2,1)} %constant.75.clone.g_hbm.forward_ref) | copy-start | bytes 1179652
  35.7 33.3 %copy-start.3 = (bf16[768,256]{1,0:T(8,128)(2,1)S(1)}, bf16[768,256]{1,0:T(8,128)(2,1)}, u32[]{:S(2)}) copy-start(bf16[768,256]{1,0:T(8,128)(2,1)} %constant.76.clone.inverse_ref) | copy-start | bytes 1179652
  35.7 33.3 %copy-start.5 = (f32[8,8,128]{2,1,0:T(8,128)S(1)}, f32[8,8,128]{2,1,0:T(8,128)}, u32[]{:S(2)}) copy-start(f32[8,8,128]{2,1,0:T(8,128)} %multiply_bitcast_fusion.refs_1_.gain_ref) | copy-start | bytes 98308
  35.7 33.3 %copy-start.6 = (f32[2,8,128]{2,1,0:T(8,128)S(1)}, f32[2,8,128]{2,1,0:T(8,128)}, u32[]{:S(2)}) copy-start(f32[2,8,128]{2,1,0:T(8,128)} %constant.77.clone.twiddle_hbm.refs_0_.twiddle_ref) | copy-start | bytes 24580
  73.2 28.6 %copy-start.2 = (bf16[768,256]{1,0:T(8,128)(2,1)S(1)}, bf16[768,256]{1,0:T(8,128)(2,1)}, u32[]{:S(2)}) copy-start(bf16[768,256]{1,0:T(8,128)(2,1)} %constant.73.clone.refs_1_.forward_ref) | copy-start | bytes 1179652
  73.2 28.6 %copy-start.4 = (bf16[768,256]{1,0:T(8,128)(2,1)S(1)}, bf16[768,256]{1,0:T(8,128)(2,1)}, u32[]{:S(2)}) copy-start(bf16[768,256]{1,0:T(8,128)(2,1)} %constant.74.clone.inverse_hbm.inverse_ref) | copy-start | bytes 1179652
